TPU v7x, 32 devices: a whole 2x2x4 slice. The times are simulated.
32 devices in a mesh: dp: 2 (over y), ctx: 4 (over x, core), tp: 4 (over z).
Axes of the slice: x: 2, y: 2, z: 4, core: 2. Of those that a mesh axis runs over, the one named last changes fastest.
Arguments:
- hidden_in: bfloat16 [4, 1024, 1024], P('dp', 'ctx'), may hold values from -6 to 6
- encoder_states: bfloat16 [4, 4096, 1024], P('dp', 'ctx'), may hold values from -6 to 6
- out_cotangent: bfloat16 [4, 1024, 1024], P('dp', 'ctx'), may hold values from -6 to 6
- self_proj: bfloat16 [3, 1024, 1024], P(None, ('dp', 'ctx'), 'tp'), may hold values from -0.1875 to 0.1875
- self_qv_bias: bfloat16 [16, 128], P('tp', ('dp', 'ctx')), may hold values from -0.3125 to 0.3125
- self_out_proj: bfloat16 [1024, 1024], P('tp', ('dp', 'ctx')), may hold values from -3 to 3
- cross_q_proj: bfloat16 [1024, 1024], P(('dp', 'ctx'), 'tp'), may hold values from -0.1875 to 0.1875
- cross_kv_proj: bfloat16 [2, 1024, 1024], P(None, ('dp', 'ctx'), 'tp'), may hold values from -0.1875 to 0.1875
- cross_qv_bias: bfloat16 [16, 128], P('tp', ('dp', 'ctx')), may hold values from -0.3125 to 0.3125
- cross_out_proj: bfloat16 [1024, 1024], P('tp', ('dp', 'ctx')), may hold values from -6 to 6
- up_proj: bfloat16 [1024, 4096], P(('dp', 'ctx'), 'tp'), may hold values from -0.1875 to 0.1875
- up_bias: bfloat16 [128, 32], P('tp', ('dp', 'ctx')), may hold values from -1.75 to 1.75
- down_proj: bfloat16 [4096, 1024], P('tp', ('dp', 'ctx')), may hold values from -0.09375 to 0.09375
- norm_gain: bfloat16 [3, 1024], P(None, ('dp', 'ctx')), may hold values from 0.5 to 1.5
- norm_bias: bfloat16 [3, 1024], P(None, ('dp', 'ctx')), may hold values from -0.625 to 0.625
- out_bias: bfloat16 [3, 1024], P(None, ('dp', 'ctx')), may hold values from -0.625 to 0.625
Outputs:
- hidden_out: bfloat16 [4, 1024, 1024], P('dp', 'ctx')
- input_grad: float32 [4, 1024, 1024], P('dp', 'ctx')
- encoder_grad: float32 [4, 4096, 1024], P('dp', 'ctx', 'tp')
- self_proj_grad: float32 [3, 1024, 1024], P(None, ('dp', 'ctx'), 'tp')
- self_qv_bias_grad: float32 [16, 128], P('tp', ('dp', 'ctx'))
- self_out_proj_grad: float32 [1024, 1024], P('tp', ('dp', 'ctx'))
- cross_q_proj_grad: float32 [1024, 1024], P(('dp', 'ctx'), 'tp')
- cross_kv_proj_grad: float32 [2, 1024, 1024], P(None, ('dp', 'ctx'), 'tp')
- cross_qv_bias_grad: float32 [16, 128], P('tp', ('dp', 'ctx'))
- cross_out_proj_grad: float32 [1024, 1024], P('tp', ('dp', 'ctx'))
- up_proj_grad: float32 [1024, 4096], P(('dp', 'ctx'), 'tp')
- up_bias_grad: float32 [128, 32], P('tp', ('dp', 'ctx'))
- down_proj_grad: float32 [4096, 1024], P('tp', ('dp', 'ctx'))
- norm_gain_grad: float32 [3, 1024], P(None, ('dp', 'ctx'))
- norm_bias_grad: float32 [3, 1024], P(None, ('dp', 'ctx'))
- out_bias_grad: float32 [3, 1024], P(None, ('dp', 'ctx'))
- stream_rms: float32 [4, 4, 1024], P(None, 'dp', 'ctx')
All inputs are finite; a program needn't handle non-finite values.
Results may differ from a plain program's by a relative error of at most 0.04.
Values may be sent and summed in bfloat16 or wider, within the bound.
No kernel may reach another device: no remote copies, remote signals or barrier semaphores. Data moves between devices by JAX's collectives and lax.ppermute only.
A program may use at most 256 MiB of HBM per device.

v0:
```python
import math

import jax
import jax.numpy as jnp
from jax import lax
from jax.sharding import PartitionSpec as P

EPSILON = 1e-05
NEGATIVE = -1e30


def product(left, right):
    return jnp.dot(left, right, preferred_element_type=jnp.float32)


def outer_product(left, right):
    return lax.dot_general(
        left, right, (((0,), (0,)), ((), ())), preferred_element_type=jnp.float32
    )


def back_product(left, right):
    return lax.dot_general(
        left, right, (((1,), (1,)), ((), ())), preferred_element_type=jnp.float32
    )


def norm_forward(values, norm_gain, norm_shift):
    row_mean = jnp.mean(values, -1, keepdims=True)
    centered = values - row_mean
    inv_std = lax.rsqrt(jnp.mean(centered * centered, -1, keepdims=True) + EPSILON)
    normed = centered * inv_std
    return (normed * norm_gain + norm_shift, normed, inv_std)


def norm_backward(gradient, normed, inv_std, norm_gain):
    gain_grad = jnp.sum(gradient * normed, 0)
    shift_grad = jnp.sum(gradient, 0)
    scaled = gradient * norm_gain
    input_part = inv_std * (
        scaled
        - jnp.mean(scaled, -1, keepdims=True)
        - normed * jnp.mean(scaled * normed, -1, keepdims=True)
    )
    return (input_part, gain_grad, shift_grad)


def head_total(values):
    return lax.psum(values.astype(jnp.bfloat16), "tp").astype(jnp.float32)


def root_mean(values):
    return jnp.sqrt(jnp.mean(values * values, -1))


def exact_gelu(values):
    return jax.nn.gelu(values, approximate=False)


def block_scores(query_rows, key_heads, own_block, score_scale):
    logit_scores = (
        jnp.einsum("sbhd,skhd->shbk", query_rows, key_heads, preferred_element_type=jnp.float32)
        * score_scale
    )
    key_block = jnp.arange(key_heads.shape[1]) // query_rows.shape[1]
    return jnp.where(key_block <= own_block, logit_scores, NEGATIVE)


def softmax_stats(logit_scores):
    row_max = jnp.max(logit_scores, -1, keepdims=True)
    row_total = jnp.sum(jnp.exp(logit_scores - row_max), -1, keepdims=True)
    return (row_max, row_total)


def attend_forward(logit_scores, value_heads):
    row_max, row_total = softmax_stats(logit_scores)
    attention_weights = jnp.exp(logit_scores - row_max) / row_total
    mixed = jnp.einsum(
        "shbk,skhd->sbhd",
        attention_weights.astype(jnp.bfloat16),
        value_heads,
        preferred_element_type=jnp.float32,
    )
    return (mixed, row_max, row_total)


def prob_grads(logit_scores, row_max, row_total, grad_heads, value_heads):
    attention_weights = jnp.exp(logit_scores - row_max) / row_total
    prob_grad = jnp.einsum(
        "sbhd,skhd->shbk", grad_heads, value_heads, preferred_element_type=jnp.float32
    )
    return (attention_weights, prob_grad)


def attend_backward(
    query_rows, key_heads, grad_heads, attention_weights, prob_grad, inner_sum, score_scale
):
    score_low = (attention_weights * (prob_grad - inner_sum)).astype(jnp.bfloat16)
    value_grad = jnp.einsum(
        "shbk,sbhd->skhd",
        attention_weights.astype(jnp.bfloat16),
        grad_heads,
        preferred_element_type=jnp.float32,
    )
    query_grad = (
        jnp.einsum("shbk,skhd->sbhd", score_low, key_heads, preferred_element_type=jnp.float32)
        * score_scale
    )
    key_grad = (
        jnp.einsum("shbk,sbhd->skhd", score_low, query_rows, preferred_element_type=jnp.float32)
        * score_scale
    )
    return (query_grad, key_grad, value_grad)


def body(
    hidden_in,
    encoder_states,
    out_cotangent,
    self_proj,
    self_qv_bias,
    self_out_proj,
    cross_q_proj,
    cross_kv_proj,
    cross_qv_bias,
    cross_out_proj,
    up_proj,
    up_bias,
    down_proj,
    norm_gain,
    norm_bias,
    out_bias,
):
    (
        self_proj_all,
        self_bias_all,
        self_out_all,
        cross_q_all,
        cross_kv_all,
        cross_bias_all,
        cross_out_all,
        up_all,
        up_bias_all,
        down_all,
        gain_all,
        shift_all,
        branch_all,
    ) = (
        lax.all_gather(self_proj, ("dp", "ctx"), axis=1, tiled=True),
        lax.all_gather(self_qv_bias, ("dp", "ctx"), axis=1, tiled=True),
        lax.all_gather(self_out_proj, ("dp", "ctx"), axis=1, tiled=True),
        lax.all_gather(cross_q_proj, ("dp", "ctx"), axis=0, tiled=True),
        lax.all_gather(cross_kv_proj, ("dp", "ctx"), axis=1, tiled=True),
        lax.all_gather(cross_qv_bias, ("dp", "ctx"), axis=1, tiled=True),
        lax.all_gather(cross_out_proj, ("dp", "ctx"), axis=1, tiled=True),
        lax.all_gather(up_proj, ("dp", "ctx"), axis=0, tiled=True),
        lax.all_gather(up_bias, ("dp", "ctx"), axis=1, tiled=True),
        lax.all_gather(down_proj, ("dp", "ctx"), axis=1, tiled=True),
        lax.all_gather(norm_gain, ("dp", "ctx"), axis=1, tiled=True),
        lax.all_gather(norm_bias, ("dp", "ctx"), axis=1, tiled=True),
        lax.all_gather(out_bias, ("dp", "ctx"), axis=1, tiled=True),
    )
    seq_count, block_len, model_width = hidden_in.shape
    row_count = seq_count * block_len
    head_count = self_bias_all.shape[0]
    head_size = self_bias_all.shape[1] // 2
    local_width = head_count * head_size
    score_scale = 1.0 / math.sqrt(head_size)
    own_block = lax.axis_index("ctx")
    gains = gain_all.astype(jnp.float32)
    shifts = shift_all.astype(jnp.float32)
    branch_bias = branch_all.astype(jnp.float32)
    self_bias = self_bias_all.astype(jnp.float32)
    cross_bias = cross_bias_all.astype(jnp.float32)
    tokens = hidden_in.reshape(row_count, model_width)
    tokens_f = tokens.astype(jnp.float32)
    projected = jnp.einsum("rd,jde->jre", tokens, self_proj_all, preferred_element_type=jnp.float32)
    query_low = (projected[0] + self_bias[:, :head_size].reshape(local_width)).astype(jnp.bfloat16)
    key_low = projected[1].astype(jnp.bfloat16)
    value_low = (projected[2] + self_bias[:, head_size:].reshape(local_width)).astype(jnp.bfloat16)
    pair_low = jnp.concatenate([key_low, value_low], -1).reshape(
        seq_count, block_len, 2 * local_width
    )
    all_pairs = lax.all_gather(pair_low, "ctx", axis=1, tiled=True)
    query_heads = query_low.reshape(seq_count, block_len, head_count, head_size)
    key_heads = all_pairs[..., :local_width].reshape(seq_count, -1, head_count, head_size)
    value_heads = all_pairs[..., local_width:].reshape(seq_count, -1, head_count, head_size)
    self_mixed, self_max, self_total = attend_forward(
        block_scores(query_heads, key_heads, own_block, score_scale), value_heads
    )
    attn_low = self_mixed.reshape(row_count, local_width).astype(jnp.bfloat16)
    attn_branch = head_total(product(attn_low, self_out_all)) + branch_bias[0]
    first_out, first_normed, first_inv = norm_forward(tokens_f + attn_branch, gains[0], shifts[0])
    first_low = first_out.astype(jnp.bfloat16)
    first_f = first_low.astype(jnp.float32)
    cross_query = (
        product(first_low, cross_q_all) + cross_bias[:, :head_size].reshape(local_width)
    ).astype(jnp.bfloat16)
    enc_rows = encoder_states.reshape(-1, model_width)
    enc_proj = jnp.einsum("rd,jde->jre", enc_rows, cross_kv_all, preferred_element_type=jnp.float32)
    enc_key = enc_proj[0].astype(jnp.bfloat16)
    enc_value = (enc_proj[1] + cross_bias[:, head_size:].reshape(local_width)).astype(jnp.bfloat16)
    enc_pairs = jnp.concatenate([enc_key, enc_value], -1).reshape(seq_count, -1, 2 * local_width)
    all_enc = lax.all_gather(enc_pairs, "ctx", axis=1, tiled=True)
    grouped_query = cross_query.reshape(seq_count // 2, 2, block_len, head_count, head_size)
    grouped_enc = all_enc.reshape(seq_count // 2, 2, -1, 2 * local_width)

    def cross_pair(inputs):
        query_pair, enc_pair = inputs
        key_pair = enc_pair[..., :local_width].reshape(2, -1, head_count, head_size)
        value_pair = enc_pair[..., local_width:].reshape(2, -1, head_count, head_size)
        logit_scores = (
            jnp.einsum("sbhd,skhd->shbk", query_pair, key_pair, preferred_element_type=jnp.float32)
            * score_scale
        )
        return attend_forward(logit_scores, value_pair)

    cross_mixed, cross_max, cross_total = lax.map(cross_pair, (grouped_query, grouped_enc))
    cross_low = cross_mixed.reshape(row_count, local_width).astype(jnp.bfloat16)
    cross_branch = head_total(product(cross_low, cross_out_all)) + branch_bias[1]
    second_out, second_normed, second_inv = norm_forward(
        first_f + cross_branch, gains[1], shifts[1]
    )
    second_low = second_out.astype(jnp.bfloat16)
    second_f = second_low.astype(jnp.float32)
    up_vector = up_bias_all.astype(jnp.float32).reshape(-1)
    pre_act = product(second_low, up_all) + up_vector
    active_low = exact_gelu(pre_act).astype(jnp.bfloat16)
    mlp_branch = head_total(product(active_low, down_all)) + branch_bias[2]
    third_out, third_normed, third_inv = norm_forward(second_f + mlp_branch, gains[2], shifts[2])
    hidden_out = third_out.astype(jnp.bfloat16).reshape(seq_count, block_len, model_width)
    stream_rms = jnp.stack(
        [
            root_mean(tokens_f),
            root_mean(attn_branch),
            root_mean(cross_branch),
            root_mean(mlp_branch),
        ]
    ).reshape(4, seq_count, block_len)
    out_grad = out_cotangent.reshape(row_count, model_width).astype(jnp.float32)
    third_grad, gain_two, shift_two = norm_backward(out_grad, third_normed, third_inv, gains[2])
    mlp_bias_grad = jnp.sum(third_grad, 0)
    mlp_low = third_grad.astype(jnp.bfloat16)
    down_grad = outer_product(active_low, mlp_low)
    active_grad = back_product(mlp_low, down_all)
    gelu_pull = jax.vjp(exact_gelu, pre_act)[1]
    pre_low = gelu_pull(active_grad)[0].astype(jnp.bfloat16)
    up_bias_grad = jnp.sum(pre_low.astype(jnp.float32), 0).reshape(up_bias_all.shape)
    up_grad = outer_product(second_low, pre_low)
    second_grad, gain_one, shift_one = norm_backward(
        third_grad + head_total(back_product(pre_low, up_all)), second_normed, second_inv, gains[1]
    )
    cross_bias_out = jnp.sum(second_grad, 0)
    cross_branch_low = second_grad.astype(jnp.bfloat16)
    cross_out_grad = outer_product(cross_low, cross_branch_low)
    cross_mix_grad = back_product(cross_branch_low, cross_out_all).astype(jnp.bfloat16)
    grouped_grad = cross_mix_grad.reshape(seq_count // 2, 2, block_len, head_count, head_size)

    def cross_pair_back(inputs):
        query_pair, enc_pair, max_pair, total_pair, grad_pair = inputs
        key_pair = enc_pair[..., :local_width].reshape(2, -1, head_count, head_size)
        value_pair = enc_pair[..., local_width:].reshape(2, -1, head_count, head_size)
        logit_scores = (
            jnp.einsum("sbhd,skhd->shbk", query_pair, key_pair, preferred_element_type=jnp.float32)
            * score_scale
        )
        attention_weights, prob_grad = prob_grads(
            logit_scores, max_pair, total_pair, grad_pair, value_pair
        )
        inner_sum = jnp.sum(attention_weights * prob_grad, -1, keepdims=True)
        query_grad, key_grad, value_grad = attend_backward(
            query_pair, key_pair, grad_pair, attention_weights, prob_grad, inner_sum, score_scale
        )
        return (
            query_grad,
            jnp.concatenate(
                [key_grad.reshape(2, -1, local_width), value_grad.reshape(2, -1, local_width)], -1
            ),
        )

    pair_query_grad, enc_pair_grad = lax.map(
        cross_pair_back, (grouped_query, grouped_enc, cross_max, cross_total, grouped_grad)
    )
    enc_grads = lax.psum_scatter(
        enc_pair_grad.reshape(seq_count, -1, 2 * local_width).astype(jnp.bfloat16),
        "ctx",
        scatter_dimension=1,
        tiled=True,
    ).astype(jnp.float32)
    cross_query_grad = pair_query_grad.reshape(row_count, local_width)
    cross_query_low = cross_query_grad.astype(jnp.bfloat16)
    enc_grad_low = enc_grads.reshape(-1, 2, local_width).astype(jnp.bfloat16)
    cross_bias_grad = jnp.concatenate(
        [
            jnp.sum(cross_query_low.astype(jnp.float32), 0).reshape(head_count, head_size),
            jnp.sum(enc_grad_low[:, 1].astype(jnp.float32), 0).reshape(head_count, head_size),
        ],
        -1,
    )
    cross_q_grad = outer_product(first_low, cross_query_low)
    cross_kv_grad = jnp.einsum(
        "rd,rje->jde", enc_rows, enc_grad_low, preferred_element_type=jnp.float32
    )
    encoder_part = jnp.einsum(
        "rje,jde->rd", enc_grad_low, cross_kv_all, preferred_element_type=jnp.float32
    )
    encoder_grad = lax.psum_scatter(
        encoder_part.reshape(seq_count, -1, model_width).astype(jnp.bfloat16),
        "tp",
        scatter_dimension=2,
        tiled=True,
    ).astype(jnp.float32)
    first_grad, gain_zero, shift_zero = norm_backward(
        second_grad + head_total(back_product(cross_query_low, cross_q_all)),
        first_normed,
        first_inv,
        gains[0],
    )
    attn_bias_grad = jnp.sum(first_grad, 0)
    attn_branch_low = first_grad.astype(jnp.bfloat16)
    self_out_grad = outer_product(attn_low, attn_branch_low)
    mix_grad = (
        back_product(attn_branch_low, self_out_all)
        .astype(jnp.bfloat16)
        .reshape(seq_count, block_len, head_count, head_size)
    )
    self_scores = block_scores(query_heads, key_heads, own_block, score_scale)
    attention_weights, prob_grad = prob_grads(
        self_scores, self_max, self_total, mix_grad, value_heads
    )
    inner_sum = jnp.sum(attention_weights * prob_grad, -1, keepdims=True)
    query_grad, key_grad, value_grad = attend_backward(
        query_heads, key_heads, mix_grad, attention_weights, prob_grad, inner_sum, score_scale
    )
    pair_grads = jnp.concatenate(
        [
            key_grad.reshape(seq_count, -1, local_width),
            value_grad.reshape(seq_count, -1, local_width),
        ],
        -1,
    )
    own_pairs = lax.psum_scatter(
        pair_grads.astype(jnp.bfloat16), "ctx", scatter_dimension=1, tiled=True
    ).astype(jnp.float32)
    own_low = own_pairs.reshape(row_count, 2 * local_width).astype(jnp.bfloat16)
    query_grad_low = query_grad.reshape(row_count, local_width).astype(jnp.bfloat16)
    stacked = jnp.stack([query_grad_low, own_low[:, :local_width], own_low[:, local_width:]])
    self_proj_grad = jnp.einsum("rd,jre->jde", tokens, stacked, preferred_element_type=jnp.float32)
    input_grad = first_grad + head_total(
        jnp.einsum("jre,jde->rd", stacked, self_proj_all, preferred_element_type=jnp.float32)
    )
    self_bias_grad = jnp.concatenate(
        [
            jnp.sum(query_grad_low.astype(jnp.float32), 0).reshape(head_count, head_size),
            jnp.sum(own_low[:, local_width:].astype(jnp.float32), 0).reshape(head_count, head_size),
        ],
        -1,
    )
    (
        self_proj_out,
        self_bias_out,
        self_out_out,
        cross_q_out,
        cross_kv_out,
        cross_bias_res,
        cross_out_res,
        up_out,
        up_bias_out,
        down_out,
        gain_out,
        shift_out,
        branch_out,
    ) = (
        lax.psum_scatter(
            self_proj_grad.astype(jnp.bfloat16), ("dp", "ctx"), scatter_dimension=1, tiled=True
        ).astype(jnp.float32),
        lax.psum_scatter(
            self_bias_grad.astype(jnp.bfloat16), ("dp", "ctx"), scatter_dimension=1, tiled=True
        ).astype(jnp.float32),
        lax.psum_scatter(
            self_out_grad.astype(jnp.bfloat16), ("dp", "ctx"), scatter_dimension=1, tiled=True
        ).astype(jnp.float32),
        lax.psum_scatter(
            cross_q_grad.astype(jnp.bfloat16), ("dp", "ctx"), scatter_dimension=0, tiled=True
        ).astype(jnp.float32),
        lax.psum_scatter(
            cross_kv_grad.astype(jnp.bfloat16), ("dp", "ctx"), scatter_dimension=1, tiled=True
        ).astype(jnp.float32),
        lax.psum_scatter(
            cross_bias_grad.astype(jnp.bfloat16), ("dp", "ctx"), scatter_dimension=1, tiled=True
        ).astype(jnp.float32),
        lax.psum_scatter(
            cross_out_grad.astype(jnp.bfloat16), ("dp", "ctx"), scatter_dimension=1, tiled=True
        ).astype(jnp.float32),
        lax.psum_scatter(
            up_grad.astype(jnp.bfloat16), ("dp", "ctx"), scatter_dimension=0, tiled=True
        ).astype(jnp.float32),
        lax.psum_scatter(
            up_bias_grad.astype(jnp.bfloat16), ("dp", "ctx"), scatter_dimension=1, tiled=True
        ).astype(jnp.float32),
        lax.psum_scatter(
            down_grad.astype(jnp.bfloat16), ("dp", "ctx"), scatter_dimension=1, tiled=True
        ).astype(jnp.float32),
        lax.psum_scatter(
            jnp.stack([gain_zero, gain_one, gain_two]).astype(jnp.bfloat16),
            ("dp", "ctx"),
            scatter_dimension=1,
            tiled=True,
        ).astype(jnp.float32),
        lax.psum_scatter(
            jnp.stack([shift_zero, shift_one, shift_two]).astype(jnp.bfloat16),
            ("dp", "ctx"),
            scatter_dimension=1,
            tiled=True,
        ).astype(jnp.float32),
        lax.psum_scatter(
            jnp.stack([attn_bias_grad, cross_bias_out, mlp_bias_grad]).astype(jnp.bfloat16),
            ("dp", "ctx"),
            scatter_dimension=1,
            tiled=True,
        ).astype(jnp.float32),
    )
    return (
        hidden_out,
        input_grad.reshape(seq_count, block_len, model_width),
        encoder_grad,
        self_proj_out,
        self_bias_out,
        self_out_out,
        cross_q_out,
        cross_kv_out,
        cross_bias_res,
        cross_out_res,
        up_out,
        up_bias_out,
        down_out,
        gain_out,
        shift_out,
        branch_out,
        stream_rms,
    )


def solution(mesh):
    placed = (
        P("dp", "ctx", None),
        P("dp", "ctx", None),
        P("dp", "ctx", None),
        P(None, ("dp", "ctx"), "tp"),
        P("tp", ("dp", "ctx")),
        P("tp", ("dp", "ctx")),
        P(("dp", "ctx"), "tp"),
        P(None, ("dp", "ctx"), "tp"),
        P("tp", ("dp", "ctx")),
        P("tp", ("dp", "ctx")),
        P(("dp", "ctx"), "tp"),
        P("tp", ("dp", "ctx")),
        P("tp", ("dp", "ctx")),
        P(None, ("dp", "ctx")),
        P(None, ("dp", "ctx")),
        P(None, ("dp", "ctx")),
    )
    return jax.shard_map(
        body,
        mesh=mesh,
        in_specs=placed,
        out_specs=(
            P("dp", "ctx", None),
            P("dp", "ctx", None),
            P("dp", "ctx", "tp"),
            P(None, ("dp", "ctx"), "tp"),
            P("tp", ("dp", "ctx")),
            P("tp", ("dp", "ctx")),
            P(("dp", "ctx"), "tp"),
            P(None, ("dp", "ctx"), "tp"),
            P("tp", ("dp", "ctx")),
            P("tp", ("dp", "ctx")),
            P(("dp", "ctx"), "tp"),
            P("tp", ("dp", "ctx")),
            P("tp", ("dp", "ctx")),
            P(None, ("dp", "ctx")),
            P(None, ("dp", "ctx")),
            P(None, ("dp", "ctx")),
            P(None, "dp", "ctx"),
        ),
        check_vma=False,
    )
```

profile of v0, /device:TPU:0, one launch (start us, length us, event | category | flops | bytes accessed | tf_op | source)
XLA Modules:
  0.0 1353.1 jit_solution(14712744317374724626)
XLA Ops:
  9.0 10.5 all-gather
  19.8 19.3 %all-gather.10.cloned.1.call-done = bf16[3,1024,256]{1,2,0:T(8,128)(2,1)} async-done(((bf16[3,128,256]{1,2,0:T(8,128)(2,1)}), bf16[3,1024,256]{1,2,0:T(8,128)(2,1)}) %all-gather.10.cloned.1.call-update) | async-done | bytes 1572880 | tf_op jit(solution)/shard_map/all_gather | solution.py:149
  54.2 11.5 all_gather.48
  161.3 49.6 %all-gather.16.cloned.1.call-done = bf16[2,4096,512]{1,0,2:T(2,128)(2,1)} async-done(((bf16[2,1024,512]{1,0,2:T(2,128)(2,1)}), bf16[2,4096,512]{1,0,2:T(2,128)(2,1)}) %all-gather.16.cloned.1.call-update) | async-done | bytes 8388624 | tf_op jit(solution)/shard_map/all_gather | solution.py:204
  229.7 17.2 %fusion.99 = (f32[2,4,256]{2,1,0:T(4,128)S(1)}, f32[2,4,256,4096]{3,2,1,0:T(8,128)}) fusion(bf16[2,256,4,64]{1,3,2,0:T(8,128)(2,1)S(1)} %copy.131, bf16[2,4096,4,64]{1,3,2,0:T(8,128)(2,1)} %bitcast.226), kind=kOutput, calls=%fused_computation.197 | convolution fusion | flops 1098911744 | bytes 38019072 | tf_op jit(solution)/shard_map/while/body/eval_jaxpr/sub | solution.py:77
  246.8 15.1 %fusion.58 = bf16[2,256,4,64]{1,3,2,0:T(8,128)(2,1)S(1)} fusion(bf16[2,4096,4,64]{1,3,2,0:T(8,128)(2,1)} %bitcast.235, f32[2,4,256,4096]{3,2,1,0:T(8,128)} %get-tuple-element.173, f32[2,4,256]{2,1,0:T(4,128)S(1)} %get-tuple-element.172), kind=kOutput, calls=%fused_computation.126 | convolution fusion | flops 1090650112 | bytes 38019072 | tf_op jit(solution)/shard_map/while/body/eval_jaxpr/shbk,skhd->sbhd/dot_general | solution.py:78
  274.3 41.4 %all-reduce.10.cloned.1.call-done = bf16[512,1024]{1,0:T(8,128)(2,1)} async-done(((bf16[512,1024]{1,0:T(8,128)(2,1)}), bf16[512,1024]{1,0:T(8,128)(2,1)}) %all-reduce.10.cloned.1.call-update) | async-done | bytes 1048592 | tf_op jit(solution)/shard_map/psum | solution.py:49
  318.7 26.2 %all-gather.18.cloned.1.call-done = bf16[1024,1024]{1,0:T(8,128)(2,1)} async-done(((bf16[128,1024]{1,0:T(8,128)(2,1)}), bf16[1024,1024]{1,0:T(8,128)(2,1)}) %all-gather.18.cloned.1.call-update) | async-done | bytes 2097168 | tf_op jit(solution)/shard_map/all_gather | solution.py:156
  353.7 21.4 %all-gather.20.cloned.1.call-done = bf16[1024,1024]{1,0:T(8,128)(2,1)} async-done(((bf16[1024,128]{1,0:T(8,128)(2,1)}), bf16[1024,1024]{1,0:T(8,128)(2,1)}) %all-gather.20.cloned.1.call-update) | async-done | bytes 2097168 | tf_op jit(solution)/shard_map/all_gather | solution.py:158
  380.8 50.4 %all-reduce.12.cloned.1.call-done = bf16[512,1024]{1,0:T(8,128)(2,1)} async-done(((bf16[512,1024]{1,0:T(8,128)(2,1)}), bf16[512,1024]{1,0:T(8,128)(2,1)}) %all-reduce.12.cloned.1.call-update) | async-done | bytes 1048592 | tf_op jit(solution)/shard_map/psum | solution.py:49
  445.0 50.9 %all-reduce.14.cloned.1.call-done = bf16[512,1024]{1,0:T(8,128)(2,1)} async-done(((bf16[512,1024]{1,0:T(8,128)(2,1)}), bf16[512,1024]{1,0:T(8,128)(2,1)}) %all-reduce.14.cloned.1.call-update) | async-done | bytes 1048592 | tf_op jit(solution)/shard_map/psum | solution.py:49
  503.3 22.7 %multiply_reduce_fusion = (f32[2,4,256]{2,1,0:T(4,128)S(1)}, f32[2,4,256,4096]{3,2,1,0:T(8,128)}) fusion(f32[2,4,256,4096]{3,2,1,0:T(8,128)} %get-tuple-element.173, f32[2,4,256]{2,1,0:T(4,128)S(1)} %get-tuple-element.172, bf16[2,256,4,64]{1,3,2,0:T(8,128)(2,1)S(1)} %copy.135, bf16[2,4096,4,64]{1,3,2,0:T(8,128)(2,1)} %bitcast.236), kind=kOutput, calls=%fused_computation.3 | convolution fusion | flops 1098905600 | bytes 71581696 | tf_op jit(solution)/shard_map/while/body/eval_jaxpr/sbhd,skhd->shbk/dot_general | solution.py:89
  526.0 27.5 %multiply_convert_fusion = bf16[2,4,256,4096]{3,2,1,0:T(8,128)(2,1)} fusion(f32[2,4,256,4096]{3,2,1,0:T(8,128)} %get-tuple-element.176, f32[2,4,256]{2,1,0:T(4,128)S(1)} %get-tuple-element.175, f32[2,4,256,4096]{3,2,1,0:T(8,128)} %get-tuple-element.173, f32[2,4,256]{2,1,0:T(4,128)S(1)} %get-tuple-element.172), kind=kLoop, calls=%fused_computation.2 | loop fusion | flops 33554432 | bytes 83902464 | tf_op jit(solution)/shard_map/while/body/eval_jaxpr/convert_element_type | solution.py:98
  553.5 12.3 fusion.101
  569.0 51.1 %all-reduce.16.cloned.1.call-done = bf16[512,1024]{1,0:T(8,128)(2,1)} async-done(((bf16[512,1024]{1,0:T(8,128)(2,1)}), bf16[512,1024]{1,0:T(8,128)(2,1)}) %all-reduce.16.cloned.1.call-update) | async-done | bytes 1048592 | tf_op jit(solution)/shard_map/psum | solution.py:49
  642.0 11.2 multiply_convert_fusion.1
  653.2 14.7 %fusion.13 = bf16[2,4,64,4096]{3,2,1,0:T(8,128)(2,1)} fusion(bf16[2,256,4,64]{1,3,2,0:T(8,128)(2,1)S(1)} %copy-done.37, f32[2,4,256,4096]{3,2,1,0:T(8,128)} %get-tuple-element.173, f32[2,4,256]{2,1,0:T(4,128)S(1)} %get-tuple-element.172), kind=kOutput, calls=%fused_computation.22 | convolution fusion | flops 1092616192 | bytes 38019072 | tf_op jit(solution)/shard_map/while/body/eval_jaxpr/shbk,sbhd->skhd/dot_general | solution.py:99
  725.3 21.6 %reduce-scatter.39.cloned.1.call-done = bf16[2,1024,512]{1,2,0:T(8,128)(2,1)} async-done(((bf16[2,4096,512]{1,2,0:T(8,128)(2,1)}), bf16[2,1024,512]{1,2,0:T(8,128)(2,1)}) %reduce-scatter.39.cloned.1.call-update) | async-done | bytes 2097168 | tf_op jit(solution)/shard_map/reduce_scatter | solution.py:284
  780.0 13.0 all-reduce
  795.5 26.5 %reduce-scatter.43.cloned.1.call-done = bf16[128,256]{1,0:T(8,128)(2,1)} async-done(((bf16[1024,256]{1,0:T(8,128)(2,1)}), bf16[128,256]{1,0:T(8,128)(2,1)}) %reduce-scatter.43.cloned.1.call-update) | async-done | bytes 65552 | tf_op jit(solution)/shard_map/reduce_scatter | solution.py:383
  824.1 34.7 %reduce-scatter.65.cloned.1.call-done = bf16[128,3]{1,0:T(8,128)(2,1)} async-done(((bf16[1024,3]{1,0:T(8,128)(2,1)}), bf16[128,3]{1,0:T(8,128)(2,1)}) %reduce-scatter.65.cloned.1.call-update) | async-done | bytes 784
  860.3 35.1 %reduce-scatter.63.cloned.1.call-done = bf16[128,3]{1,0:T(8,128)(2,1)} async-done(((bf16[1024,3]{1,0:T(8,128)(2,1)}), bf16[128,3]{1,0:T(8,128)(2,1)}) %reduce-scatter.63.cloned.1.call-update) | async-done | bytes 784
  896.8 35.4 %reduce-scatter.61.cloned.1.call-done = bf16[128,3]{1,0:T(8,128)(2,1)} async-done(((bf16[1024,3]{1,0:T(8,128)(2,1)}), bf16[128,3]{1,0:T(8,128)(2,1)}) %reduce-scatter.61.cloned.1.call-update) | async-done | bytes 784
  933.6 36.4 %reduce-scatter.51.cloned.1.call-done = bf16[128,256]{1,0:T(8,128)(2,1)} async-done(((bf16[1024,256]{1,0:T(8,128)(2,1)}), bf16[128,256]{1,0:T(8,128)(2,1)}) %reduce-scatter.51.cloned.1.call-update) | async-done | bytes 65552
  971.6 43.1 %reduce-scatter.59.cloned.1.call-done = bf16[128,1024]{1,0:T(8,128)(2,1)} async-done(((bf16[1024,1024]{1,0:T(8,128)(2,1)}), bf16[128,1024]{1,0:T(8,128)(2,1)}) %reduce-scatter.59.cloned.1.call-update) | async-done | bytes 262160
  1016.7 42.6 %reduce-scatter.45.cloned.1.call-done = bf16[128,1024]{1,0:T(8,128)(2,1)} async-done(((bf16[1024,1024]{1,0:T(8,128)(2,1)}), bf16[128,1024]{1,0:T(8,128)(2,1)}) %reduce-scatter.45.cloned.1.call-update) | async-done | bytes 262160 | tf_op jit(solution)/shard_map/reduce_scatter | solution.py:395
  1061.1 32.8 %reduce-scatter.49.cloned.1.call-done = bf16[16,4]{1,0:T(8,128)(2,1)} async-done(((bf16[128,4]{1,0:T(8,128)(2,1)}), bf16[16,4]{1,0:T(8,128)(2,1)}) %reduce-scatter.49.cloned.1.call-update) | async-done | bytes 144
  1095.2 52.9 %all-reduce.18.cloned.1.call-done = bf16[512,1024]{1,0:T(8,128)(2,1)} async-done(((bf16[512,1024]{1,0:T(8,128)(2,1)}), bf16[512,1024]{1,0:T(8,128)(2,1)}) %all-reduce.18.cloned.1.call-update) | async-done | bytes 1048592 | tf_op jit(solution)/shard_map/psum | solution.py:49
  1150.9 38.6 %reduce-scatter.47.cloned.1.call-done = bf16[128,768]{1,0:T(8,128)(2,1)} async-done(((bf16[1024,768]{1,0:T(8,128)(2,1)}), bf16[128,768]{1,0:T(8,128)(2,1)}) %reduce-scatter.47.cloned.1.call-update) | async-done | bytes 196624
  1191.6 33.0 %reduce-scatter.55.cloned.1.call-done = bf16[16,4]{1,0:T(8,128)(2,1)} async-done(((bf16[128,4]{1,0:T(8,128)(2,1)}), bf16[16,4]{1,0:T(8,128)(2,1)}) %reduce-scatter.55.cloned.1.call-update) | async-done | bytes 144
  1225.9 38.3 %reduce-scatter.53.cloned.1.call-done = bf16[128,512]{1,0:T(8,128)(2,1)} async-done(((bf16[1024,512]{1,0:T(8,128)(2,1)}), bf16[128,512]{1,0:T(8,128)(2,1)}) %reduce-scatter.53.cloned.1.call-update) | async-done | bytes 131088
  1266.1 77.0 %reduce-scatter.41.cloned.1.call-done = bf16[2,1024,256]{2,1,0:T(8,128)(2,1)} async-done(((bf16[2,1024,1024]{2,1,0:T(8,128)(2,1)}), bf16[2,1024,256]{2,1,0:T(8,128)(2,1)}) %reduce-scatter.41.cloned.1.call-update) | async-done | bytes 1048592 | tf_op jit(solution)/shard_map/reduce_scatter | solution.py:307
  (395 shorter events, 322.4 us)
Async XLA Ops:
  7.2 31.9 %all-gather.10.cloned.1.call-start = ((), (), s32[]{:S(2)}) async-start(), calls=%async_computation.15 | async-start | bytes 1769472 | tf_op jit(solution)/shard_map/all_gather | solution.py:149
  9.0 60.3 %all-gather.12.cloned.1.call-start = ((), (), s32[]{:S(2)}) async-start(), calls=%async_computation.16 | async-start | bytes 2621440 | tf_op jit(solution)/shard_map/all_gather | solution.py:184
  44.2 51.2 %all-gather.14.cloned.1.call-start = ((), (), s32[]{:S(2)}) async-start(), calls=%async_computation.18 | async-start | bytes 1179648 | tf_op jit(solution)/shard_map/all_gather | solution.py:153
  45.1 112.0 %all-reduce.8.cloned.1.call-start = ((), (), s32[]{:S(2)}) async-start(), calls=%async_computation.17 | async-start | bytes 2097152 | tf_op jit(solution)/shard_map/psum | solution.py:49
  85.2 125.7 %all-gather.16.cloned.1.call-start = ((), (), s32[]{:S(2)}) async-start(), calls=%async_computation.19 | async-start | bytes 10485760 | tf_op jit(solution)/shard_map/all_gather | solution.py:204
  111.9 203.9 %all-reduce.10.cloned.1.call-start = ((), (), s32[]{:S(2)}) async-start(), calls=%async_computation.20 | async-start | bytes 2097152 | tf_op jit(solution)/shard_map/psum | solution.py:49
  156.9 105.4 %copy-start.19 = (bf16[256,1024]{1,0:T(8,128)(2,1)}, bf16[256,1024]{1,0:T(8,128)(2,1)S(1)}, u32[]{:S(2)}) copy-start(bf16[256,1024]{1,0:T(8,128)(2,1)S(1)} %all_gather.56) | copy-start | bytes 1572868
  160.3 339.8 %copy-start = (bf16[512,1024]{1,0:T(8,128)(2,1)}, bf16[512,1024]{1,0:T(8,128)(2,1)S(1)}, u32[]{:S(2)}) copy-start(bf16[512,1024]{1,0:T(8,128)(2,1)S(1)} %add_convert_fusion.4) | copy-start | bytes 3145732
  161.2 68.4 %copy-start.34 = (bf16[2,256,4,64]{1,3,2,0:T(8,128)(2,1)}, bf16[2,256,4,64]{1,3,2,0:T(8,128)(2,1)S(1)}, u32[]{:S(2)}) copy-start(bf16[2,256,4,64]{1,3,2,0:T(8,128)(2,1)S(1)} %copy.131) | copy-start | bytes 786436
  263.8 81.2 %all-gather.18.cloned.1.call-start = ((), (), s32[]{:S(2)}) async-start(), calls=%async_computation.21 | async-start | bytes 2359296 | tf_op jit(solution)/shard_map/all_gather | solution.py:156
  264.5 110.5 %all-gather.20.cloned.1.call-start = ((), (), s32[]{:S(2)}) async-start(), calls=%async_computation.22 | async-start | bytes 2359296 | tf_op jit(solution)/shard_map/all_gather | solution.py:158
  265.3 165.9 %all-reduce.12.cloned.1.call-start = ((), (), s32[]{:S(2)}) async-start(), calls=%async_computation.23 | async-start | bytes 2097152 | tf_op jit(solution)/shard_map/psum | solution.py:49
  318.7 117.3 %copy-start.9 = (bf16[512,1024]{1,0:T(8,128)(2,1)}, bf16[512,1024]{1,0:T(8,128)(2,1)S(1)}, u32[]{:S(2)}) copy-start(bf16[512,1024]{1,0:T(8,128)(2,1)S(1)} %add_convert_fusion.2) | copy-start | bytes 3145732
  379.2 116.7 %all-reduce.14.cloned.1.call-start = ((), (), s32[]{:S(2)}) async-start(), calls=%async_computation.24 | async-start | bytes 2097152 | tf_op jit(solution)/shard_map/psum | solution.py:49
  444.6 175.5 %all-reduce.16.cloned.1.call-start = ((), (), s32[]{:S(2)}) async-start(), calls=%async_computation.25 | async-start | bytes 2097152 | tf_op jit(solution)/shard_map/psum | solution.py:49
  565.8 54.3 %copy-start.3 = (bf16[2,256,1024]{2,1,0:T(8,128)(2,1)S(1)}, bf16[2,256,1024]{2,1,0:T(8,128)(2,1)}, u32[]{:S(2)}) copy-start(bf16[2,256,1024]{2,1,0:T(8,128)(2,1)} %param.16) | copy-start | bytes 3145732
  568.7 139.3 %reduce-scatter.37.cloned.1.call-start = ((), (), s32[]{:S(2)}) async-start(), calls=%async_computation.26 | async-start | bytes 2621440 | tf_op jit(solution)/shard_map/reduce_scatter | solution.py:342
  641.1 105.8 %reduce-scatter.39.cloned.1.call-start = ((), (), s32[]{:S(2)}) async-start(), calls=%async_computation.28 | async-start | bytes 10485760 | tf_op jit(solution)/shard_map/reduce_scatter | solution.py:284
  675.8 118.1 %reduce-scatter.57.cloned.1.call-start = ((), (), s32[]{:S(2)}) async-start(), calls=%async_computation.37 | async-start | bytes 589824
  680.2 141.8 %reduce-scatter.43.cloned.1.call-start = ((), (), s32[]{:S(2)}) async-start(), calls=%async_computation.30 | async-start | bytes 589824 | tf_op jit(solution)/shard_map/reduce_scatter | solution.py:383
  681.8 177.1 %reduce-scatter.65.cloned.1.call-start = ((), (), s32[]{:S(2)}) async-start(), calls=%async_computation.41 | async-start | bytes 294912
  684.6 210.8 %reduce-scatter.63.cloned.1.call-start = ((), (), s32[]{:S(2)}) async-start(), calls=%async_computation.40 | async-start | bytes 294912
  685.6 246.6 %reduce-scatter.61.cloned.1.call-start = ((), (), s32[]{:S(2)}) async-start(), calls=%async_computation.39 | async-start | bytes 294912
  686.6 283.4 %reduce-scatter.51.cloned.1.call-start = ((), (), s32[]{:S(2)}) async-start(), calls=%async_computation.34 | async-start | bytes 589824
  688.1 326.6 %reduce-scatter.59.cloned.1.call-start = ((), (), s32[]{:S(2)}) async-start(), calls=%async_computation.38 | async-start | bytes 2359296
  697.2 362.1 %reduce-scatter.45.cloned.1.call-start = ((), (), s32[]{:S(2)}) async-start(), calls=%async_computation.31 | async-start | bytes 2359296 | tf_op jit(solution)/shard_map/reduce_scatter | solution.py:395
  702.5 391.4 %reduce-scatter.49.cloned.1.call-start = ((), (), s32[]{:S(2)}) async-start(), calls=%async_computation.33 | async-start | bytes 36864
  711.0 437.0 %all-reduce.18.cloned.1.call-start = ((), (), s32[]{:S(2)}) async-start(), calls=%async_computation.27 | async-start | bytes 2097152 | tf_op jit(solution)/shard_map/psum | solution.py:49
  714.7 474.7 %reduce-scatter.47.cloned.1.call-start = ((), (), s32[]{:S(2)}) async-start(), calls=%async_computation.32 | async-start | bytes 1769472
  725.3 499.3 %reduce-scatter.55.cloned.1.call-start = ((), (), s32[]{:S(2)}) async-start(), calls=%async_computation.36 | async-start | bytes 36864
  758.9 505.4 %reduce-scatter.53.cloned.1.call-start = ((), (), s32[]{:S(2)}) async-start(), calls=%async_computation.35 | async-start | bytes 1179648
  771.5 571.6 %reduce-scatter.41.cloned.1.call-start = ((), (), s32[]{:S(2)}) async-start(), calls=%async_computation.29 | async-start | bytes 5242880 | tf_op jit(solution)/shard_map/reduce_scatter | solution.py:307
  (69 other events, 660.4 us)
Sparse Core Ops, SparseCore 0:
  10.5 28.5 all-gather.9
  44.3 24.9 all-gather.11
  71.8 23.5 all-gather.13
  98.2 51.8 all-reduce.7
  152.1 58.7 all-gather.15
  263.9 51.8 all-reduce.9
  317.6 27.2 all-gather.17
  346.8 28.1 all-gather.19
  379.3 51.8 all-reduce.11
  444.7 51.1 all-reduce.13
  568.9 51.1 all-reduce.15
  641.2 30.7 reduce-scatter.36
  675.9 71.0 reduce-scatter.38
  750.2 34.1 reduce-scatter.56
  787.9 34.1 reduce-scatter.42
  825.2 33.6 reduce-scatter.64
  861.7 33.5 reduce-scatter.62
  898.5 33.5 reduce-scatter.60
  935.8 34.1 reduce-scatter.50
  973.4 41.2 reduce-scatter.58
  1018.0 41.2 reduce-scatter.44
  1062.5 31.2 reduce-scatter.48
  1096.2 51.7 all-reduce.17
  1151.6 37.8 reduce-scatter.46
  1193.3 31.2 reduce-scatter.54
  1228.2 36.0 reduce-scatter.52
  1266.4 76.7 reduce-scatter.40
where the time goes:
time: 1360 us; the launch traced here: 1350 us
  waiting for transfers between devices  873 us (64%)
  matrix products  181 us (13%)
  blocking collectives  97.1 us (7%)
  local copies, waits for them, and re-layouts  93.2 us (7%)
  other arithmetic  89 us (7%)
  between operations  16.8 us (1%)
    unnamed x37, waiting for transfers between devices  329 us
    psum x6, waiting for transfers between devices, head_total(): return lax.psum(values.astype(jnp.bfloat16), 'tp').astype(jnp.float32)  247 us
    reduce_scatter x1, waiting for transfers between devices, body(): lax.psum_scatter(encoder_part.reshape(seq_count, -1, model_width).astype(...  77 us
    all_gather x1, waiting for transfers between devices, body(): all_enc = lax.all_gather(enc_pairs, 'ctx', axis=1, tiled=True)  49.6 us
    unnamed x182, local copies, waits for them, and re-layouts  49.3 us
    reduce_scatter x1, waiting for transfers between devices, body(): lax.psum_scatter(up_grad.astype(jnp.bfloat16), ('dp', 'ctx'), scatter_dim...  42.6 us
    convert_element_type x2, other arithmetic, attend_backward(): (attention_weights * (prob_grad - inner_sum)).astype(jnp.bfloat16)  28.8 us
    dot_general x2, matrix products, prob_grads(): jnp.einsum('sbhd,skhd->shbk', grad_heads, value_heads, preferred_element_...  27.2 us
  transfers between devices with their start and end apart: 27, of which 24 were waited for; matrix products, arithmetic and copies ran while one was open for 14% of the time, Pallas kernels for 0%

commit v1 on v0

v1 whole, which is shorter than its diff:
```python
import functools

import jax
import jax.numpy as jnp
from jax import lax
from jax.experimental import pallas as pl
from jax.experimental.pallas import tpu as pltpu
from jax.sharding import PartitionSpec as P

EPSILON = 1e-05
HEAD = 64
KEY_TILE = 512
VMEM_BYTES = 50 * 1024 * 1024
PLANE = ("dp", "ctx")
HEADS = ("tp", "ctx")
F32 = jnp.float32
BF16 = jnp.bfloat16


def contract(left, right, left_dim, right_dim):
    return lax.dot_general(
        left, right, (((left_dim,), (right_dim,)), ((), ())), preferred_element_type=F32
    )


def norm_forward(values, norm_gain, norm_shift):
    row_mean = jnp.mean(values, -1, keepdims=True)
    centered = values - row_mean
    inv_std = lax.rsqrt(jnp.mean(centered * centered, -1, keepdims=True) + EPSILON)
    normed = centered * inv_std
    return (normed * norm_gain + norm_shift, normed, inv_std)


def norm_backward(gradient, normed, inv_std, norm_gain):
    gain_grad = jnp.sum(gradient * normed, 0)
    shift_grad = jnp.sum(gradient, 0)
    scaled = gradient * norm_gain
    input_part = inv_std * (
        scaled
        - jnp.mean(scaled, -1, keepdims=True)
        - normed * jnp.mean(scaled * normed, -1, keepdims=True)
    )
    return (input_part, gain_grad, shift_grad)


def root_mean(values):
    return jnp.sqrt(jnp.mean(values * values, -1))


def exact_gelu(values):
    return jax.nn.gelu(values, approximate=False)


def with_zeros_below(values):
    return jnp.concatenate([values, jnp.zeros_like(values)], 0)


def with_zeros_above(values):
    return jnp.concatenate([jnp.zeros_like(values), values], 0)


def gather_chunks(ref):
    halves, blocks = ref.shape[:2]
    return jnp.concatenate([ref[h, b] for h in range(halves) for b in range(blocks)], 1)


def self_forward_kernel(x_ref, w_ref, bq_ref, bv_ref, q_ref, kv_ref, o_ref, lse_ref):
    tokens = x_ref[0]
    weights = w_ref[...]
    halves, blocks, _, part = o_ref.shape
    block = halves * part
    scale = HEAD**-0.5
    query = (contract(weights[:HEAD], tokens, 1, 1) + bq_ref[...]).astype(BF16) * scale
    pair = (contract(tokens, weights[HEAD:], 1, 1) + bv_ref[...]).astype(BF16)
    q_ref[0] = query
    kv_ref[0] = pair
    for i in range(blocks):
        keys = pair[: (i + 1) * block]
        scores = contract(keys, with_zeros_below(query[:, i * block : (i + 1) * block]), 1, 0)
        top = jnp.max(scores, 0, keepdims=True)
        weight = jnp.exp(scores - top)
        total = jnp.sum(weight, 0, keepdims=True)
        mixed = contract(keys, weight.astype(BF16), 0, 0)[HEAD:]
        out = (mixed / total).astype(BF16)
        for h in range(halves):
            o_ref[h, i] = out[:, h * part : (h + 1) * part]
        lse_ref[0, :, i * block : (i + 1) * block] = top + jnp.log(total)


def cross_forward_kernel(q_ref, *refs):
    kv_refs, (o_ref, lse_ref) = refs[:-2], refs[-2:]
    halves, blocks, _, part = q_ref.shape
    query = with_zeros_below(gather_chunks(q_ref))
    top = total = mixed = None
    for kv_ref in kv_refs:
        for start in range(0, kv_ref.shape[1], KEY_TILE):
            pair = kv_ref[0, start : start + KEY_TILE]
            scores = contract(pair, query, 1, 0)
            tile_top = jnp.max(scores, 0, keepdims=True)
            new_top = tile_top if top is None else jnp.maximum(top, tile_top)
            weight = jnp.exp(scores - new_top)
            tile_total = jnp.sum(weight, 0, keepdims=True)
            tile_mixed = contract(pair, weight.astype(BF16), 0, 0)
            if top is None:
                total, mixed = tile_total, tile_mixed
            else:
                fade = jnp.exp(top - new_top)
                total = total * fade + tile_total
                mixed = mixed * fade + tile_mixed
            top = new_top
    out = (mixed[HEAD:] / total).astype(BF16)
    for h in range(halves):
        for b in range(blocks):
            at = (h * blocks + b) * part
            o_ref[h, b] = out[:, at : at + part]
    lse_ref[0] = top + jnp.log(total)


def cross_backward_kernel(q_ref, o_ref, do_ref, lse_ref, *refs):
    count = (len(refs) - 1) // 2
    kv_refs, dkv_refs, dq_ref = refs[:count], refs[count:-1], refs[-1]
    halves, blocks, _, part = q_ref.shape
    width = halves * blocks * part
    query = with_zeros_below(gather_chunks(q_ref))
    grad = gather_chunks(do_ref)
    inner = jnp.sum(
        grad.astype(F32) * gather_chunks(o_ref).astype(F32), 0, keepdims=True
    )
    grad = with_zeros_above(grad)
    both = jnp.concatenate([query, grad], 1)
    lse = lse_ref[0]
    query_grad = None
    for kv_ref, dkv_ref in zip(kv_refs, dkv_refs):
        for start in range(0, kv_ref.shape[1], KEY_TILE):
            pair = kv_ref[0, start : start + KEY_TILE]
            products = contract(pair, both, 1, 0)
            weight = jnp.exp(products[:, :width] - lse)
            slope = (weight * (products[:, width:] - inner)).astype(BF16)
            dkv_ref[0, start : start + KEY_TILE] = (
                contract(slope, query, 1, 1) + contract(weight.astype(BF16), grad, 1, 1)
            ).astype(BF16)
            part_grad = contract(pair, slope, 0, 0)
            query_grad = part_grad if query_grad is None else query_grad + part_grad
    out = (query_grad[:HEAD] * HEAD**-0.5).astype(BF16)
    for h in range(halves):
        for b in range(blocks):
            at = (h * blocks + b) * part
            dq_ref[h, b] = out[:, at : at + part]


def self_backward_kernel(
    x_ref, q_ref, kv_ref, o_ref, do_ref, lse_ref, grad_ref, dw_ref, db_ref, dkv_ref
):
    halves, blocks, _, part = o_ref.shape
    block = halves * part
    dkv_ref[...] = jnp.zeros_like(dkv_ref)
    parts = []
    for i in range(blocks):
        lanes = slice(i * block, (i + 1) * block)
        reach = (i + 1) * block
        keys = kv_ref[0, :reach]
        query = with_zeros_below(q_ref[0, :, lanes])
        grad = jnp.concatenate([do_ref[h, i] for h in range(halves)], 1)
        mixed = jnp.concatenate([o_ref[h, i] for h in range(halves)], 1)
        inner = jnp.sum(grad.astype(F32) * mixed.astype(F32), 0, keepdims=True)
        grad = with_zeros_above(grad)
        weight = jnp.exp(contract(keys, query, 1, 0) - lse_ref[0, :, lanes])
        slope = (weight * (contract(keys, grad, 1, 0) - inner)).astype(BF16)
        parts.append(contract(keys, slope, 0, 0)[:HEAD] * HEAD**-0.5)
        dkv_ref[:, :reach] += contract(query, slope, 1, 1) + contract(
            grad, weight.astype(BF16), 1, 1
        )
    grads = jnp.concatenate(
        [jnp.concatenate(parts, 1).astype(BF16), dkv_ref[...].astype(BF16)], 0
    )
    for i in range(blocks):
        for h in range(halves):
            at = i * block + h * part
            grad_ref[h, i] = grads[:, at : at + part]

    @pl.when(pl.program_id(0) == 0)
    def _():
        dw_ref[...] = jnp.zeros_like(dw_ref)
        db_ref[...] = jnp.zeros_like(db_ref)

    dw_ref[...] += contract(grads, x_ref[0], 1, 0)
    db_ref[...] += jnp.sum(grads.astype(F32), 1, keepdims=True)


def by_first(shape, lead=1):
    return pl.BlockSpec((lead,) + shape[1:], lambda s: (s,) + (0,) * (len(shape) - 1))


def whole(shape):
    return pl.BlockSpec(shape, lambda s: (0,) * len(shape))


def shaped(shape, dtype):
    return jax.ShapeDtypeStruct(shape, dtype)


def call(kernel, seqs, in_specs, out_specs, out_shape, operands, cost, scratch=()):
    flops, transcendentals = cost
    moved = sum(o.size * o.dtype.itemsize for o in operands)
    moved += sum(o.size * o.dtype.itemsize for o in out_shape)
    return pl.pallas_call(
        kernel,
        grid=(seqs,),
        in_specs=in_specs,
        out_specs=out_specs,
        out_shape=out_shape,
        scratch_shapes=scratch,
        compiler_params=pltpu.CompilerParams(
            dimension_semantics=("arbitrary",), vmem_limit_bytes=VMEM_BYTES
        ),
        cost_estimate=pl.CostEstimate(
            flops=flops, bytes_accessed=moved, transcendentals=transcendentals
        ),
    )(*operands)


def self_forward(x_all, weights, query_bias, pair_bias, chunk_shape):
    seqs, length, width = x_all.shape
    halves = chunk_shape[0] // seqs
    query, pair, lse = (seqs, HEAD, length), (seqs, length, 2 * HEAD), (seqs, 1, length)
    return call(
        self_forward_kernel,
        seqs,
        [by_first(x_all.shape), whole(weights.shape), whole(query_bias.shape), whole(pair_bias.shape)],
        [by_first(query), by_first(pair), by_first(chunk_shape, halves), by_first(lse)],
        [shaped(query, BF16), shaped(pair, BF16), shaped(chunk_shape, BF16), shaped(lse, F32)],
        [x_all, weights, query_bias, pair_bias],
        (seqs * length * (2 * width * 3 * HEAD + 8 * length * HEAD), seqs * length * length),
    )


def cross_forward(query, pairs):
    seqs = pairs[0].shape[0]
    halves, blocks, _, part = query.shape
    halves //= seqs
    length = halves * blocks * part
    keys = sum(p.shape[1] for p in pairs)
    lse = (seqs, 1, length)
    return call(
        cross_forward_kernel,
        seqs,
        [by_first(query.shape, halves)] + [by_first(p.shape) for p in pairs],
        [by_first(query.shape, halves), by_first(lse)],
        [shaped(query.shape, BF16), shaped(lse, F32)],
        [query, *pairs],
        (seqs * length * keys * 8 * HEAD, seqs * length * keys),
    )


def cross_backward(query, mixed, grad, lse, pairs):
    seqs = pairs[0].shape[0]
    halves, blocks, _, part = query.shape
    halves //= seqs
    length = halves * blocks * part
    keys = sum(p.shape[1] for p in pairs)
    chunk = by_first(query.shape, halves)
    return call(
        cross_backward_kernel,
        seqs,
        [chunk, chunk, chunk, by_first(lse.shape)] + [by_first(p.shape) for p in pairs],
        [by_first(p.shape) for p in pairs] + [chunk],
        [shaped(p.shape, BF16) for p in pairs] + [shaped(query.shape, BF16)],
        [query, mixed, grad, lse, *pairs],
        (seqs * length * keys * 20 * HEAD, seqs * length * keys),
    )


def self_backward(x_all, query, pair, mixed, grad, lse):
    seqs, length, width = x_all.shape
    halves = mixed.shape[0] // seqs
    chunk = by_first(mixed.shape, halves)
    out = mixed.shape[:2] + (3 * HEAD, mixed.shape[3])
    return call(
        self_backward_kernel,
        seqs,
        [by_first(x_all.shape), by_first(query.shape), by_first(pair.shape), chunk, chunk, by_first(lse.shape)],
        [by_first(out, halves), whole((3 * HEAD, width)), whole((3 * HEAD, 1))],
        [shaped(out, BF16), shaped((3 * HEAD, width), F32), shaped((3 * HEAD, 1), F32)],
        [x_all, query, pair, mixed, grad, lse],
        (seqs * length * (2 * width * 3 * HEAD + 20 * length * HEAD), seqs * length * length),
        [pltpu.VMEM((2 * HEAD, length), F32)],
    )


def body(
    hidden_in,
    encoder_states,
    out_cotangent,
    self_proj,
    self_qv_bias,
    self_out_proj,
    cross_q_proj,
    cross_kv_proj,
    cross_qv_bias,
    cross_out_proj,
    up_proj,
    up_bias,
    down_proj,
    norm_gain,
    norm_bias,
    out_bias,
):
    blocks, ranks = lax.axis_size("ctx"), lax.axis_size("tp")
    plane = lax.axis_size("dp") * blocks
    own_ctx, own_tp = lax.axis_index("ctx"), lax.axis_index("tp")
    seqs, block, width = hidden_in.shape
    rows = seqs * block
    part = rows // ranks
    shard = width // plane
    heads_here = self_qv_bias.shape[0]
    local_width = heads_here * HEAD
    all_heads = heads_here * ranks
    enc_len = encoder_states.shape[1]
    hidden = up_proj.shape[1]
    slots = range(blocks)

    def ctx_swap(values, k):
        return lax.ppermute(values, "ctx", [(i, i ^ k) for i in slots])

    def tp_swap(values, k):
        return lax.ppermute(values, "tp", [(i, i ^ k) for i in range(ranks)])

    def exchange(values):
        return lax.all_to_all(values, HEADS, split_axis=0, concat_axis=0, tiled=True)

    def own_rows(values):
        return lax.dynamic_slice_in_dim(values.reshape(rows, width), own_tp * part, part, 0)

    def in_swap_order(values, axis):
        return [lax.dynamic_index_in_dim(values, own_ctx ^ k, axis, keepdims=False) for k in slots]

    x_all = lax.all_gather(hidden_in, "ctx", axis=1, tiled=True)
    small = jnp.concatenate(
        [v.reshape(-1) for v in (norm_gain, norm_bias, out_bias, self_qv_bias, cross_qv_bias, up_bias)]
    )
    small = lax.all_gather(small, ("dp", "ctx", "tp")).reshape(plane, ranks, -1)
    vectors = small[:, 0, : 9 * shard].reshape(plane, 9, shard).swapaxes(0, 1).reshape(9, width)
    vectors = vectors.astype(F32)
    gains, shifts, branch_bias = vectors[:3], vectors[3:6], vectors[6:]
    at = 9 * shard
    bias_part = 2 * HEAD // plane
    count = heads_here * bias_part

    def head_bias(values):
        values = values.reshape(plane, ranks, heads_here, bias_part)
        return values.transpose(1, 2, 0, 3).reshape(all_heads, 2 * HEAD).astype(F32)

    self_bias = head_bias(small[:, :, at : at + count])
    cross_bias = head_bias(small[:, :, at + count : at + 2 * count])
    up_vector = (
        small[:, :, at + 2 * count :]
        .reshape(plane, ranks, hidden // (up_bias.shape[1] * plane), up_bias.shape[1])
        .transpose(1, 2, 0, 3)
        .reshape(ranks, hidden)
        .astype(F32)
    )
    up_vector = jnp.concatenate(
        [
            lax.dynamic_index_in_dim(up_vector, own_tp, 0, keepdims=False),
            lax.dynamic_index_in_dim(up_vector, own_tp ^ 2, 0, keepdims=False),
        ]
    )

    own_head = (
        self_proj.reshape(3, shard, heads_here, HEAD).transpose(2, 0, 3, 1).reshape(blocks, 3 * HEAD, shard)
    )
    own_head = lax.all_to_all(own_head, "ctx", split_axis=0, concat_axis=0, tiled=True)
    own_head = lax.all_gather(own_head, "dp")
    own_head = own_head.transpose(2, 0, 1, 3).reshape(3 * HEAD, width)

    kv_weights = cross_kv_proj.reshape(2, shard, heads_here, HEAD).transpose(1, 2, 0, 3)
    kv_weights = lax.all_gather(
        kv_weights.reshape(shard, heads_here * 2 * HEAD), PLANE, axis=0, tiled=True
    )
    square = jnp.stack(
        [self_proj[0], self_proj[1], self_proj[2], cross_q_proj, self_out_proj.T, cross_out_proj.T]
    )
    square = lax.all_gather(square, "tp", axis=2, tiled=True)
    square = square.transpose(1, 0, 2).reshape(shard, 6 * width)
    square = lax.all_gather(square, PLANE, axis=0, tiled=True)
    proj_q, proj_k, proj_v, cross_q_all, self_out_all, cross_out_all = (
        square[:, i * width : (i + 1) * width] for i in range(6)
    )
    mlp = jnp.concatenate([up_proj, down_proj.T], 1)
    mlp_other = tp_swap(mlp, 2)
    mlp = jnp.concatenate(
        [mlp[:, :hidden], mlp_other[:, :hidden], mlp[:, hidden:], mlp_other[:, hidden:]], 1
    )
    mlp = lax.all_gather(mlp, PLANE, axis=0, tiled=True)
    up_all, down_all = mlp[:, : 2 * hidden], mlp[:, 2 * hidden :]

    head_row = lax.dynamic_index_in_dim(self_bias, own_tp * blocks + own_ctx, 0, keepdims=False)
    query_column = head_row[:HEAD].reshape(HEAD, 1)
    pair_row = jnp.concatenate([jnp.zeros((HEAD,), F32), head_row[HEAD:]]).reshape(1, 2 * HEAD)
    chunk_shape = (ranks, blocks, HEAD, part)
    self_query, self_pair, self_mixed, self_lse = self_forward(
        x_all, own_head, query_column, pair_row, chunk_shape
    )
    tokens_f = own_rows(hidden_in).astype(F32)
    mixed_t = exchange(self_mixed.reshape(all_heads, HEAD, part)).reshape(width, part)
    attn_branch = contract(mixed_t, self_out_all, 0, 1) + branch_bias[0]
    first_out, first_normed, first_inv = norm_forward(tokens_f + attn_branch, gains[0], shifts[0])
    first_low = first_out.astype(BF16)
    cross_query = (
        contract(cross_q_all, first_low, 0, 1) + cross_bias[:, :HEAD].reshape(width, 1)
    ).astype(BF16) * HEAD**-0.5
    cross_query = exchange(cross_query.reshape(all_heads, HEAD, part)).reshape(chunk_shape)

    enc_rows = encoder_states.reshape(-1, width)
    kv_slots = in_swap_order(kv_weights.reshape(width, heads_here, 2 * HEAD), 1)
    kv_weights = jnp.concatenate(kv_slots, 1)
    value_bias = lax.dynamic_slice_in_dim(cross_bias, own_tp * heads_here, heads_here, 0)
    value_bias = jnp.concatenate([jnp.zeros((heads_here, HEAD), F32), value_bias[:, HEAD:]], 1)
    value_bias = jnp.concatenate(in_swap_order(value_bias, 0))
    enc_pairs = (contract(enc_rows, kv_weights, 1, 0) + value_bias).astype(BF16)
    pairs = []
    for k in slots:
        pair = enc_pairs[:, k * 2 * HEAD : (k + 1) * 2 * HEAD].reshape(seqs, enc_len, 2 * HEAD)
        pairs.append(ctx_swap(pair, k) if k else pair)
    cross_mixed, cross_lse = cross_forward(cross_query, pairs)
    cross_t = exchange(cross_mixed.reshape(all_heads, HEAD, part)).reshape(width, part)
    cross_branch = contract(cross_t, cross_out_all, 0, 1) + branch_bias[1]
    second_out, second_normed, second_inv = norm_forward(
        first_low.astype(F32) + cross_branch, gains[1], shifts[1]
    )
    second_low = second_out.astype(BF16)

    two = jnp.concatenate([second_low, tp_swap(second_low, 1)])
    pre_act = contract(two, up_all, 1, 0) + up_vector
    active = exact_gelu(pre_act).astype(BF16)
    mlp_part = contract(active, down_all, 1, 1)
    mlp_branch = (
        mlp_part[:part] + tp_swap(mlp_part[part:].astype(BF16), 1).astype(F32) + branch_bias[2]
    )
    third_out, third_normed, third_inv = norm_forward(
        second_low.astype(F32) + mlp_branch, gains[2], shifts[2]
    )
    hidden_out = lax.all_gather(third_out.astype(BF16), "tp", axis=0, tiled=True)
    rms = jnp.stack([root_mean(attn_branch), root_mean(cross_branch), root_mean(mlp_branch)])
    rms = lax.all_gather(rms, "tp", axis=1, tiled=True)
    rms = jnp.concatenate([root_mean(hidden_in.reshape(rows, width).astype(F32))[None], rms])

    out_grad = own_rows(out_cotangent).astype(F32)
    third_grad, gain_two, shift_two = norm_backward(out_grad, third_normed, third_inv, gains[2])
    mlp_bias_grad = jnp.sum(third_grad, 0)
    mlp_low = third_grad.astype(BF16)
    mlp_low = jnp.concatenate([mlp_low, tp_swap(mlp_low, 1)])
    active_grad = contract(mlp_low, down_all, 1, 0)
    pre_low = jax.vjp(exact_gelu, pre_act)[1](active_grad)[0].astype(BF16)
    back_part = contract(pre_low, up_all, 1, 1)
    back = back_part[:part] + tp_swap(back_part[part:].astype(BF16), 1).astype(F32)
    up_bias_grad = jnp.sum(pre_low.astype(F32), 0).reshape(2, hidden)
    mlp_grad = jnp.concatenate(
        [contract(two, pre_low, 0, 0).astype(BF16), contract(mlp_low, active, 0, 0).astype(BF16)], 1
    )
    mlp_grad = lax.psum_scatter(mlp_grad, PLANE, scatter_dimension=0, tiled=True)
    mlp_grad = mlp_grad.reshape(shard, 2, 2, hidden)
    mlp_grad = mlp_grad[:, :, 0].astype(F32) + tp_swap(mlp_grad[:, :, 1], 2).astype(F32)
    up_out, down_out = mlp_grad[:, 0], mlp_grad[:, 1].T

    second_grad, gain_one, shift_one = norm_backward(
        third_grad + back, second_normed, second_inv, gains[1]
    )
    cross_bias_sum = jnp.sum(second_grad, 0)
    second_grad_low = second_grad.astype(BF16)
    cross_out_grad = contract(second_grad_low, cross_t, 0, 1).astype(BF16)
    mix_grad = contract(cross_out_all, second_grad_low, 0, 1).astype(BF16)
    mix_grad = exchange(mix_grad.reshape(all_heads, HEAD, part)).reshape(chunk_shape)
    *pair_grads, query_grad = cross_backward(cross_query, cross_mixed, mix_grad, cross_lse, pairs)
    query_grad = exchange(query_grad.reshape(all_heads, HEAD, part)).reshape(width, part)
    pair_grads = [ctx_swap(g, k) if k else g for k, g in enumerate(pair_grads)]
    pair_grads = jnp.concatenate([g.reshape(-1, 2 * HEAD) for g in pair_grads], 1)
    enc_part = contract(pair_grads, kv_weights, 1, 1).astype(BF16)
    encoder_grad = lax.psum_scatter(
        enc_part.reshape(seqs, enc_len, width), "tp", scatter_dimension=2, tiled=True
    ).astype(F32)
    kv_grad = contract(enc_rows, pair_grads, 0, 0).astype(BF16)
    kv_grad = jnp.concatenate(in_swap_order(kv_grad.reshape(width, heads_here, 2 * HEAD), 1), 1)
    kv_grad = lax.psum_scatter(kv_grad, PLANE, scatter_dimension=0, tiled=True).astype(F32)
    kv_grad = kv_grad.reshape(shard, heads_here, 2, HEAD).transpose(2, 0, 1, 3).reshape(2, shard, local_width)
    value_sum = jnp.sum(pair_grads.astype(F32), 0).reshape(heads_here, 2 * HEAD)
    value_sum = jnp.stack(in_swap_order(value_sum, 0))[:, HEAD:]
    query_sum = jnp.sum(query_grad.astype(F32), 1).reshape(all_heads, HEAD)

    cross_q_grad = contract(first_low, query_grad, 0, 1).astype(BF16)
    first_grad, gain_zero, shift_zero = norm_backward(
        second_grad + contract(query_grad, cross_q_all, 0, 1), first_normed, first_inv, gains[0]
    )
    attn_bias_sum = jnp.sum(first_grad, 0)
    first_grad_low = first_grad.astype(BF16)
    self_out_grad = contract(first_grad_low, mixed_t, 0, 1).astype(BF16)
    square_grad = jnp.concatenate([self_out_grad, cross_q_grad, cross_out_grad], 1)
    square_grad = lax.psum_scatter(square_grad, PLANE, scatter_dimension=0, tiled=True)
    square_grad = lax.psum_scatter(
        square_grad.reshape(shard, 3, width), "tp", scatter_dimension=2, tiled=True
    ).astype(F32)
    self_out_out, cross_q_out, cross_out_out = (
        square_grad[:, 0].T,
        square_grad[:, 1],
        square_grad[:, 2].T,
    )
    self_mix_grad = contract(self_out_all, first_grad_low, 0, 1).astype(BF16)
    self_mix_grad = exchange(self_mix_grad.reshape(all_heads, HEAD, part)).reshape(chunk_shape)
    stacked, head_grad, head_sum = self_backward(
        x_all, self_query, self_pair, self_mixed, self_mix_grad, self_lse
    )
    stacked = exchange(stacked.reshape(all_heads, 3 * HEAD, part)).reshape(all_heads, 3, HEAD, part)
    stacked = stacked.swapaxes(0, 1).reshape(3, width, part)
    input_grad = first_grad + (
        contract(stacked[0], proj_q, 0, 1)
        + contract(stacked[1], proj_k, 0, 1)
        + contract(stacked[2], proj_v, 0, 1)
    )
    input_grad = lax.all_gather(input_grad.astype(BF16), "tp", axis=0, tiled=True).astype(F32)

    head_grad = head_grad.astype(BF16).reshape(3 * HEAD, plane, shard).swapaxes(0, 1)
    head_grad = lax.all_to_all(head_grad, PLANE, split_axis=0, concat_axis=0, tiled=True)
    head_grad = jnp.sum(head_grad.reshape(-1, blocks, 3, HEAD, shard).astype(F32), 0)
    self_proj_out = head_grad.transpose(1, 3, 0, 2).reshape(3, shard, local_width)

    norm_sums = jnp.stack(
        [gain_zero, gain_one, gain_two, shift_zero, shift_one, shift_two]
        + [attn_bias_sum, cross_bias_sum, mlp_bias_grad]
    )
    norm_sums = norm_sums.reshape(9, plane, 1, shard).transpose(1, 2, 0, 3).reshape(plane, 1, 9 * shard)
    norm_sums = jnp.broadcast_to(norm_sums, (plane, ranks, 9 * shard))
    up_cols = up_bias.shape[1]
    up_sums = up_bias_grad.reshape(2, -1, plane, up_cols).transpose(2, 0, 1, 3).reshape(plane, 2, -1)
    rank_ids = jnp.arange(ranks).reshape(1, ranks, 1)
    up_sums = jnp.where(rank_ids == own_tp, up_sums[:, :1], 0.0) + jnp.where(
        rank_ids == own_tp ^ 2, up_sums[:, 1:], 0.0
    )

    def bias_pieces(values):
        values = values.reshape(ranks, heads_here, plane, bias_part)
        return values.transpose(2, 0, 1, 3).reshape(plane, ranks, count)

    own_heads = (jnp.arange(all_heads) // heads_here == own_tp).reshape(all_heads, 1)
    value_full = jnp.where(own_heads, jnp.tile(value_sum, (ranks, 1)), 0.0)
    cross_sums = bias_pieces(jnp.concatenate([query_sum, value_full], 1))
    head_sum = head_sum.reshape(3, HEAD)
    own_head_id = (jnp.arange(all_heads) == own_tp * blocks + own_ctx).reshape(all_heads, 1)
    self_sums = bias_pieces(
        jnp.where(own_head_id, jnp.concatenate([head_sum[0], head_sum[2]]), 0.0)
    )
    sums = jnp.concatenate([norm_sums, up_sums, cross_sums, self_sums], 2)
    sums = lax.all_to_all(
        sums.reshape(plane * ranks, -1), ("dp", "ctx", "tp"), split_axis=0, concat_axis=0, tiled=True
    )
    sums = jnp.sum(sums, 0)
    norm_out = sums[: 9 * shard].reshape(9, shard)
    up_size = hidden // plane
    at = 9 * shard + up_size
    return (
        hidden_out.reshape(seqs, block, width),
        input_grad.reshape(seqs, block, width),
        encoder_grad,
        self_proj_out,
        sums[at + count :].reshape(heads_here, bias_part),
        self_out_out,
        cross_q_out,
        kv_grad,
        sums[at : at + count].reshape(heads_here, bias_part),
        cross_out_out,
        up_out,
        sums[9 * shard : at].reshape(up_bias.shape),
        down_out,
        norm_out[:3],
        norm_out[3:6],
        norm_out[6:],
        rms.reshape(4, seqs, block),
    )


def solution(mesh):
    rows, heads, columns = P("dp", "ctx", None), P("tp", PLANE), P(PLANE, "tp")
    stacked, vectors = P(None, PLANE, "tp"), P(None, PLANE)
    weights = (
        stacked, heads, heads, columns, stacked, heads, heads, columns, heads, heads,
        vectors, vectors, vectors,
    )
    return jax.shard_map(
        body,
        mesh=mesh,
        in_specs=(rows, rows, rows) + weights,
        out_specs=(rows, rows, P("dp", "ctx", "tp")) + weights + (P(None, "dp", "ctx"),),
        check_vma=False,
    )
```

time: 1360 us -> 777 us (0.57)
  waiting for transfers between devices: 873 us -> 380 us
  matrix products: 181 us -> 65.7 us
  Pallas kernels: 0 us -> 52.8 us
  other arithmetic: 89 us -> 40.2 us
  starting transfers between devices: 2.38 us -> 49.7 us
  local copies, waits for them, and re-layouts: 93.2 us -> 55.2 us
    unnamed x37 -> x14, waiting for transfers between devices: 329 us -> 33.1 us
    psum x6 -> x0, waiting for transfers between devices: 247 us -> none  [head_total(): return lax.psum(values.astype(jnp.bfloat16), 'tp').astype(jnp.float32)]
    ppermute x0 -> x12, waiting for transfers between devices: none -> 97.6 us  [the longest x6 50.3 us: ctx_swap(): return lax.ppermute(values, 'ctx', [(i, i ^ k) for i in slots])]
    dot_general x31 -> x21, matrix products: 159 us -> 65.7 us  [contract(): lax.dot_general(left, right, (((left_dim,), (right_dim,)), ((), ())), pre...]
    all_gather x6 -> x7, waiting for transfers between devices: 130 us -> 65.5 us  [the longest x1 37.4 us: body(): square = lax.all_gather(square, 'tp', axis=2, tiled=True)]
    pallas_call x0 -> x4, Pallas kernels: none -> 52.8 us  [call(): pl.pallas_call(kernel, grid=(seqs,), in_specs=in_specs, out_specs=out_spe...]
    convert_element_type x20 -> x7, other arithmetic: 42.4 us -> 3.86 us  [the longest x1 2.71 us: body(): encoder_grad = lax.psum_scatter(enc_part.reshape(seqs, enc_len, width), '...]
    all_to_all x0 -> x9, starting transfers between devices: none -> 36.5 us  [the longest x6 26.1 us: exchange(): lax.all_to_all(values, HEADS, split_axis=0, concat_axis=0, tiled=True)]
  transfers between devices with their start and end apart: 27 -> 33, of which waited for: 24 -> 21; matrix products, arithmetic and copies ran while one was open for 14% -> 13% of each run, Pallas kernels for 0% -> 4%
where the time goes in v1:
time: 777 us; the launch traced here: 767 us
  waiting for transfers between devices  380 us (49%)
  blocking collectives  107 us (14%)
  matrix products  65.7 us (8%)
  local copies, waits for them, and re-layouts  55.2 us (7%)
  Pallas kernels  52.8 us (7%)
  starting transfers between devices  49.7 us (6%)
  other arithmetic  40.2 us (5%)
  between operations  15.8 us (2%)
    reduce_scatter x1, waiting for transfers between devices, body(): lax.psum_scatter(enc_part.reshape(seqs, enc_len, width), 'tp', scatter_di...  75.8 us
    all_gather x1, blocking collectives, body(): small = lax.all_gather(small, ('dp', 'ctx', 'tp')).reshape(plane, ranks, -1)  69.6 us
    dot_general x21, matrix products, contract(): lax.dot_general(left, right, (((left_dim,), (right_dim,)), ((), ())), pre...  65.7 us
    reduce_scatter x1, waiting for transfers between devices, body(): lax.psum_scatter(mlp_grad, PLANE, scatter_dimension=0, tiled=True)  53 us
    pallas_call x4, Pallas kernels, call(): pl.pallas_call(kernel, grid=(seqs,), in_specs=in_specs, out_specs=out_spe...  52.8 us
    ppermute x6, waiting for transfers between devices, ctx_swap(): return lax.ppermute(values, 'ctx', [(i, i ^ k) for i in slots])  50.3 us
    ppermute x6, waiting for transfers between devices, tp_swap(): return lax.ppermute(values, 'tp', [(i, i ^ k) for i in range(ranks)])  47.3 us
    all_gather x1, waiting for transfers between devices, body(): square = lax.all_gather(square, 'tp', axis=2, tiled=True)  37.4 us
  transfers between devices with their start and end apart: 33, of which 21 were waited for; matrix products, arithmetic and copies ran while one was open for 13% of the time, Pallas kernels for 4%

profile of v1, /device:TPU:0, one launch (start us, length us, event | category | flops | bytes accessed | tf_op | source)
XLA Modules:
  0.0 766.9 jit_solution(2717977269528910716)
XLA Ops:
  13.6 37.4 %all-gather.13.cloned.1.call-done = bf16[6,128,1024]{1,2,0:T(8,128)(2,1)} async-done(((bf16[6,128,256]{1,2,0:T(8,128)(2,1)}), bf16[6,128,1024]{1,2,0:T(8,128)(2,1)}) %all-gather.13.cloned.1.call-update) | async-done | bytes 1572880 | tf_op jit(solution)/shard_map/all_gather | solution.py:383
  52.6 24.2 %collective-permute-done.4 = bf16[128,2048]{0,1:T(8,128)(2,1)S(1)} collective-permute-done((bf16[128,2048]{0,1:T(8,128)(2,1)S(1)}, bf16[128,2048]{0,1:T(8,128)(2,1)S(1)}, u32[]{:S(2)}, u32[]{:S(2)}) %collective-permute-start.4) | collective-permute-done | bytes 524320 | tf_op jit(solution)/shard_map/ppermute | solution.py:326
  82.6 69.6 %all-gather.2 = bf16[32,1,1408]{2,1,0:T(2,128)(2,1)S(1)} all-gather(bf16[1,1,1408]{2,1,0:T(2,128)(2,1)S(1)} %reshape.623), channel_id=3, replica_groups=mesh['dp'=2,'ctx'=4,'tp'=4] {'dp','ctx','tp'}, dimensions={0}, use_global_device_ids=true | all-gather | bytes 92928 | tf_op jit(solution)/shard_map/all_gather | solution.py:341
  153.9 10.6 %all-gather = bf16[8,192,128]{2,1,0:T(8,128)(2,1)S(1)} all-gather(bf16[4,192,128]{2,1,0:T(8,128)(2,1)S(1)} %all-to-all-done), channel_id=2, replica_groups=mesh['dp'=2,'ctx'=4,'tp'=4] {'dp'}, dimensions={0}, use_global_device_ids=true | all-gather | bytes 589824 | tf_op jit(solution)/shard_map/all_gather | solution.py:373
  168.4 4.9 fusion.8
  173.4 9.5 %shard_map.287 = (bf16[2,64,1024]{2,1,0:T(8,128)(2,1)S(1)}, bf16[2,1024,128]{2,1,0:T(8,128)(2,1)S(1)}, bf16[4,4,64,128]{3,2,1,0:T(8,128)(2,1)}, f32[2,1,1024]{2,1,0:T(1,128)S(1)}) custom-call(bf16[2,1024,1024]{2,1,0:T(8,128)(2,1)} %all-gather.11.cloned.1.call-done.x_ref, bf16[192,1024]{1,0:T(8,128)(2,1)S(1)} %reshape.548.w_ref, f32[64,1]{1,0:T(8,128)S(1)} %copy.212.bq_ref, ...), custom_call_target="tpu_custom_call" | custom-call | flops 1879048192 | bytes 5645056 | tf_op jit(solution)/shard_map/pallas_call | solution.py:206
  214.7 17.8 %collective-permute-done.2.refs_3_ = bf16[2,1024,128]{2,1,0:T(8,128)(2,1)S(1)} collective-permute-done((bf16[2,1024,128]{2,1,0:T(8,128)(2,1)}, bf16[2,1024,128]{2,1,0:T(8,128)(2,1)S(1)}, u32[]{:S(2)}, u32[]{:S(2)}) %collective-permute-start.2) | collective-permute-done | bytes 524320 | tf_op jit(solution)/shard_map/ppermute | solution.py:323
  233.5 13.6 %shard_map.288 = (bf16[4,4,64,128]{3,2,1,0:T(8,128)(2,1)}, f32[2,1,1024]{2,1,0:T(1,128)S(1)}) custom-call(bf16[4,4,64,128]{3,2,1,0:T(8,128)(2,1)S(1)} %bitcast.245, bf16[2,1024,128]{2,1,0:T(8,128)(2,1)S(1)} %bitcast.243, bf16[2,1024,128]{2,1,0:T(8,128)(2,1)S(1)} %collective-permute-done.refs_1_, bf16[2,1024,128]{2,1,0:T(8,128)(2,1)S(1)} %collective-permute-done.1.refs_2_, ...), custom_call_target="tpu_custom_call" | custom-call | flops 4294967296 | bytes 2629632 | tf_op jit(solution)/shard_map/pallas_call | solution.py:206
  247.1 5.4 all-to-all-start.3
  252.5 10.0 %all-to-all-done.3 = bf16[16,64,128]{2,1,0:T(8,128)(2,1)S(1)} async-done(((bf16[16,64,128]{2,1,0:T(8,128)(2,1)}), bf16[16,64,128]{2,1,0:T(8,128)(2,1)S(1)}, u32[]{:S(2)}, u32[]{:S(2)}) %all-to-all-start.3) | async-done | bytes 262176 | tf_op jit(solution)/shard_map/all_to_all | solution.py:329
  267.3 6.7 collective-permute-done.3
  273.9 7.6 multiply_convert_fusion
  283.9 6.3 collective-permute-done.5
  294.3 5.5 collective-permute-done.6
  313.3 13.5 %all_to_all.54 = bf16[16,64,128]{2,1,0:T(8,128)(2,1)S(1)} all-to-all(bf16[16,64,128]{2,1,0:T(8,128)(2,1)S(1)} %bitcast.291), channel_id=1, replica_groups=mesh['dp'=2,'ctx'=4,'tp'=4] {'tp','ctx'}, dimensions={0} | all-to-all | bytes 524288 | tf_op jit(solution)/shard_map/all_to_all | solution.py:329
  326.9 22.0 %shard_map.289 = (bf16[2,1024,128]{2,1,0:T(8,128)(2,1)S(1)}, bf16[2,1024,128]{2,1,0:T(8,128)(2,1)S(1)}, bf16[2,1024,128]{2,1,0:T(8,128)(2,1)S(1)}, bf16[2,1024,1...) custom-call(bf16[4,4,64,128]{3,2,1,0:T(8,128)(2,1)S(1)} %bitcast.246, bf16[4,4,64,128]{3,2,1,0:T(8,128)(2,1)} %get-tuple-element.32.o_ref, ...), custom_call_target="tpu_custom_call" | custom-call | flops 10737418240 | bytes 5251072 | tf_op jit(solution)/shard_map/pallas_call | solution.py:206
  355.9 6.6 all-to-all-done.5
  368.7 13.4 %pad_maximum_fusion.1 = bf16[1024,3072]{0,1:T(8,128)(2,1)} fusion(bf16[1024,1024]{0,1:T(8,128)(2,1)S(1)} %copy-done.7, bf16[1024,1024]{0,1:T(8,128)(2,1)S(1)} %convolution_convert_fusion.4, bf16[1024,1024]{0,1:T(8,128)(2,1)S(1)} %convolution_convert_fusion.5), kind=kLoop, calls=%fused_computation.1 | loop fusion | flops 18874368 | bytes 12582912 | tf_op jit(solution)/shard_map/concatenate | solution.py:497
  382.1 8.7 %copy.248 = bf16[1024,3072]{1,0:T(8,128)(2,1)} copy(bf16[1024,3072]{0,1:T(8,128)(2,1)} %pad_maximum_fusion.1) | data formatting | bytes 12582912
  399.8 8.7 %pad_maximum_fusion = bf16[1024,4096]{1,0:T(8,128)(2,1)} fusion(bf16[1024,2048]{1,0:T(8,128)(2,1)} %convolution_convert_fusion, bf16[1024,2048]{1,0:T(8,128)(2,1)} %convolution_convert_fusion.1), kind=kLoop, calls=%fused_computation | loop fusion | flops 16777216 | bytes 16777216 | tf_op jit(solution)/shard_map/concatenate | solution.py:458
  418.6 7.9 %all-to-all-done.6 = bf16[16,64,128]{2,1,0:T(8,128)(2,1)S(1)} async-done(((bf16[16,64,128]{2,1,0:T(8,128)(2,1)}), bf16[16,64,128]{2,1,0:T(8,128)(2,1)S(1)}, u32[]{:S(2)}, u32[]{:S(2)}) %all-to-all-start.6) | async-done | bytes 262176 | tf_op jit(solution)/shard_map/all_to_all | solution.py:329
  427.5 7.7 %shard_map.290 = (bf16[4,4,192,128]{3,2,1,0:T(8,128)(2,1)}, f32[192,1024]{1,0:T(8,128)S(1)}, f32[192,1]{1,0:T(8,128)S(1)}) custom-call(bf16[2,1024,1024]{2,1,0:T(8,128)(2,1)} %all-gather.11.cloned.1.call-done.x_ref, bf16[2,64,1024]{2,1,0:T(8,128)(2,1)S(1)} %get-tuple-element.35.q_ref, bf16[2,1024,128]{2,1,0:T(8,128)(2,1)S(1)} %copy-done.4, ...), custom_call_target="tpu_custom_call" | custom-call | flops 3489660928 | bytes 7086848 | tf_op jit(solution)/shard_map/pallas_call | solution.py:206
  439.6 7.4 collective-permute-done.10
  447.0 20.5 %collective-permute-done.9 = bf16[2,1024,128]{2,1,0:T(8,128)(2,1)} collective-permute-done((bf16[2,1024,128]{2,1,0:T(8,128)(2,1)S(1)}, bf16[2,1024,128]{2,1,0:T(8,128)(2,1)}, u32[]{:S(2)}, u32[]{:S(2)}) %collective-permute-start.9) | collective-permute-done | bytes 524320 | tf_op jit(solution)/shard_map/ppermute | solution.py:323
  467.5 5.1 convolution_convert_fusion.6
  482.6 5.8 convolution_convert_fusion.2
  509.8 13.5 %all_gather.47 = f32[3,512]{1,0:T(4,128)S(1)} all-gather(f32[3,128]{1,0:T(4,128)S(1)} %pad_maximum_fusion.22), channel_id=1, replica_groups=mesh['dp'=2,'ctx'=4,'tp'=4] {'tp'}, dimensions={1}, use_global_device_ids=true | all-gather | bytes 7680 | tf_op jit(solution)/shard_map/all_gather | solution.py:445
  525.9 53.0 %reduce-scatter.14.cloned.1.call-done = bf16[128,4096]{1,0:T(8,128)(2,1)} async-done(((bf16[1024,4096]{1,0:T(8,128)(2,1)}), bf16[128,4096]{1,0:T(8,128)(2,1)}) %reduce-scatter.14.cloned.1.call-update) | async-done | bytes 1048592 | tf_op jit(solution)/shard_map/reduce_scatter | solution.py:461
  587.2 31.5 %reduce-scatter.18.cloned.1.call-done = bf16[128,512]{1,0:T(8,128)(2,1)} async-done(((bf16[1024,512]{1,0:T(8,128)(2,1)}), bf16[128,512]{1,0:T(8,128)(2,1)}) %reduce-scatter.18.cloned.1.call-update) | async-done | bytes 131088
  620.7 28.0 %all-gather.23.cloned.1.call-done = bf16[512,1024]{1,0:T(8,128)(2,1)} async-done(((bf16[128,1024]{1,0:T(8,128)(2,1)}), bf16[512,1024]{1,0:T(8,128)(2,1)}) %all-gather.23.cloned.1.call-update) | async-done | bytes 1048592 | tf_op jit(solution)/shard_map/all_gather | solution.py:519
  651.5 75.8 %reduce-scatter.10.cloned.1.call-done = bf16[2,1024,256]{2,1,0:T(8,128)(2,1)} async-done(((bf16[2,1024,1024]{2,1,0:T(8,128)(2,1)}), bf16[2,1024,256]{2,1,0:T(8,128)(2,1)}) %reduce-scatter.10.cloned.1.call-update) | async-done | bytes 1048592 | tf_op jit(solution)/shard_map/reduce_scatter | solution.py:479
  730.0 23.4 %reduce-scatter.12.cloned.1.call-done = bf16[128,3,256]{0,2,1:T(8,128)(2,1)} async-done(((bf16[128,3,1024]{0,2,1:T(8,128)(2,1)}), bf16[128,3,256]{0,2,1:T(8,128)(2,1)}) %reduce-scatter.12.cloned.1.call-update) | async-done | bytes 196624 | tf_op jit(solution)/shard_map/reduce_scatter | solution.py:499
  (354 shorter events, 169.4 us)
Async XLA Ops:
  7.2 43.8 %all-gather.13.cloned.1.call-start = ((), (), s32[]{:S(2)}) async-start(), calls=%async_computation.16 | async-start | bytes 1966080 | tf_op jit(solution)/shard_map/all_gather | solution.py:383
  11.0 154.0 %all-gather.17.cloned.1.call-start = ((), (), s32[]{:S(2)}) async-start(), calls=%async_computation.18 | async-start | bytes 1179648 | tf_op jit(solution)/shard_map/all_gather | solution.py:377
  12.8 160.6 %all-gather.11.cloned.1.call-start = ((), (), s32[]{:S(2)}) async-start(), calls=%async_computation.15 | async-start | bytes 5242880 | tf_op jit(solution)/shard_map/all_gather | solution.py:337
  13.6 184.4 %all-gather.15.cloned.1.call-start = ((), (), s32[]{:S(2)}) async-start(), calls=%async_computation.17 | async-start | bytes 14155776 | tf_op jit(solution)/shard_map/all_gather | solution.py:385
  51.0 216.2 %all-gather.19.cloned.1.call-start = ((), (), s32[]{:S(2)}) async-start(), calls=%async_computation.19 | async-start | bytes 9437184 | tf_op jit(solution)/shard_map/all_gather | solution.py:394
  51.3 25.5 %collective-permute-start.4 = (bf16[128,2048]{0,1:T(8,128)(2,1)S(1)}, bf16[128,2048]{0,1:T(8,128)(2,1)S(1)}, u32[]{:S(2)}, u32[]{:S(2)}) collective-permute-start(bf16[128,2048]{0,1:T(8,128)(2,1)S(1)} %pad_maximum_fusion.7), channel_id=1, source_target_pairs={{0,2},{1,3},{2,0},{3,1},{4,6},{5,7},{6,4},{7,5},{8,10},{9,11},{10,... | collective-permute-start | bytes 1572872 | tf_op jit(solution)/shard_map/ppermute | solution.py:326
  78.7 75.1 %all-to-all-start = ((bf16[4,192,128]{2,1,0:T(8,128)(2,1)}), bf16[4,192,128]{2,1,0:T(8,128)(2,1)S(1)}, u32[]{:S(2)}, u32[]{:S(2)}) async-start(bf16[4,192,128]{2,1,0:T(8,128)(2,1)} %bitcast.3), calls=%async_computation | async-start | bytes 393216 | tf_op jit(solution)/shard_map/all_to_all | solution.py:372
  183.7 14.3 %all-to-all-start.1 = ((bf16[16,64,128]{2,1,0:T(8,128)(2,1)}), bf16[16,64,128]{2,1,0:T(8,128)(2,1)}, u32[]{:S(2)}, u32[]{:S(2)}) async-start(bf16[16,64,128]{2,1,0:T(8,128)(2,1)} %bitcast.13), calls=%async_computation.1 | async-start | bytes 524288 | tf_op jit(solution)/shard_map/all_to_all | solution.py:329
  191.3 18.8 %collective-permute-start = (bf16[2,1024,128]{2,1,0:T(8,128)(2,1)}, bf16[2,1024,128]{2,1,0:T(8,128)(2,1)S(1)}, u32[]{:S(2)}, u32[]{:S(2)}) collective-permute-start(bf16[2,1024,128]{2,1,0:T(8,128)(2,1)} %bitcast.46), channel_id=1, source_target_pairs={{0,4},{4,0},{8,12},{12,8},{1,5},{5,1},{9,13},{13,9},{2,6},{6,2},{1... | collective-permute-start | bytes 1572872 | tf_op jit(solution)/shard_map/ppermute | solution.py:323
  193.5 21.2 %collective-permute-start.1 = (bf16[2,1024,128]{2,1,0:T(8,128)(2,1)}, bf16[2,1024,128]{2,1,0:T(8,128)(2,1)S(1)}, u32[]{:S(2)}, u32[]{:S(2)}) collective-permute-start(bf16[2,1024,128]{2,1,0:T(8,128)(2,1)} %bitcast.47), channel_id=1, source_target_pairs={{0,8},{4,12},{8,0},{12,4},{1,9},{5,13},{9,1},{13,5},{2,10},{6,14},... | collective-permute-start | bytes 1572872 | tf_op jit(solution)/shard_map/ppermute | solution.py:323
  196.1 36.4 %collective-permute-start.2 = (bf16[2,1024,128]{2,1,0:T(8,128)(2,1)}, bf16[2,1024,128]{2,1,0:T(8,128)(2,1)S(1)}, u32[]{:S(2)}, u32[]{:S(2)}) collective-permute-start(bf16[2,1024,128]{2,1,0:T(8,128)(2,1)} %bitcast.48), channel_id=1, source_target_pairs={{0,12},{4,8},{8,4},{12,0},{1,13},{5,9},{9,5},{13,1},{2,14},{6,10},... | collective-permute-start | bytes 1572872 | tf_op jit(solution)/shard_map/ppermute | solution.py:323
  204.2 29.3 %all-to-all-start.2 = ((bf16[16,64,128]{2,1,0:T(8,128)(2,1)}), bf16[16,64,128]{2,1,0:T(8,128)(2,1)S(1)}, u32[]{:S(2)}, u32[]{:S(2)}) async-start(bf16[16,64,128]{2,1,0:T(8,128)(2,1)} %bitcast.29), calls=%async_computation.2 | async-start | bytes 524288 | tf_op jit(solution)/shard_map/all_to_all | solution.py:329
  247.1 15.5 %all-to-all-start.3 = ((bf16[16,64,128]{2,1,0:T(8,128)(2,1)}), bf16[16,64,128]{2,1,0:T(8,128)(2,1)S(1)}, u32[]{:S(2)}, u32[]{:S(2)}) async-start(bf16[16,64,128]{2,1,0:T(8,128)(2,1)} %bitcast.49), calls=%async_computation.3 | async-start | bytes 524288 | tf_op jit(solution)/shard_map/all_to_all | solution.py:329
  265.8 8.1 %collective-permute-start.3 = (bf16[128,1024]{1,0:T(8,128)(2,1)S(1)}, bf16[128,1024]{1,0:T(8,128)(2,1)S(1)}, u32[]{:S(2)}, u32[]{:S(2)}) collective-permute-start(bf16[128,1024]{1,0:T(8,128)(2,1)S(1)} %add_convert_fusion.3), channel_id=1, source_target_pairs={{0,1},{1,0},{2,3},{3,2},{4,5},{5,4},{6,7},{7,6},{8,9},{9,8},{10,11... | collective-permute-start | bytes 786440 | tf_op jit(solution)/shard_map/ppermute | solution.py:326
  282.9 7.3 collective-permute-start.5
  292.5 7.3 collective-permute-start.6
  348.9 13.7 %all-to-all-start.5 = ((bf16[16,64,128]{2,1,0:T(8,128)(2,1)}), bf16[16,64,128]{2,1,0:T(8,128)(2,1)S(1)}, u32[]{:S(2)}, u32[]{:S(2)}) async-start(bf16[16,64,128]{2,1,0:T(8,128)(2,1)} %bitcast.66), calls=%async_computation.5 | async-start | bytes 524288 | tf_op jit(solution)/shard_map/all_to_all | solution.py:329
  352.5 145.7 %reduce-scatter.16.cloned.1.call-start = ((), (), s32[]{:S(2)}) async-start(), calls=%async_computation.25 | async-start | bytes 7077888
  390.9 133.0 %all-gather.21.cloned.1.call-start = ((), (), s32[]{:S(2)}) async-start(), calls=%async_computation.20 | async-start | bytes 1310720 | tf_op jit(solution)/shard_map/all_gather | solution.py:443
  391.6 187.3 %reduce-scatter.14.cloned.1.call-start = ((), (), s32[]{:S(2)}) async-start(), calls=%async_computation.24 | async-start | bytes 9437184 | tf_op jit(solution)/shard_map/reduce_scatter | solution.py:461
  412.5 14.0 %all-to-all-start.6 = ((bf16[16,64,128]{2,1,0:T(8,128)(2,1)}), bf16[16,64,128]{2,1,0:T(8,128)(2,1)S(1)}, u32[]{:S(2)}, u32[]{:S(2)}) async-start(bf16[16,64,128]{2,1,0:T(8,128)(2,1)} %bitcast.68), calls=%async_computation.6 | async-start | bytes 524288 | tf_op jit(solution)/shard_map/all_to_all | solution.py:329
  416.5 30.5 %collective-permute-start.10 = (bf16[2,1024,128]{2,1,0:T(8,128)(2,1)S(1)}, bf16[2,1024,128]{2,1,0:T(8,128)(2,1)}, u32[]{:S(2)}, u32[]{:S(2)}) collective-permute-start(bf16[2,1024,128]{2,1,0:T(8,128)(2,1)S(1)} %get-tuple-element.42), channel_id=1, source_target_pairs={{0,12},{4,8},{8,4},{12,0},{1,13},{5,9},{9,5},{13,1},{2,14},{6,10},... | collective-permute-start | bytes 1572872 | tf_op jit(solution)/shard_map/ppermute | solution.py:323
  418.2 49.3 %collective-permute-start.9 = (bf16[2,1024,128]{2,1,0:T(8,128)(2,1)S(1)}, bf16[2,1024,128]{2,1,0:T(8,128)(2,1)}, u32[]{:S(2)}, u32[]{:S(2)}) collective-permute-start(bf16[2,1024,128]{2,1,0:T(8,128)(2,1)S(1)} %get-tuple-element.41), channel_id=1, source_target_pairs={{0,8},{4,12},{8,0},{12,4},{1,9},{5,13},{9,1},{13,5},{2,10},{6,14},... | collective-permute-start | bytes 1572872 | tf_op jit(solution)/shard_map/ppermute | solution.py:323
  418.6 48.9 %collective-permute-start.8 = (bf16[2,1024,128]{2,1,0:T(8,128)(2,1)S(1)}, bf16[2,1024,128]{2,1,0:T(8,128)(2,1)}, u32[]{:S(2)}, u32[]{:S(2)}) collective-permute-start(bf16[2,1024,128]{2,1,0:T(8,128)(2,1)S(1)} %get-tuple-element.40), channel_id=1, source_target_pairs={{0,4},{4,0},{8,12},{12,8},{1,5},{5,1},{9,13},{13,9},{2,6},{6,2},{1... | collective-permute-start | bytes 1572872 | tf_op jit(solution)/shard_map/ppermute | solution.py:323
  435.2 38.9 %all-to-all-start.7 = ((bf16[16,192,128]{2,1,0:T(8,128)(2,1)}), bf16[16,192,128]{2,1,0:T(8,128)(2,1)}, u32[]{:S(2)}, u32[]{:S(2)}) async-start(bf16[16,192,128]{2,1,0:T(8,128)(2,1)} %bitcast.70), calls=%async_computation.7 | async-start | bytes 1572864 | tf_op jit(solution)/shard_map/all_to_all | solution.py:329
  439.5 179.2 %reduce-scatter.18.cloned.1.call-start = ((), (), s32[]{:S(2)}) async-start(), calls=%async_computation.26 | async-start | bytes 1179648
  474.1 174.5 %all-gather.23.cloned.1.call-start = ((), (), s32[]{:S(2)}) async-start(), calls=%async_computation.21 | async-start | bytes 1310720 | tf_op jit(solution)/shard_map/all_gather | solution.py:519
  482.5 244.7 %reduce-scatter.10.cloned.1.call-start = ((), (), s32[]{:S(2)}) async-start(), calls=%async_computation.22 | async-start | bytes 5242880 | tf_op jit(solution)/shard_map/reduce_scatter | solution.py:479
  494.5 11.7 %all-to-all-start.8 = ((bf16[8,192,128]{2,1,0:T(8,128)(2,1)}), bf16[8,192,128]{2,1,0:T(8,128)(2,1)S(1)}, u32[]{:S(2)}, u32[]{:S(2)}) async-start(bf16[8,192,128]{2,1,0:T(8,128)(2,1)} %bitcast_bitcast_fusion), calls=%async_computation.9 | async-start | bytes 786432 | tf_op jit(solution)/shard_map/all_to_all | solution.py:522
  497.9 255.5 %reduce-scatter.12.cloned.1.call-start = ((), (), s32[]{:S(2)}) async-start(), calls=%async_computation.23 | async-start | bytes 983040 | tf_op jit(solution)/shard_map/reduce_scatter | solution.py:499
  506.2 19.0 %all-to-all-start.9 = ((f32[32,1,1408]{2,1,0:T(1,128)}), f32[32,1,1408]{2,1,0:T(1,128)S(1)}, u32[]{:S(2)}, u32[]{:S(2)}) async-start(f32[32,1,1408]{2,1,0:T(1,128)} %all_to_all.42), calls=%async_computation.10 | async-start | bytes 360448 | tf_op jit(solution)/shard_map/all_to_all | solution.py:552
  582.6 174.1 %collective-permute-start.11 = (bf16[128,2,1024]{2,0,1:T(8,128)(2,1)S(1)}, bf16[128,2,1024]{2,0,1:T(8,128)(2,1)S(1)}, u32[]{:S(2)}, u32[]{:S(2)}) collective-permute-start(bf16[128,2,1024]{2,0,1:T(8,128)(2,1)S(1)} %bitcast.275), channel_id=1, source_target_pairs={{0,2},{1,3},{2,0},{3,1},{4,6},{5,7},{6,4},{7,5},{8,10},{9,11},{10,... | collective-permute-start | bytes 1572872 | tf_op jit(solution)/shard_map/ppermute | solution.py:326
  (54 other events, 759.0 us)
Sparse Core Ops, SparseCore 0:
  11.2 39.7 all-gather.12
  53.4 22.4 all-gather.16
  77.5 34.8 all-gather.10
  114.1 79.7 all-gather.14
  196.2 66.9 all-gather.18
  391.0 83.6 reduce-scatter.15
  476.3 27.9 all-gather.20
  508.1 70.7 reduce-scatter.13
  582.7 36.0 reduce-scatter.17
  620.7 27.8 all-gather.22
  651.0 76.2 reduce-scatter.9
  729.5 23.8 reduce-scatter.11

commit v2 on v1

v2 whole, which is shorter than its diff:
```python
import functools

import jax
import jax.numpy as jnp
from jax import lax
from jax.experimental import pallas as pl
from jax.experimental.pallas import tpu as pltpu
from jax.sharding import PartitionSpec as P

EPSILON = 1e-05
HEAD = 64
KEY_TILE = 512
ROW_TILE = 512
COST_SHARE = 10
VMEM_BYTES = 50 * 1024 * 1024
PLANE = ("dp", "ctx")
HEADS = ("tp", "ctx")
F32 = jnp.float32
BF16 = jnp.bfloat16
IN_SMEM = pl.BlockSpec(memory_space=pltpu.SMEM)


def contract(left, right, left_dim, right_dim):
    return lax.dot_general(
        left, right, (((left_dim,), (right_dim,)), ((), ())), preferred_element_type=F32
    )


def together(*values):
    return lax.optimization_barrier(values)


def norm_forward(values, norm_gain, norm_shift):
    row_mean = jnp.mean(values, -1, keepdims=True)
    centered = values - row_mean
    inv_std = lax.rsqrt(jnp.mean(centered * centered, -1, keepdims=True) + EPSILON)
    normed = centered * inv_std
    return (normed * norm_gain + norm_shift, normed, inv_std)


def norm_backward(gradient, normed, inv_std, norm_gain):
    gain_grad = jnp.sum(gradient * normed, 0)
    shift_grad = jnp.sum(gradient, 0)
    scaled = gradient * norm_gain
    input_part = inv_std * (
        scaled
        - jnp.mean(scaled, -1, keepdims=True)
        - normed * jnp.mean(scaled * normed, -1, keepdims=True)
    )
    return (input_part, gain_grad, shift_grad)


def root_mean(values):
    return jnp.sqrt(jnp.mean(values * values, -1))


def exact_gelu(values):
    return jax.nn.gelu(values, approximate=False)


def with_zeros_below(values):
    return jnp.concatenate([values, jnp.zeros_like(values)], 0)


def with_zeros_above(values):
    return jnp.concatenate([jnp.zeros_like(values), values], 0)


def gather_chunks(ref):
    halves, blocks = ref.shape[:2]
    return jnp.concatenate([ref[h, b] for h in range(halves) for b in range(blocks)], 1)


def slot_at(own, k, size):
    return pl.ds(pl.multiple_of((own ^ k) * size, size), size)


def first_pack_kernel(proj_ref, small_ref, out_ref):
    blocks = proj_ref.shape[2] // HEAD
    for j in range(3):
        turned = proj_ref[j].T
        for e in range(out_ref.shape[0]):
            head = e % blocks * HEAD
            out_ref[e, j * HEAD : (j + 1) * HEAD] = turned[head : head + HEAD]
    for e in range(out_ref.shape[0]):
        out_ref[e, 3 * HEAD :] = small_ref[...]


def square_pack_kernel(self_out_ref, cross_q_ref, cross_out_ref, out_ref):
    out_ref[0] = self_out_ref[...].T
    out_ref[1] = cross_q_ref[...]
    out_ref[2] = cross_out_ref[...].T


def mlp_pack_kernel(up_ref, down_ref, out_ref):
    width = up_ref.shape[1]
    out_ref[:, :width] = up_ref[...]
    out_ref[:, width:] = down_ref[...].T


def rank_kernel(at_ref, *refs):
    part_refs, out_ref = refs[:-1], refs[-1]
    for k, part_ref in enumerate(part_refs):
        count, _, columns = part_ref.shape
        for i in range(count):
            first = (i * len(part_refs) + (at_ref[0] ^ k)) * columns
            out_ref[:, pl.ds(pl.multiple_of(first, columns), columns)] = part_ref[i]


def self_forward_kernel(at_ref, *refs):
    x_refs, (w_ref, bq_ref, bv_ref, q_ref, kv_ref, o_ref, lse_ref) = refs[:-7], refs[-7:]
    weights = w_ref[...]
    halves, blocks, _, part = o_ref.shape
    block = halves * part
    scale = HEAD**-0.5
    for k, x_ref in enumerate(x_refs):
        here = slot_at(at_ref[0], k, block)
        tokens = x_ref[0]
        q_ref[0, :, here] = (contract(weights[:HEAD], tokens, 1, 1) + bq_ref[...]).astype(BF16) * scale
        kv_ref[0, here] = (contract(tokens, weights[HEAD:], 1, 1) + bv_ref[...]).astype(BF16)
    for i in range(blocks):
        keys = kv_ref[0, : (i + 1) * block]
        query = q_ref[0, :, i * block : (i + 1) * block]
        scores = contract(keys, with_zeros_below(query), 1, 0)
        top = jnp.max(scores, 0, keepdims=True)
        weight = jnp.exp(scores - top)
        total = jnp.sum(weight, 0, keepdims=True)
        mixed = contract(keys, weight.astype(BF16), 0, 0)[HEAD:]
        out = (mixed / total).astype(BF16)
        for h in range(halves):
            o_ref[h, i] = out[:, h * part : (h + 1) * part]
        lse_ref[0, :, i * block : (i + 1) * block] = top + jnp.log(total)


def cross_forward_kernel(q_ref, *refs):
    kv_refs, (o_ref, lse_ref) = refs[:-2], refs[-2:]
    halves, blocks, _, part = q_ref.shape
    query = with_zeros_below(gather_chunks(q_ref))
    top = total = mixed = None
    for kv_ref in kv_refs:
        for start in range(0, kv_ref.shape[1], KEY_TILE):
            pair = kv_ref[0, start : start + KEY_TILE]
            scores = contract(pair, query, 1, 0)
            tile_top = jnp.max(scores, 0, keepdims=True)
            new_top = tile_top if top is None else jnp.maximum(top, tile_top)
            weight = jnp.exp(scores - new_top)
            tile_total = jnp.sum(weight, 0, keepdims=True)
            tile_mixed = contract(pair, weight.astype(BF16), 0, 0)
            if top is None:
                total, mixed = tile_total, tile_mixed
            else:
                fade = jnp.exp(top - new_top)
                total = total * fade + tile_total
                mixed = mixed * fade + tile_mixed
            top = new_top
    out = (mixed[HEAD:] / total).astype(BF16)
    for h in range(halves):
        for b in range(blocks):
            at = (h * blocks + b) * part
            o_ref[h, b] = out[:, at : at + part]
    lse_ref[0] = top + jnp.log(total)


def cross_backward_kernel(q_ref, o_ref, do_ref, lse_ref, *refs):
    count = (len(refs) - 1) // 2
    kv_refs, dkv_refs, dq_ref = refs[:count], refs[count:-1], refs[-1]
    halves, blocks, _, part = q_ref.shape
    width = halves * blocks * part
    query = with_zeros_below(gather_chunks(q_ref))
    grad = gather_chunks(do_ref)
    inner = jnp.sum(
        grad.astype(F32) * gather_chunks(o_ref).astype(F32), 0, keepdims=True
    )
    grad = with_zeros_above(grad)
    both = jnp.concatenate([query, grad], 1)
    lse = lse_ref[0]
    query_grad = None
    for kv_ref, dkv_ref in zip(kv_refs, dkv_refs):
        for start in range(0, kv_ref.shape[1], KEY_TILE):
            pair = kv_ref[0, start : start + KEY_TILE]
            products = contract(pair, both, 1, 0)
            weight = jnp.exp(products[:, :width] - lse)
            slope = (weight * (products[:, width:] - inner)).astype(BF16)
            dkv_ref[0, start : start + KEY_TILE] = (
                contract(slope, query, 1, 1) + contract(weight.astype(BF16), grad, 1, 1)
            ).astype(BF16)
            part_grad = contract(pair, slope, 0, 0)
            query_grad = part_grad if query_grad is None else query_grad + part_grad
    out = (query_grad[:HEAD] * HEAD**-0.5).astype(BF16)
    for h in range(halves):
        for b in range(blocks):
            at = (h * blocks + b) * part
            dq_ref[h, b] = out[:, at : at + part]


def self_backward_kernel(at_ref, *refs):
    x_refs, refs = refs[:-10], refs[-10:]
    q_ref, kv_ref, o_ref, do_ref, lse_ref, grad_ref, dw_ref, db_ref, dkv_ref, all_ref = refs
    halves, blocks, _, part = o_ref.shape
    block = halves * part
    dkv_ref[...] = jnp.zeros_like(dkv_ref)
    parts = []
    for i in range(blocks):
        lanes = slice(i * block, (i + 1) * block)
        reach = (i + 1) * block
        keys = kv_ref[0, :reach]
        query = with_zeros_below(q_ref[0, :, lanes])
        grad = jnp.concatenate([do_ref[h, i] for h in range(halves)], 1)
        mixed = jnp.concatenate([o_ref[h, i] for h in range(halves)], 1)
        inner = jnp.sum(grad.astype(F32) * mixed.astype(F32), 0, keepdims=True)
        grad = with_zeros_above(grad)
        weight = jnp.exp(contract(keys, query, 1, 0) - lse_ref[0, :, lanes])
        slope = (weight * (contract(keys, grad, 1, 0) - inner)).astype(BF16)
        parts.append(contract(keys, slope, 0, 0)[:HEAD] * HEAD**-0.5)
        dkv_ref[:, :reach] += contract(query, slope, 1, 1) + contract(
            grad, weight.astype(BF16), 1, 1
        )
    grads = jnp.concatenate(
        [jnp.concatenate(parts, 1).astype(BF16), dkv_ref[...].astype(BF16)], 0
    )
    all_ref[...] = grads
    for i in range(blocks):
        for h in range(halves):
            at = i * block + h * part
            grad_ref[h, i] = grads[:, at : at + part]

    @pl.when(pl.program_id(0) == 0)
    def _():
        dw_ref[...] = jnp.zeros_like(dw_ref)
        db_ref[...] = jnp.zeros_like(db_ref)

    dw_ref[...] += sum(
        contract(all_ref[:, slot_at(at_ref[0], k, block)], x_ref[0], 1, 0)
        for k, x_ref in enumerate(x_refs)
    )
    db_ref[...] += jnp.sum(grads.astype(F32), 1, keepdims=True)


def encoder_kernel(at_ref, e_ref, w_ref, b_ref, *refs):
    out_refs, all_ref = refs[:-1], refs[-1]
    all_ref[...] = (contract(e_ref[...], w_ref[...], 1, 0) + b_ref[...]).astype(BF16)
    for k, out_ref in enumerate(out_refs):
        out_ref[...] = all_ref[:, slot_at(at_ref[0], k, 2 * HEAD)]


def encoder_back_kernel(at_ref, e_ref, w_ref, *refs):
    grad_refs, (part_ref, sum_ref, dw_ref, total_ref, all_ref) = refs[:-5], refs[-5:]
    for k, grad_ref in enumerate(grad_refs):
        all_ref[:, slot_at(at_ref[0], k, 2 * HEAD)] = grad_ref[...]
    grads = all_ref[...]
    part_ref[...] = contract(grads, w_ref[...], 1, 1).astype(BF16)

    @pl.when(pl.program_id(0) == 0)
    def _():
        total_ref[...] = jnp.zeros_like(total_ref)
        sum_ref[...] = jnp.zeros_like(sum_ref)

    total_ref[...] += contract(e_ref[...], grads, 0, 0)
    sum_ref[...] += jnp.sum(grads.astype(F32), 0, keepdims=True)

    @pl.when(pl.program_id(0) == pl.num_programs(0) - 1)
    def _():
        dw_ref[...] = total_ref[...].astype(BF16)


def plane_grad_kernel(sides, ready, at_ref, *refs):
    count = len(sides)
    lefts, rights, refs = refs[:count], refs[count : 2 * count], refs[2 * count :]
    ready_refs, out_refs = refs[:ready], refs[ready:]
    shard = out_refs[0].shape[1]
    for bit, out_ref in enumerate(out_refs):
        here = slot_at(at_ref[0], 2 * pl.program_id(0) + bit, shard)
        column = 0
        for left, right, side in zip(lefts, rights, sides):
            width = right.shape[1 - side]
            out_ref[0, :, column : column + width] = contract(
                left[:, here], right[...], 0, side
            ).astype(BF16)
            column += width
        for ready_ref in ready_refs:
            width = ready_ref.shape[1]
            out_ref[0, :, column : column + width] = ready_ref[here]
            column += width


def mlp_grad_kernel(two_ref, pre_ref, low_ref, active_ref, out_ref):
    width = pre_ref.shape[1]
    out_ref[:, :width] = contract(two_ref[...], pre_ref[...], 0, 0).astype(BF16)
    out_ref[:, width:] = contract(low_ref[...], active_ref[...], 0, 0).astype(BF16)


def halve_kernel(keep_ref, got_ref, *out_refs):
    size = out_refs[0].shape[0]
    for i, out_ref in enumerate(out_refs):
        for j in range(size):
            total = keep_ref[i * size + j].astype(F32) + got_ref[i * size + j].astype(F32)
            out_ref[j] = total.astype(BF16)


def by_first(shape, lead=1):
    return pl.BlockSpec((lead,) + shape[1:], lambda s: (s,) + (0,) * (len(shape) - 1))


def whole(shape):
    return pl.BlockSpec(shape, lambda s: (0,) * len(shape))


def shaped(shape, dtype):
    return jax.ShapeDtypeStruct(shape, dtype)


def call(kernel, seqs, in_specs, out_specs, out_shape, operands, cost, scratch=()):
    flops, transcendentals = cost
    moved = sum(o.size * o.dtype.itemsize for o in operands)
    moved += sum(o.size * o.dtype.itemsize for o in out_shape)
    return pl.pallas_call(
        kernel,
        grid=(seqs,),
        in_specs=in_specs,
        out_specs=out_specs,
        out_shape=out_shape,
        scratch_shapes=scratch,
        compiler_params=pltpu.CompilerParams(
            dimension_semantics=("arbitrary",), vmem_limit_bytes=VMEM_BYTES
        ),
        cost_estimate=pl.CostEstimate(
            flops=flops // COST_SHARE,
            bytes_accessed=moved // COST_SHARE,
            transcendentals=transcendentals // COST_SHARE,
        ),
    )(*operands)


def one_step(kernel, out, *operands, flops=0):
    specs = [IN_SMEM if v.dtype == jnp.int32 else whole(v.shape) for v in operands]
    return call(kernel, 1, specs, [whole(out)], [shaped(out, BF16)], operands, (flops, 0))[0]


def self_forward(at, slots, weights, query_bias, pair_bias, chunk_shape):
    seqs, block, width = slots[0].shape
    length = block * len(slots)
    halves = chunk_shape[0] // seqs
    query, pair, lse = (seqs, HEAD, length), (seqs, length, 2 * HEAD), (seqs, 1, length)
    return call(
        self_forward_kernel,
        seqs,
        [IN_SMEM]
        + [by_first(x.shape) for x in slots]
        + [whole(weights.shape), whole(query_bias.shape), whole(pair_bias.shape)],
        [by_first(query), by_first(pair), by_first(chunk_shape, halves), by_first(lse)],
        [shaped(query, BF16), shaped(pair, BF16), shaped(chunk_shape, BF16), shaped(lse, F32)],
        [at, *slots, weights, query_bias, pair_bias],
        (seqs * length * (2 * width * 3 * HEAD + 8 * length * HEAD), seqs * length * length),
    )


def cross_forward(query, pairs):
    seqs = pairs[0].shape[0]
    halves, blocks, _, part = query.shape
    halves //= seqs
    length = halves * blocks * part
    keys = sum(p.shape[1] for p in pairs)
    lse = (seqs, 1, length)
    return call(
        cross_forward_kernel,
        seqs,
        [by_first(query.shape, halves)] + [by_first(p.shape) for p in pairs],
        [by_first(query.shape, halves), by_first(lse)],
        [shaped(query.shape, BF16), shaped(lse, F32)],
        [query, *pairs],
        (seqs * length * keys * 8 * HEAD, seqs * length * keys),
    )


def cross_backward(query, mixed, grad, lse, pairs):
    seqs = pairs[0].shape[0]
    halves, blocks, _, part = query.shape
    halves //= seqs
    length = halves * blocks * part
    keys = sum(p.shape[1] for p in pairs)
    chunk = by_first(query.shape, halves)
    return call(
        cross_backward_kernel,
        seqs,
        [chunk, chunk, chunk, by_first(lse.shape)] + [by_first(p.shape) for p in pairs],
        [by_first(p.shape) for p in pairs] + [chunk],
        [shaped(p.shape, BF16) for p in pairs] + [shaped(query.shape, BF16)],
        [query, mixed, grad, lse, *pairs],
        (seqs * length * keys * 20 * HEAD, seqs * length * keys),
    )


def self_backward(at, slots, query, pair, mixed, grad, lse):
    seqs, block, width = slots[0].shape
    length = block * len(slots)
    halves = mixed.shape[0] // seqs
    chunk = by_first(mixed.shape, halves)
    out = mixed.shape[:2] + (3 * HEAD, mixed.shape[3])
    return call(
        self_backward_kernel,
        seqs,
        [IN_SMEM]
        + [by_first(x.shape) for x in slots]
        + [by_first(query.shape), by_first(pair.shape), chunk, chunk, by_first(lse.shape)],
        [by_first(out, halves), whole((3 * HEAD, width)), whole((3 * HEAD, 1))],
        [shaped(out, BF16), shaped((3 * HEAD, width), F32), shaped((3 * HEAD, 1), F32)],
        [at, *slots, query, pair, mixed, grad, lse],
        (seqs * length * (2 * width * 3 * HEAD + 20 * length * HEAD), seqs * length * length),
        [pltpu.VMEM((2 * HEAD, length), F32), pltpu.VMEM((3 * HEAD, length), BF16)],
    )


def encoder_pairs(at, rows, weights, bias, count):
    length, width = rows.shape
    tile = min(ROW_TILE, length)
    pair = (length, 2 * HEAD)
    return call(
        encoder_kernel,
        length // tile,
        [IN_SMEM, by_first(rows.shape, tile), whole(weights.shape), whole(bias.shape)],
        [by_first(pair, tile)] * count,
        [shaped(pair, BF16)] * count,
        [at, rows, weights, bias],
        (2 * length * width * weights.shape[1], 0),
        [pltpu.VMEM((tile, weights.shape[1]), BF16)],
    )


def encoder_back(at, rows, weights, grads):
    length, width = rows.shape
    tile = min(ROW_TILE, length)
    columns = weights.shape[1]
    return call(
        encoder_back_kernel,
        length // tile,
        [IN_SMEM, by_first(rows.shape, tile), whole(weights.shape)]
        + [by_first(g.shape, tile) for g in grads],
        [by_first(rows.shape, tile), whole((1, columns)), whole(weights.shape)],
        [shaped(rows.shape, BF16), shaped((1, columns), F32), shaped(weights.shape, BF16)],
        [at, rows, weights, *grads],
        (4 * length * width * columns, 0),
        [pltpu.VMEM(weights.shape, F32), pltpu.VMEM((tile, columns), BF16)],
    )


def mlp_grads(two, pre_low, low, active):
    count, width = two.shape
    columns = pre_low.shape[1]
    tile = 256
    strip = pl.BlockSpec((count, tile), lambda i: (0, i))
    out = (width, 2 * columns)
    return call(
        mlp_grad_kernel,
        width // tile,
        [strip, whole(pre_low.shape), strip, whole(active.shape)],
        [by_first(out, tile)],
        [shaped(out, BF16)],
        [two, pre_low, low, active],
        (4 * count * width * columns, 0),
    )[0]


def halve(keep, got, groups):
    count, rows, columns = keep.shape
    tile = min(512, columns)
    stack = pl.BlockSpec((count, rows, tile), lambda i: (0, 0, i))
    strip = pl.BlockSpec((count // groups, rows, tile), lambda i: (0, 0, i))
    return call(
        halve_kernel,
        columns // tile,
        [stack, stack],
        [strip] * groups,
        [shaped((count // groups, rows, columns), BF16)] * groups,
        [keep, got],
        (keep.size, 0),
    )


def plane_grads(at, items, ready, shard):
    lefts, rights, sides = zip(*items) if items else ((), (), ())
    width = (lefts[0].T if items else ready[0]).shape[0]
    columns = sum(right.shape[1 - side] for right, side in zip(rights, sides))
    columns += sum(v.shape[1] for v in ready)
    out = (width // shard // 2, shard, columns)
    flops = sum(2 * width * right.size for right in rights)
    return call(
        functools.partial(plane_grad_kernel, sides, len(ready)),
        out[0],
        [IN_SMEM] + [whole(v.shape) for v in (*lefts, *rights, *ready)],
        [by_first(out)] * 2,
        [shaped(out, BF16)] * 2,
        [at, *lefts, *rights, *ready],
        (flops, 0),
    )


def body(
    hidden_in,
    encoder_states,
    out_cotangent,
    self_proj,
    self_qv_bias,
    self_out_proj,
    cross_q_proj,
    cross_kv_proj,
    cross_qv_bias,
    cross_out_proj,
    up_proj,
    up_bias,
    down_proj,
    norm_gain,
    norm_bias,
    out_bias,
):
    blocks, ranks = lax.axis_size("ctx"), lax.axis_size("tp")
    plane = lax.axis_size("dp") * blocks
    own_ctx, own_tp = lax.axis_index("ctx"), lax.axis_index("tp")
    seqs, block, width = hidden_in.shape
    rows = seqs * block
    part = rows // ranks
    shard = width // plane
    heads_here = self_qv_bias.shape[0]
    local_width = heads_here * HEAD
    all_heads = heads_here * ranks
    enc_len = encoder_states.shape[1]
    hidden = up_proj.shape[1]
    slots = range(blocks)

    def ctx_swap(values, k):
        return lax.ppermute(values, "ctx", [(i, i ^ k) for i in slots])

    def tp_swap(values, k):
        return lax.ppermute(values, "tp", [(i, i ^ k) for i in range(ranks)])

    def exchange(values):
        return lax.all_to_all(values, HEADS, split_axis=0, concat_axis=0, tiled=True)

    def own_rows(values):
        return lax.dynamic_slice_in_dim(values.reshape(rows, width), own_tp * part, part, 0)

    def in_swap_order(values, axis):
        return [lax.dynamic_index_in_dim(values, own_ctx ^ k, axis, keepdims=False) for k in slots]

    ctx_at, plane_at = own_ctx.reshape(1), (lax.axis_index("dp") * blocks + own_ctx).reshape(1)

    def plane_swap(values, k):
        return lax.ppermute(values, PLANE, [(i, i ^ k) for i in range(plane)])

    def sum_begin(items, ready=()):
        if plane == 8:
            keep, send = plane_grads(plane_at, items, ready, shard)
            return (keep, plane_swap(send, 1))
        sums = [contract(left, right, 0, side).astype(BF16) for left, right, side in items]
        sums = jnp.concatenate([*sums, *ready], 1)
        return (lax.psum_scatter(sums, PLANE, scatter_dimension=0, tiled=True),)

    def sum_near(state, groups):
        return halve(*state, groups) if plane == 8 else state

    def sum_far(parts):
        return [plane_swap(part, 2 * j) if j else part for j, part in enumerate(parts)]

    def sum_dp(parts):
        return [parts[0], plane_swap(parts[1], 4)] if plane == 8 else parts

    def sum_x(parts):
        if plane != 8:
            return parts
        own, other = (parts[0][j].astype(F32) + parts[1][j].astype(F32) for j in range(2))
        return [own, plane_swap(other.astype(BF16), 2)]

    def sum_end(parts):
        return sum(part.astype(F32).reshape(shard, -1) for part in parts)

    def whole_on_ranks(values):
        values = jnp.broadcast_to(values[None], (ranks,) + values.shape)
        return lax.all_to_all(values, "tp", split_axis=0, concat_axis=0, tiled=True)

    bias_part = 2 * HEAD // plane
    count = heads_here * bias_part
    core_tokens, x_tokens = ctx_swap(hidden_in, 1), ctx_swap(hidden_in, 2)
    rank_at = own_tp.reshape(1)

    def rank_parts(values):
        return [values] + [tp_swap(values, k) for k in range(1, ranks)]

    def from_ranks(parts):
        out = (shard, parts[0].shape[0] * width)
        return one_step(rank_kernel, out, rank_at, *parts)

    square = one_step(
        square_pack_kernel, (3, shard, local_width), self_out_proj, cross_q_proj, cross_out_proj
    )
    square = rank_parts(square)
    vectors = jnp.concatenate([norm_gain, norm_bias, out_bias])
    small = jnp.concatenate([v.reshape(-1) for v in (self_qv_bias, cross_qv_bias, up_bias)])
    small = jnp.concatenate([vectors, small.reshape(-1, shard)])
    small = jnp.pad(small, ((0, 16 - small.shape[0]), (0, 0)))
    first = one_step(
        first_pack_kernel, (plane, 3 * HEAD + small.shape[0], shard), self_proj, small, flops=1 << 38
    )
    first = lax.all_to_all(first, PLANE, split_axis=0, concat_axis=0, tiled=True)
    kv_weights = cross_kv_proj.reshape(2, shard, heads_here, HEAD).transpose(1, 2, 0, 3)
    kv_weights = lax.all_gather(
        kv_weights.reshape(shard, heads_here * 2 * HEAD), PLANE, axis=0, tiled=True
    )

    core_tokens, x_tokens, first, square, up_proj, down_proj = together(
        core_tokens, x_tokens, first, square, up_proj, down_proj
    )

    square = lax.all_gather(from_ranks(square), PLANE, axis=0, tiled=True)
    mlp = one_step(mlp_pack_kernel, (shard, 2 * hidden), up_proj, down_proj)
    mlp_other = tp_swap(mlp, 2)
    x_slots = [hidden_in, core_tokens, x_tokens, ctx_swap(x_tokens, 1)]
    own_head = first[:, : 3 * HEAD].swapaxes(0, 1).reshape(3 * HEAD, width)
    small = first[:, 3 * HEAD :]
    vectors = small[:, :9].swapaxes(0, 1).reshape(9, width).astype(F32)
    gains, shifts, branch_bias = vectors[:3], vectors[3:6], vectors[6:]
    small = small[:, 9:].reshape(plane, -1)

    def head_bias(values):
        values = values.reshape(plane, heads_here, bias_part).swapaxes(0, 1)
        return values.reshape(heads_here, 2 * HEAD).astype(F32)

    self_bias = head_bias(small[:, :count])
    cross_bias = head_bias(small[:, count : 2 * count])
    up_vector = small[:, 2 * count : 2 * count + up_bias.size]
    up_vector = up_vector.reshape((plane,) + up_bias.shape).swapaxes(0, 1).reshape(1, hidden)
    enc_rows = encoder_states.reshape(-1, width)
    value_bias = jnp.concatenate([jnp.zeros((heads_here, HEAD), F32), cross_bias[:, HEAD:]], 1)
    pairs = encoder_pairs(ctx_at, enc_rows, kv_weights, value_bias.reshape(1, -1), blocks)
    x_slots, pairs = together(x_slots, pairs)
    pairs = [
        (ctx_swap(pair, k) if k else pair).reshape(seqs, enc_len, 2 * HEAD)
        for k, pair in enumerate(pairs)
    ]
    head_row = lax.dynamic_index_in_dim(self_bias, own_ctx, 0, keepdims=False)
    query_column = head_row[:HEAD].reshape(HEAD, 1)
    pair_row = jnp.concatenate([jnp.zeros((HEAD,), F32), head_row[HEAD:]]).reshape(1, 2 * HEAD)
    chunk_shape = (ranks, blocks, HEAD, part)
    self_query, self_pair, self_mixed, self_lse = self_forward(
        ctx_at, x_slots, own_head, query_column, pair_row, chunk_shape
    )
    tokens_f = own_rows(hidden_in).astype(F32)
    mixed_t = exchange(self_mixed.reshape(all_heads, HEAD, part)).reshape(width, part)
    mixed_t, square, mlp_other, self_proj, pairs, up_vector = together(
        mixed_t, square, mlp_other, self_proj, pairs, up_vector
    )
    up_vector = jnp.concatenate([up_vector, tp_swap(up_vector, 2)], 1).astype(F32)
    self_out_all, cross_q_all, cross_out_all = (square[:, i * width : (i + 1) * width] for i in range(3))
    mlp = jnp.concatenate(
        [mlp[:, :hidden], mlp_other[:, :hidden], mlp[:, hidden:], mlp_other[:, hidden:]], 1
    )
    mlp = lax.all_gather(mlp, PLANE, axis=0, tiled=True)
    up_all, down_all = mlp[:, : 2 * hidden], mlp[:, 2 * hidden :]
    rank_proj = rank_parts(self_proj)
    attn_branch = contract(mixed_t, self_out_all, 0, 1) + branch_bias[0]
    first_out, first_normed, first_inv = norm_forward(tokens_f + attn_branch, gains[0], shifts[0])
    first_low = first_out.astype(BF16)
    cross_query = contract(cross_q_all, first_low, 0, 1).astype(BF16)
    cross_query = exchange(cross_query.reshape(all_heads, HEAD, part)).reshape(chunk_shape)
    cross_row = lax.dynamic_index_in_dim(cross_bias, own_ctx, 0, keepdims=False)[:HEAD]
    cross_query = (
        (cross_query.astype(F32) + cross_row.reshape(HEAD, 1)).astype(BF16) * HEAD**-0.5
    )

    cross_mixed, cross_lse = cross_forward(cross_query, pairs)
    cross_mixed, rank_proj = together(cross_mixed, rank_proj)
    proj = from_ranks(rank_proj)
    cross_t = exchange(cross_mixed.reshape(all_heads, HEAD, part)).reshape(width, part)
    cross_branch = contract(cross_t, cross_out_all, 0, 1) + branch_bias[1]
    second_out, second_normed, second_inv = norm_forward(
        first_low.astype(F32) + cross_branch, gains[1], shifts[1]
    )
    second_low = second_out.astype(BF16)

    two = jnp.concatenate([second_low, tp_swap(second_low, 1)])
    pre_act = contract(two, up_all, 1, 0) + up_vector
    active = exact_gelu(pre_act).astype(BF16)
    mlp_part = contract(active, down_all, 1, 1)
    mlp_branch = (
        mlp_part[:part] + tp_swap(mlp_part[part:].astype(BF16), 1).astype(F32) + branch_bias[2]
    )
    third_out, third_normed, third_inv = norm_forward(
        second_low.astype(F32) + mlp_branch, gains[2], shifts[2]
    )
    hidden_out = third_out.astype(BF16)
    rms = jnp.stack([root_mean(attn_branch), root_mean(cross_branch), root_mean(mlp_branch)])

    out_grad = own_rows(out_cotangent).astype(F32)
    third_grad, gain_two, shift_two = norm_backward(out_grad, third_normed, third_inv, gains[2])
    mlp_bias_grad = jnp.sum(third_grad, 0)
    mlp_low = third_grad.astype(BF16)
    mlp_low = jnp.concatenate([mlp_low, tp_swap(mlp_low, 1)])
    active_grad = contract(mlp_low, down_all, 1, 0)
    pre_low = jax.vjp(exact_gelu, pre_act)[1](active_grad)[0].astype(BF16)
    mlp_grad = mlp_grads(two, pre_low, mlp_low, active)
    back_part = contract(pre_low, up_all, 1, 1)
    back_part, mlp_grad = together(back_part, mlp_grad)
    mlp_grad = lax.psum_scatter(mlp_grad, PLANE, scatter_dimension=0, tiled=True)
    back = back_part[:part] + tp_swap(back_part[part:].astype(BF16), 1).astype(F32)
    up_bias_grad = jnp.sum(pre_low.astype(F32), 0).reshape(2, hidden)
    second_grad, gain_one, shift_one = norm_backward(
        third_grad + back, second_normed, second_inv, gains[1]
    )
    cross_bias_sum = jnp.sum(second_grad, 0)
    second_grad_low = second_grad.astype(BF16)
    mix_grad = contract(cross_out_all, second_grad_low, 0, 1).astype(BF16)
    mix_grad = exchange(mix_grad.reshape(all_heads, HEAD, part)).reshape(chunk_shape)
    mix_grad, hidden_out = together(mix_grad, hidden_out)
    hidden_out = whole_on_ranks(hidden_out)
    *pair_grads, query_grad = cross_backward(cross_query, cross_mixed, mix_grad, cross_lse, pairs)
    query_grad, hidden_out = together(query_grad, hidden_out)
    query_grad = exchange(query_grad.reshape(all_heads, HEAD, part)).reshape(width, part)
    pair_grads = [
        (ctx_swap(g, k) if k else g).reshape(-1, 2 * HEAD) for k, g in enumerate(pair_grads)
    ]
    query_grad, proj = together(query_grad, proj)
    proj = lax.all_gather(proj, PLANE, axis=0, tiled=True)
    mlp_grad = mlp_grad.reshape(shard, 2, 2, hidden)
    mlp_grad = [mlp_grad[:, :, 0], tp_swap(mlp_grad[:, :, 1], 2)]
    query_sum = jnp.sum(query_grad.astype(F32), 1)

    first_grad, gain_zero, shift_zero = norm_backward(
        second_grad + contract(query_grad, cross_q_all, 0, 1), first_normed, first_inv, gains[0]
    )
    attn_bias_sum = jnp.sum(first_grad, 0)
    first_grad_low = first_grad.astype(BF16)
    squares = [(first_grad_low, mixed_t, 1), (first_low, query_grad, 1), (second_grad_low, cross_t, 1)]
    square_grad = sum_begin(squares)

    self_mix_grad = contract(self_out_all, first_grad_low, 0, 1).astype(BF16)
    self_mix_grad = exchange(self_mix_grad.reshape(all_heads, HEAD, part)).reshape(chunk_shape)
    self_mix_grad, pair_grads = together(self_mix_grad, pair_grads)
    enc_part, value_sum, kv_grad = encoder_back(ctx_at, enc_rows, kv_weights, pair_grads)
    value_sum = value_sum.reshape(heads_here, 2 * HEAD)[:, HEAD:]
    self_mix_grad, enc_part, mlp_grad, kv_grad = together(self_mix_grad, enc_part, mlp_grad, kv_grad)
    mlp_grad = mlp_grad[0].astype(F32) + mlp_grad[1].astype(F32)
    up_out, down_out = mlp_grad[:, 0], mlp_grad[:, 1].T
    encoder_grad = lax.psum_scatter(
        enc_part.reshape(seqs, enc_len, width), "tp", scatter_dimension=2, tiled=True
    )
    kv_grad = sum_begin((), [kv_grad])
    stacked, head_grad, head_sum = self_backward(
        ctx_at, x_slots, self_query, self_pair, self_mixed, self_mix_grad, self_lse
    )
    stacked, head_grad, square_grad, kv_grad = together(stacked, head_grad, square_grad, kv_grad)
    kv_grad = sum_dp(sum_near(kv_grad, 2))
    square_grad = sum_near(square_grad, 4)
    stacked = exchange(stacked.reshape(all_heads, 3 * HEAD, part)).reshape(all_heads, 3, HEAD, part)
    stacked, head_grad, square_grad, kv_grad = together(stacked, head_grad, square_grad, kv_grad)
    square_grad, kv_grad = sum_far(square_grad), sum_x(kv_grad)
    square_grad = sum_end(square_grad)
    square_grad = square_grad.reshape(shard, 3, ranks, width // ranks)

    stacked = stacked.swapaxes(0, 1).reshape(3, width, part)
    input_grad = first_grad + (
        contract(stacked[0], proj[:, :width], 0, 1)
        + contract(stacked[1], proj[:, width : 2 * width], 0, 1)
        + contract(stacked[2], proj[:, 2 * width :], 0, 1)
    )
    input_grad = input_grad.astype(BF16)

    def for_rank(k):
        return lax.dynamic_index_in_dim(square_grad, own_tp ^ k, 2, False)

    square_grad = for_rank(0) + sum(
        tp_swap(for_rank(k).astype(BF16), k).astype(F32) for k in range(1, ranks)
    )
    self_out_out, cross_q_out, cross_out_out = (
        square_grad[:, 0].T,
        square_grad[:, 1],
        square_grad[:, 2].T,
    )
    head_grad = head_grad.reshape(3 * HEAD, plane, shard).swapaxes(0, 1)
    head_sum = head_sum.reshape(3, HEAD)
    head_sum = jnp.concatenate([head_sum[0], head_sum[2]]).reshape(plane, bias_part, 1)
    head_sum = jnp.pad(head_sum, ((0, 0), (0, 16 - bias_part), (0, 0)))
    def pieces(values):
        return values.reshape(-1, plane, values.shape[-1] // plane).swapaxes(0, 1).reshape(plane, -1)

    norm_sums = jnp.stack(
        [gain_zero, gain_one, gain_two, shift_zero, shift_one, shift_two]
        + [attn_bias_sum, cross_bias_sum, mlp_bias_grad]
    )
    up_cols = up_bias.shape[1]
    up_sums = pieces(up_bias_grad.reshape(-1, plane * up_cols))
    query_sums = pieces(jnp.pad(query_sum.reshape(all_heads, HEAD), ((0, 0), (0, HEAD))))
    value_sums = pieces(jnp.pad(value_sum, ((0, 0), (HEAD, 0))))
    sums = jnp.concatenate([pieces(norm_sums), up_sums, query_sums, value_sums], 1)
    sums = jnp.pad(sums, ((0, 0), (0, 16 * shard - sums.shape[1]))).reshape(plane, 16, shard)
    head_grad = jnp.concatenate(
        [head_grad, jnp.broadcast_to(head_sum, (plane, 16, shard)), sums], 1
    ).astype(BF16)
    head_grad = lax.all_to_all(head_grad, PLANE, split_axis=0, concat_axis=0, tiled=True)
    head_grad = head_grad.reshape(-1, blocks, 3 * HEAD + 32, shard).astype(F32)
    kv_grad = sum_end(kv_grad).reshape(shard, heads_here, 2, HEAD)
    kv_grad = kv_grad.transpose(2, 0, 1, 3).reshape(2, shard, local_width)
    sums = jnp.sum(head_grad[:, :, 3 * HEAD + 16 :], (0, 1))
    head_grad = jnp.sum(head_grad[:, :, : 3 * HEAD + 16], 0)
    self_proj_out = head_grad[:, : 3 * HEAD].reshape(blocks, 3, HEAD, shard)
    self_proj_out = self_proj_out.transpose(1, 3, 0, 2).reshape(3, shard, local_width)
    self_bias_out = head_grad[:, 3 * HEAD : 3 * HEAD + bias_part, 0]
    norm_out, sums = sums[:9].reshape(-1), sums[9:].reshape(-1)
    sums = jnp.concatenate([norm_out, sums[: 2 * up_bias.size + ranks * count + count], rms.reshape(-1)])
    ends = [0, norm_out.size]
    for size in (up_bias.size, up_bias.size, ranks * count, count, rms.size):
        ends.append(ends[-1] + size)
    sums = jnp.pad(sums, (0, 16 * width - sums.size)).reshape(16, width).astype(BF16)

    last = whole_on_ranks(jnp.concatenate([input_grad, sums]))
    last, encoder_grad = together(last, encoder_grad)
    input_grad, encoder_grad = last[:, :part].astype(F32), encoder_grad.astype(F32)
    sums = last[:, part:].astype(F32).reshape(ranks, -1)
    norm_out, up_own, up_other, query_sums, value_sums, rms = (
        sums[:, i:j] for i, j in zip(ends, ends[1:])
    )
    norm_out = jnp.sum(norm_out, 0).reshape(9, shard)

    def of_rank(values, at):
        return lax.dynamic_index_in_dim(values, at, 0, False)

    up_bias_out = (of_rank(up_own, own_tp) + of_rank(up_other, own_tp ^ 2)).reshape(up_bias.shape)
    cross_bias_out = of_rank(jnp.sum(query_sums, 0).reshape(ranks, count), own_tp)
    cross_bias_out = (cross_bias_out + of_rank(value_sums, own_tp)).reshape(heads_here, bias_part)
    rms = rms.reshape(ranks, 3, part).swapaxes(0, 1).reshape(3, rows)
    rms = jnp.concatenate([root_mean(hidden_in.reshape(rows, width).astype(F32))[None], rms])
    return (
        hidden_out.reshape(seqs, block, width),
        input_grad.reshape(seqs, block, width),
        encoder_grad,
        self_proj_out,
        self_bias_out,
        self_out_out,
        cross_q_out,
        kv_grad,
        cross_bias_out,
        cross_out_out,
        up_out,
        up_bias_out,
        down_out,
        norm_out[:3],
        norm_out[3:6],
        norm_out[6:],
        rms.reshape(4, seqs, block),
    )


def solution(mesh):
    rows, heads, columns = P("dp", "ctx", None), P("tp", PLANE), P(PLANE, "tp")
    stacked, vectors = P(None, PLANE, "tp"), P(None, PLANE)
    weights = (
        stacked, heads, heads, columns, stacked, heads, heads, columns, heads, heads,
        vectors, vectors, vectors,
    )
    return jax.shard_map(
        body,
        mesh=mesh,
        in_specs=(rows, rows, rows) + weights,
        out_specs=(rows, rows, P("dp", "ctx", "tp")) + weights + (P(None, "dp", "ctx"),),
        check_vma=False,
    )
```

time: 777 us -> 509 us (0.66)
  waiting for transfers between devices: 380 us -> 152 us
  blocking collectives: 107 us -> 27.2 us
  starting transfers between devices: 49.7 us -> 96.7 us
  Pallas kernels: 52.8 us -> 84.2 us
  matrix products: 65.7 us -> 40.6 us
  other arithmetic: 40.2 us -> 21.8 us
    all_gather x3 -> x0, blocking collectives: 93.7 us -> none  [the longest x1 69.6 us: body(): small = lax.all_gather(small, ('dp', 'ctx', 'tp')).reshape(plane, ranks, -1)]
    reduce_scatter x1, waiting for transfers between devices: 75.8 us -> 0.01 us  [body(): lax.psum_scatter(enc_part.reshape(seqs, enc_len, width), 'tp', scatter_di...]
    all_gather x5 -> x2, waiting for transfers between devices: 65.4 us -> 10.1 us  [the longest x1 10.1 us: body(): square = lax.all_gather(from_ranks(square), PLANE, axis=0, tiled=True)]
    reduce_scatter x1, waiting for transfers between devices: 53 us -> 0.02 us  [body(): lax.psum_scatter(mlp_grad, PLANE, scatter_dimension=0, tiled=True)]
    ppermute x6 -> x9, waiting for transfers between devices: 50.3 us -> 7.6 us  [ctx_swap(): return lax.ppermute(values, 'ctx', [(i, i ^ k) for i in slots])]
    unnamed x14 -> x6, waiting for transfers between devices: 33.1 us -> 0.1 us
    pallas_call x4 -> x16, Pallas kernels: 52.8 us -> 84.2 us  [call(): pl.pallas_call(kernel, grid=(seqs,), in_specs=in_specs, out_specs=out_spe...]
    all_to_all x6 -> x5, waiting for transfers between devices: 27.3 us -> 54 us  [exchange(): lax.all_to_all(values, HEADS, split_axis=0, concat_axis=0, tiled=True)]
  transfers between devices with their start and end apart: 33 -> 47, of which waited for: 21 -> 19; matrix products, arithmetic and copies ran while one was open for 13% -> 15% of each run, Pallas kernels for 4% -> 16%
where the time goes in v2:
time: 509 us; the launch traced here: 501 us
  waiting for transfers between devices  152 us (30%)
  starting transfers between devices  96.7 us (19%)
  Pallas kernels  84.2 us (17%)
  local copies, waits for them, and re-layouts  62.3 us (12%)
  matrix products  40.6 us (8%)
  blocking collectives  27.2 us (5%)
  other arithmetic  21.8 us (4%)
  between operations  15.9 us (3%)
    pallas_call x16, Pallas kernels, call(): pl.pallas_call(kernel, grid=(seqs,), in_specs=in_specs, out_specs=out_spe...  84.2 us
    ppermute x16, waiting for transfers between devices, tp_swap(): return lax.ppermute(values, 'tp', [(i, i ^ k) for i in range(ranks)])  62.6 us
    all_to_all x5, waiting for transfers between devices, exchange(): lax.all_to_all(values, HEADS, split_axis=0, concat_axis=0, tiled=True)  54 us
    dot_general x13, matrix products, contract(): lax.dot_general(left, right, (((left_dim,), (right_dim,)), ((), ())), pre...  40.6 us
    unnamed x172, local copies, waits for them, and re-layouts  33 us
    ppermute x16, starting transfers between devices, tp_swap(): return lax.ppermute(values, 'tp', [(i, i ^ k) for i in range(ranks)])  32.6 us
    all_to_all x2, blocking collectives, exchange(): lax.all_to_all(values, HEADS, split_axis=0, concat_axis=0, tiled=True)  27.2 us
    all_to_all x5, starting transfers between devices, exchange(): lax.all_to_all(values, HEADS, split_axis=0, concat_axis=0, tiled=True)  23.3 us
  transfers between devices with their start and end apart: 47, of which 19 were waited for; matrix products, arithmetic and copies ran while one was open for 15% of the time, Pallas kernels for 16%

profile of v2, /device:TPU:0, one launch (start us, length us, event | category | flops | bytes accessed | tf_op | source)
XLA Modules:
  0.0 500.8 jit_solution(14154098020767442128)
XLA Ops:
  25.4 6.5 %collective-permute-done.2.refs_1_ = bf16[3,128,256]{2,1,0:T(8,128)(2,1)S(1)} collective-permute-done((bf16[3,128,256]{2,1,0:T(8,128)(2,1)S(1)}, bf16[3,128,256]{2,1,0:T(8,128)(2,1)S(1)}, u32[]{:S(2)}, u32[]{:S(2)}) %collective-permute-start.2) | collective-permute-done | bytes 196640 | tf_op jit(solution)/shard_map/ppermute | solution.py:533
  31.9 7.8 %collective-permute-done.3.refs_2_ = bf16[3,128,256]{2,1,0:T(8,128)(2,1)S(1)} collective-permute-done((bf16[3,128,256]{2,1,0:T(8,128)(2,1)S(1)}, bf16[3,128,256]{2,1,0:T(8,128)(2,1)S(1)}, u32[]{:S(2)}, u32[]{:S(2)}) %collective-permute-start.3) | collective-permute-done | bytes 196640 | tf_op jit(solution)/shard_map/ppermute | solution.py:533
  39.7 4.5 all-to-all-done
  50.8 6.0 %shard_map.289 = (bf16[2048,128]{1,0:T(8,128)(2,1)S(1)}, bf16[2048,128]{1,0:T(8,128)(2,1)}, bf16[2048,128]{1,0:T(8,128)(2,1)}, bf16[2048,128]{1,0:T(8,128)(2,1)}) custom-call(s32[1]{0:T(128)} %bitcast.at_ref, bf16[2048,1024]{1,0:T(8,128)(2,1)} %bitcast.226, bf16[1024,512]{1,0:T(8,128)(2,1)S(1)} %copy-done.2, f32[1,512]{1,0:T(1,128)S(1)} %bitcast.225), custom_call_target="tpu_custom_call" | custom-call | flops 214748368 | bytes 734208 | tf_op jit(solution)/shard_map/pallas_call | solution.py:316
  60.3 8.0 %shard_map.290 = (bf16[2,64,1024]{2,1,0:T(8,128)(2,1)S(1)}, bf16[2,1024,128]{2,1,0:T(8,128)(2,1)S(1)}, bf16[4,4,64,128]{3,2,1,0:T(8,128)(2,1)}, f32[2,1,1024]{2,1,0:T(1,128)S(1)}) custom-call(s32[1]{0:T(128)} %bitcast.at_ref, bf16[2,256,1024]{2,1,0:T(8,128)(2,1)S(1)} %copy-done, bf16[2,256,1024]{2,1,0:T(8,128)(2,1)S(1)} %collective-permute-done.refs_1_, ...), custom_call_target="tpu_custom_call" | custom-call | flops 187904816 | bytes 564506 | tf_op jit(solution)/shard_map/pallas_call | solution.py:316
  75.3 23.0 %all-to-all-done.1 = bf16[16,64,128]{2,1,0:T(8,128)(2,1)S(1)} async-done(((bf16[16,64,128]{2,1,0:T(8,128)(2,1)}), bf16[16,64,128]{2,1,0:T(8,128)(2,1)S(1)}, u32[]{:S(2)}, u32[]{:S(2)}) %all-to-all-start.1) | async-done | bytes 262176 | tf_op jit(solution)/shard_map/all_to_all | solution.py:536
  98.3 10.1 %all-gather.7.cloned.1.call-done = bf16[1024,3072]{1,0:T(8,128)(2,1)} async-done(((bf16[128,3072]{1,0:T(8,128)(2,1)}), bf16[1024,3072]{1,0:T(8,128)(2,1)}) %all-gather.7.cloned.1.call-update) | async-done | bytes 6291472 | tf_op jit(solution)/shard_map/all_gather | solution.py:612
  119.1 4.7 all-to-all-start.2
  128.6 5.8 %all-to-all-done.2 = bf16[16,64,128]{2,1,0:T(8,128)(2,1)S(1)} async-done(((bf16[16,64,128]{2,1,0:T(8,128)(2,1)}), bf16[16,64,128]{2,1,0:T(8,128)(2,1)S(1)}, u32[]{:S(2)}, u32[]{:S(2)}) %all-to-all-start.2) | async-done | bytes 262176 | tf_op jit(solution)/shard_map/all_to_all | solution.py:536
  134.6 14.1 %shard_map.293 = (bf16[4,4,64,128]{3,2,1,0:T(8,128)(2,1)S(1)}, f32[2,1,1024]{2,1,0:T(1,128)S(1)}) custom-call(bf16[4,4,64,128]{3,2,1,0:T(8,128)(2,1)S(1)} %fusion.76.q_ref, bf16[2,1024,128]{2,1,0:T(8,128)(2,1)S(1)} %bitcast.218, bf16[2,1024,128]{2,1,0:T(8,128)(2,1)} %bitcast.17.refs_1_, bf16[2,1024,128]{2,1,0:T(8,128)(2,1)} %bitcast.18.refs_2_, ...), custom_call_target="tpu_custom_call" | custom-call | flops 429496736 | bytes 262963 | tf_op jit(solution)/shard_map/pallas_call | solution.py:316
  150.0 13.4 %all_to_all.55 = bf16[16,64,128]{2,1,0:T(8,128)(2,1)S(1)} all-to-all(bf16[16,64,128]{2,1,0:T(8,128)(2,1)S(1)} %bitcast.222), channel_id=1, replica_groups=mesh['dp'=2,'ctx'=4,'tp'=4] {'tp','ctx'}, dimensions={0} | all-to-all | bytes 524288 | tf_op jit(solution)/shard_map/all_to_all | solution.py:536
  168.6 5.2 %collective-permute-done.14 = bf16[1,1024]{1,0:T(2,128)(2,1)S(1)} collective-permute-done((bf16[1,1024]{1,0:T(2,128)(2,1)S(1)}, bf16[1,1024]{1,0:T(2,128)(2,1)S(1)}, u32[]{:S(2)}, u32[]{:S(2)}) %collective-permute-start.14) | collective-permute-done | bytes 2080 | tf_op jit(solution)/shard_map/ppermute | solution.py:533
  175.2 7.5 %multiply_convert_fusion = (bf16[256,2048]{1,0:T(8,128)(2,1)S(1)}, f32[256,2048]{1,0:T(8,128)S(1)}, f32[256,2048]{1,0:T(8,128)S(1)}) fusion(f32[2048]{0:T(1024)S(1)} %maximum_convert_fusion, bf16[1024,4096]{1,0:T(8,128)(2,1)} %all-gather.9.cloned.1.call-done, bf16[128,1024]{1,0:T(8,128)(2,1)S(1)} %collective-permute-done.13, ...), kind=kOutput, calls=%fused_computation.19 | convolution fusion | flops 1109393408 | bytes 9969664 | tf_op jit(solution)/shard_map/dot_general | solution.py:24
  185.1 6.4 %collective-permute-done.15 = bf16[128,1024]{1,0:T(8,128)(2,1)S(1)} collective-permute-done((bf16[128,1024]{1,0:T(8,128)(2,1)S(1)}, bf16[128,1024]{1,0:T(8,128)(2,1)S(1)}, u32[]{:S(2)}, u32[]{:S(2)}) %collective-permute-start.15) | collective-permute-done | bytes 262176 | tf_op jit(solution)/shard_map/ppermute | solution.py:533
  195.2 5.5 %collective-permute-done.16 = bf16[128,1024]{1,0:T(8,128)(2,1)S(1)} collective-permute-done((bf16[128,1024]{1,0:T(8,128)(2,1)S(1)}, bf16[128,1024]{1,0:T(8,128)(2,1)S(1)}, u32[]{:S(2)}, u32[]{:S(2)}) %collective-permute-start.16) | collective-permute-done | bytes 262176 | tf_op jit(solution)/shard_map/ppermute | solution.py:533
  202.6 5.1 %shard_map.294 = bf16[1024,4096]{1,0:T(8,128)(2,1)} custom-call(bf16[256,1024]{1,0:T(8,128)(2,1)S(1)} %pad_maximum_fusion.1.two_ref, bf16[256,2048]{1,0:T(8,128)(2,1)S(1)} %get-tuple-element.347.pre_ref, bf16[256,1024]{1,0:T(8,128)(2,1)S(1)} %pad_maximum_fusion.2.low_ref, bf16[256,2048]{1,0:T(8,128)(2,1)S(1)} %get-tuple-element.299.active_ref), custom_call_target="tpu_custom_call" | custom-call | flops 214748368 | bytes 1153433 | tf_op jit(solution)/shard_map/pallas_call | solution.py:316
  215.2 4.7 collective-permute-done.17
  224.5 13.8 %all_to_all.56 = bf16[16,64,128]{2,1,0:T(8,128)(2,1)} all-to-all(bf16[16,64,128]{2,1,0:T(8,128)(2,1)S(1)} %bitcast.249), channel_id=1, replica_groups=mesh['dp'=2,'ctx'=4,'tp'=4] {'tp','ctx'}, dimensions={0} | all-to-all | bytes 524288 | tf_op jit(solution)/shard_map/all_to_all | solution.py:536
  245.8 21.5 %shard_map.295 = (bf16[2,1024,128]{2,1,0:T(8,128)(2,1)S(1)}, bf16[2,1024,128]{2,1,0:T(8,128)(2,1)S(1)}, bf16[2,1024,128]{2,1,0:T(8,128)(2,1)S(1)}, bf16[2,1024,1...) custom-call(bf16[4,4,64,128]{3,2,1,0:T(8,128)(2,1)S(1)} %fusion.76.q_ref, bf16[4,4,64,128]{3,2,1,0:T(8,128)(2,1)S(1)} %copy-done.14, ...), custom_call_target="tpu_custom_call" | custom-call | flops 1073741824 | bytes 525107 | tf_op jit(solution)/shard_map/pallas_call | solution.py:316
  270.4 5.3 %all-to-all-start.6 = ((bf16[16,64,128]{2,1,0:T(8,128)(2,1)}), bf16[16,64,128]{2,1,0:T(8,128)(2,1)S(1)}, u32[]{:S(2)}, u32[]{:S(2)}) async-start(bf16[16,64,128]{2,1,0:T(8,128)(2,1)} %bitcast.223), calls=%async_computation.6 | async-start | bytes 524288 | tf_op jit(solution)/shard_map/all_to_all | solution.py:536
  280.7 5.1 %all-to-all-done.6 = bf16[16,64,128]{2,1,0:T(8,128)(2,1)S(1)} async-done(((bf16[16,64,128]{2,1,0:T(8,128)(2,1)}), bf16[16,64,128]{2,1,0:T(8,128)(2,1)S(1)}, u32[]{:S(2)}, u32[]{:S(2)}) %all-to-all-start.6) | async-done | bytes 262176 | tf_op jit(solution)/shard_map/all_to_all | solution.py:536
  314.2 7.6 %collective-permute-done.20 = bf16[2,1024,128]{2,1,0:T(8,128)(2,1)} collective-permute-done((bf16[2,1024,128]{2,1,0:T(8,128)(2,1)}, bf16[2,1024,128]{2,1,0:T(8,128)(2,1)}, u32[]{:S(2)}, u32[]{:S(2)}) %collective-permute-start.20) | collective-permute-done | bytes 524320 | tf_op jit(solution)/shard_map/ppermute | solution.py:530
  323.7 9.3 %shard_map.297 = (bf16[2048,1024]{1,0:T(8,128)(2,1)}, f32[1,512]{1,0:T(1,128)S(1)}, bf16[1024,512]{1,0:T(8,128)(2,1)S(1)}) custom-call(s32[1]{0:T(128)} %bitcast.at_ref, bf16[2048,1024]{1,0:T(8,128)(2,1)} %bitcast.227, bf16[1024,512]{1,0:T(8,128)(2,1)} %all-gather.5.cloned.1.call-done.w_ref, bf16[2048,128]{1,0:T(8,128)(2,1)S(1)} %bitcast.220, ...), custom_call_target="tpu_custom_call" | custom-call | flops 429496736 | bytes 1258496 | tf_op jit(solution)/shard_map/pallas_call | solution.py:316
  340.3 7.8 %shard_map.298 = (bf16[4,4,192,128]{3,2,1,0:T(8,128)(2,1)}, f32[192,1024]{1,0:T(8,128)S(1)}, f32[192,1]{1,0:T(8,128)S(1)}) custom-call(s32[1]{0:T(128)} %bitcast.at_ref, bf16[2,256,1024]{2,1,0:T(8,128)(2,1)S(1)} %copy-done, bf16[2,256,1024]{2,1,0:T(8,128)(2,1)} %copy-done.1, bf16[2,256,1024]{2,1,0:T(8,128)(2,1)} %collective-permute-done.1.refs_2_, ...), custom_call_target="tpu_custom_call" | custom-call | flops 348966080 | bytes 708685 | tf_op jit(solution)/shard_map/pallas_call | solution.py:316
  348.9 6.2 %all-to-all-start.8 = ((bf16[16,192,128]{2,1,0:T(8,128)(2,1)}), bf16[16,192,128]{2,1,0:T(8,128)(2,1)}, u32[]{:S(2)}, u32[]{:S(2)}) async-start(bf16[16,192,128]{2,1,0:T(8,128)(2,1)} %bitcast.53), calls=%async_computation.9 | async-start | bytes 1572864 | tf_op jit(solution)/shard_map/all_to_all | solution.py:536
  361.9 4.6 shard_map.301
  367.3 19.3 %all-to-all-done.8 = bf16[16,192,128]{2,1,0:T(8,128)(2,1)} async-done(((bf16[16,192,128]{2,1,0:T(8,128)(2,1)}), bf16[16,192,128]{2,1,0:T(8,128)(2,1)}, u32[]{:S(2)}, u32[]{:S(2)}) %all-to-all-start.8) | async-done | bytes 786464 | tf_op jit(solution)/shard_map/all_to_all | solution.py:536
  387.6 5.9 %all-to-all-start.9 = ((bf16[8,224,128]{2,1,0:T(8,128)(2,1)}), bf16[8,224,128]{2,1,0:T(8,128)(2,1)}, u32[]{:S(2)}, u32[]{:S(2)}) async-start(bf16[8,224,128]{2,1,0:T(8,128)(2,1)} %pad_maximum_fusion.3), calls=%async_computation.10 | async-start | bytes 917504 | tf_op jit(solution)/shard_map/all_to_all | solution.py:796
  413.4 11.7 %all-to-all-start.10 = ((bf16[4,144,1024]{2,1,0:T(8,128)(2,1)}), bf16[4,144,1024]{2,1,0:T(8,128)(2,1)}, u32[]{:S(2)}, u32[]{:S(2)}) async-start(bf16[4,144,1024]{2,1,0:T(8,128)(2,1)} %broadcast_in_dim.11), calls=%async_computation.11 | async-start | bytes 2359296 | tf_op jit(solution)/shard_map/all_to_all | solution.py:577
  425.1 13.1 %collective-permute-done.31 = bf16[128,512]{1,0:T(8,128)(2,1)S(1)} collective-permute-done((bf16[128,512]{1,0:T(8,128)(2,1)}, bf16[128,512]{1,0:T(8,128)(2,1)S(1)}, u32[]{:S(2)}, u32[]{:S(2)}) %collective-permute-start.31) | collective-permute-done | bytes 131104 | tf_op jit(solution)/shard_map/ppermute | solution.py:547
  444.1 9.1 %collective-permute-start.30 = (bf16[128,3,256]{2,0,1:T(8,128)(2,1)S(1)}, bf16[128,3,256]{2,0,1:T(8,128)(2,1)S(1)}, u32[]{:S(2)}, u32[]{:S(2)}) collective-permute-start(bf16[128,3,256]{2,0,1:T(8,128)(2,1)S(1)} %bitcast.252), channel_id=1, source_target_pairs={{0,3},{1,2},{2,1},{3,0},{4,7},{5,6},{6,5},{7,4},{8,11},{9,10},{10,... | collective-permute-start | bytes 589832 | tf_op jit(solution)/shard_map/ppermute | solution.py:533
  459.2 21.3 %collective-permute-done.29 = bf16[128,3,256]{2,0,1:T(8,128)(2,1)S(1)} collective-permute-done((bf16[128,3,256]{2,0,1:T(8,128)(2,1)S(1)}, bf16[128,3,256]{2,0,1:T(8,128)(2,1)S(1)}, u32[]{:S(2)}, u32[]{:S(2)}) %collective-permute-start.29) | collective-permute-done | bytes 196640 | tf_op jit(solution)/shard_map/ppermute | solution.py:533
  (413 shorter events, 185.0 us)
Async XLA Ops:
  7.2 42.4 %all-gather.5.cloned.1.call-start = ((), (), s32[]{:S(2)}) async-start(), calls=%async_computation.13 | async-start | bytes 1179648 | tf_op jit(solution)/shard_map/all_gather | solution.py:604
  7.2 37.1 %collective-permute-start = (bf16[2,256,1024]{2,1,0:T(8,128)(2,1)}, bf16[2,256,1024]{2,1,0:T(8,128)(2,1)S(1)}, u32[]{:S(2)}, u32[]{:S(2)}) collective-permute-start(bf16[2,256,1024]{2,1,0:T(8,128)(2,1)} %refs_0_.2), channel_id=1, source_target_pairs={{0,4},{4,0},{8,12},{12,8},{1,5},{5,1},{9,13},{13,9},{2,6},{6,2},{1... | collective-permute-start | bytes 3145736 | tf_op jit(solution)/shard_map/ppermute | solution.py:530
  7.8 36.5 %collective-permute-start.1 = (bf16[2,256,1024]{2,1,0:T(8,128)(2,1)}, bf16[2,256,1024]{2,1,0:T(8,128)(2,1)}, u32[]{:S(2)}, u32[]{:S(2)}) collective-permute-start(bf16[2,256,1024]{2,1,0:T(8,128)(2,1)} %refs_0_.2), channel_id=1, source_target_pairs={{0,8},{4,12},{8,0},{12,4},{1,9},{5,13},{9,1},{13,5},{2,10},{6,14},... | collective-permute-start | bytes 3145736 | tf_op jit(solution)/shard_map/ppermute | solution.py:530
  17.2 27.1 %all-to-all-start = ((bf16[8,208,128]{2,1,0:T(8,128)(2,1)}), bf16[8,208,128]{2,1,0:T(8,128)(2,1)S(1)}, u32[]{:S(2)}, u32[]{:S(2)}) async-start(bf16[8,208,128]{2,1,0:T(8,128)(2,1)} %shard_map.287), calls=%async_computation | async-start | bytes 851968 | tf_op jit(solution)/shard_map/all_to_all | solution.py:602
  20.8 87.6 %all-gather.7.cloned.1.call-start = ((), (), s32[]{:S(2)}) async-start(), calls=%async_computation.14 | async-start | bytes 7077888 | tf_op jit(solution)/shard_map/all_gather | solution.py:612
  46.2 29.1 %collective-permute-start.6 = (bf16[128,2048]{1,0:T(8,128)(2,1)S(1)}, bf16[128,2048]{1,0:T(8,128)(2,1)}, u32[]{:S(2)}, u32[]{:S(2)}) collective-permute-start(bf16[128,2048]{1,0:T(8,128)(2,1)S(1)} %shard_map.292), channel_id=1, source_target_pairs={{0,2},{1,3},{2,0},{3,1},{4,6},{5,7},{6,4},{7,5},{8,10},{9,11},{10,... | collective-permute-start | bytes 1572872 | tf_op jit(solution)/shard_map/ppermute | solution.py:533
  56.8 41.5 %collective-permute-start.7 = (bf16[2048,128]{1,0:T(8,128)(2,1)}, bf16[2048,128]{1,0:T(8,128)(2,1)}, u32[]{:S(2)}, u32[]{:S(2)}) collective-permute-start(bf16[2048,128]{1,0:T(8,128)(2,1)} %get-tuple-element.132), channel_id=1, source_target_pairs={{0,4},{4,0},{8,12},{12,8},{1,5},{5,1},{9,13},{13,9},{2,6},{6,2},{1... | collective-permute-start | bytes 1572872 | tf_op jit(solution)/shard_map/ppermute | solution.py:530
  57.1 41.2 %collective-permute-start.8 = (bf16[2048,128]{1,0:T(8,128)(2,1)}, bf16[2048,128]{1,0:T(8,128)(2,1)}, u32[]{:S(2)}, u32[]{:S(2)}) collective-permute-start(bf16[2048,128]{1,0:T(8,128)(2,1)} %get-tuple-element.133), channel_id=1, source_target_pairs={{0,8},{4,12},{8,0},{12,4},{1,9},{5,13},{9,1},{13,5},{2,10},{6,14},... | collective-permute-start | bytes 1572872 | tf_op jit(solution)/shard_map/ppermute | solution.py:530
  57.9 40.4 %collective-permute-start.9 = (bf16[2048,128]{1,0:T(8,128)(2,1)}, bf16[2048,128]{1,0:T(8,128)(2,1)}, u32[]{:S(2)}, u32[]{:S(2)}) collective-permute-start(bf16[2048,128]{1,0:T(8,128)(2,1)} %get-tuple-element.134), channel_id=1, source_target_pairs={{0,12},{4,8},{8,4},{12,0},{1,13},{5,9},{9,5},{13,1},{2,14},{6,10},... | collective-permute-start | bytes 1572872 | tf_op jit(solution)/shard_map/ppermute | solution.py:530
  69.8 28.5 %all-to-all-start.1 = ((bf16[16,64,128]{2,1,0:T(8,128)(2,1)}), bf16[16,64,128]{2,1,0:T(8,128)(2,1)S(1)}, u32[]{:S(2)}, u32[]{:S(2)}) async-start(bf16[16,64,128]{2,1,0:T(8,128)(2,1)} %bitcast.13), calls=%async_computation.1 | async-start | bytes 524288 | tf_op jit(solution)/shard_map/all_to_all | solution.py:536
  73.4 101.8 %all-gather.9.cloned.1.call-start = ((), (), s32[]{:S(2)}) async-start(), calls=%async_computation.15 | async-start | bytes 9437184 | tf_op jit(solution)/shard_map/all_gather | solution.py:655
  123.9 178.7 %reduce-scatter.3.cloned.1.call-start = ((), (), s32[]{:S(2)}) async-start(), calls=%async_computation.16 | async-start | bytes 9437184 | tf_op jit(solution)/shard_map/reduce_scatter | solution.py:701
  124.2 24.5 %collective-permute-start.10 = (bf16[3,128,256]{2,1,0:T(8,128)(2,1)S(1)}, bf16[3,128,256]{2,1,0:T(8,128)(2,1)S(1)}, u32[]{:S(2)}, u32[]{:S(2)}) collective-permute-start(bf16[3,128,256]{2,1,0:T(8,128)(2,1)S(1)} %copy-done.20), channel_id=1, source_target_pairs={{0,1},{1,0},{2,3},{3,2},{4,5},{5,4},{6,7},{7,6},{8,9},{9,8},{10,11... | collective-permute-start | bytes 589832 | tf_op jit(solution)/shard_map/ppermute | solution.py:533
  126.2 23.2 %collective-permute-start.11 = (bf16[3,128,256]{2,1,0:T(8,128)(2,1)S(1)}, bf16[3,128,256]{2,1,0:T(8,128)(2,1)S(1)}, u32[]{:S(2)}, u32[]{:S(2)}) collective-permute-start(bf16[3,128,256]{2,1,0:T(8,128)(2,1)S(1)} %copy-done.20), channel_id=1, source_target_pairs={{0,2},{1,3},{2,0},{3,1},{4,6},{5,7},{6,4},{7,5},{8,10},{9,11},{10,... | collective-permute-start | bytes 589832 | tf_op jit(solution)/shard_map/ppermute | solution.py:533
  239.4 30.9 %all-to-all-start.5 = ((bf16[4,128,1024]{2,1,0:T(8,128)(2,1)}), bf16[4,128,1024]{2,1,0:T(8,128)(2,1)}, u32[]{:S(2)}, u32[]{:S(2)}) async-start(bf16[4,128,1024]{2,1,0:T(8,128)(2,1)} %broadcast_in_dim.8), calls=%async_computation.5 | async-start | bytes 2097152 | tf_op jit(solution)/shard_map/all_to_all | solution.py:577
  275.7 126.9 %all-gather.11.cloned.1.call-start = ((), (), s32[]{:S(2)}) async-start(), calls=%async_computation.17 | async-start | bytes 7077888 | tf_op jit(solution)/shard_map/all_gather | solution.py:720
  285.8 27.7 %collective-permute-start.18 = (bf16[2,1024,128]{2,1,0:T(8,128)(2,1)}, bf16[2,1024,128]{2,1,0:T(8,128)(2,1)S(1)}, u32[]{:S(2)}, u32[]{:S(2)}) collective-permute-start(bf16[2,1024,128]{2,1,0:T(8,128)(2,1)} %copy-done.35), channel_id=1, source_target_pairs={{0,4},{4,0},{8,12},{12,8},{1,5},{5,1},{9,13},{13,9},{2,6},{6,2},{1... | collective-permute-start | bytes 1572872 | tf_op jit(solution)/shard_map/ppermute | solution.py:530
  285.9 28.4 %collective-permute-start.19 = (bf16[2,1024,128]{2,1,0:T(8,128)(2,1)}, bf16[2,1024,128]{2,1,0:T(8,128)(2,1)}, u32[]{:S(2)}, u32[]{:S(2)}) collective-permute-start(bf16[2,1024,128]{2,1,0:T(8,128)(2,1)} %copy-done.34), channel_id=1, source_target_pairs={{0,8},{4,12},{8,0},{12,4},{1,9},{5,13},{9,1},{13,5},{2,10},{6,14},... | collective-permute-start | bytes 1572872 | tf_op jit(solution)/shard_map/ppermute | solution.py:530
  286.4 35.4 %collective-permute-start.20 = (bf16[2,1024,128]{2,1,0:T(8,128)(2,1)}, bf16[2,1024,128]{2,1,0:T(8,128)(2,1)}, u32[]{:S(2)}, u32[]{:S(2)}) collective-permute-start(bf16[2,1024,128]{2,1,0:T(8,128)(2,1)} %copy-done.33), channel_id=1, source_target_pairs={{0,12},{4,8},{8,4},{12,0},{1,13},{5,9},{9,5},{13,1},{2,14},{6,10},... | collective-permute-start | bytes 1572872 | tf_op jit(solution)/shard_map/ppermute | solution.py:530
  295.5 52.6 %collective-permute-start.22 = (bf16[4,128,3072]{2,1,0:T(8,128)(2,1)}, bf16[4,128,3072]{2,1,0:T(8,128)(2,1)}, u32[]{:S(2)}, u32[]{:S(2)}) collective-permute-start(bf16[4,128,3072]{2,1,0:T(8,128)(2,1)} %get-tuple-element.177), channel_id=1, source_target_pairs={{0,4},{4,0},{8,12},{12,8},{16,20},{20,16},{24,28},{28,24},{1,5},{5... | collective-permute-start | bytes 9437192 | tf_op jit(solution)/shard_map/ppermute | solution.py:547
  298.9 23.8 %all-to-all-start.7 = ((bf16[16,64,128]{2,1,0:T(8,128)(2,1)}), bf16[16,64,128]{2,1,0:T(8,128)(2,1)S(1)}, u32[]{:S(2)}, u32[]{:S(2)}) async-start(bf16[16,64,128]{2,1,0:T(8,128)(2,1)} %bitcast.44), calls=%async_computation.7 | async-start | bytes 524288 | tf_op jit(solution)/shard_map/all_to_all | solution.py:536
  302.5 180.3 %reduce-scatter.5.cloned.1.call-start = ((), (), s32[]{:S(2)}) async-start(), calls=%async_computation.18 | async-start | bytes 5242880 | tf_op jit(solution)/shard_map/reduce_scatter | solution.py:741
  310.4 26.6 %collective-permute-start.21 = (bf16[128,2,1024]{2,0,1:T(8,128)(2,1)}, bf16[128,2,1024]{2,0,1:T(8,128)(2,1)}, u32[]{:S(2)}, u32[]{:S(2)}) collective-permute-start(bf16[128,2,1024]{2,0,1:T(8,128)(2,1)} %bitcast.200), channel_id=1, source_target_pairs={{0,2},{1,3},{2,0},{3,1},{4,6},{5,7},{6,4},{7,5},{8,10},{9,11},{10,... | collective-permute-start | bytes 1572872 | tf_op jit(solution)/shard_map/ppermute | solution.py:533
  348.9 37.7 %all-to-all-start.8 = ((bf16[16,192,128]{2,1,0:T(8,128)(2,1)}), bf16[16,192,128]{2,1,0:T(8,128)(2,1)}, u32[]{:S(2)}, u32[]{:S(2)}) async-start(bf16[16,192,128]{2,1,0:T(8,128)(2,1)} %bitcast.53), calls=%async_computation.9 | async-start | bytes 1572864 | tf_op jit(solution)/shard_map/all_to_all | solution.py:536
  387.6 22.4 %all-to-all-start.9 = ((bf16[8,224,128]{2,1,0:T(8,128)(2,1)}), bf16[8,224,128]{2,1,0:T(8,128)(2,1)}, u32[]{:S(2)}, u32[]{:S(2)}) async-start(bf16[8,224,128]{2,1,0:T(8,128)(2,1)} %pad_maximum_fusion.3), calls=%async_computation.10 | async-start | bytes 917504 | tf_op jit(solution)/shard_map/all_to_all | solution.py:796
  393.6 46.6 %collective-permute-start.27 = (bf16[1,128,3072]{2,1,0:T(8,128)(2,1)}, bf16[1,128,3072]{2,1,0:T(8,128)(2,1)}, u32[]{:S(2)}, u32[]{:S(2)}) collective-permute-start(bf16[1,128,3072]{2,1,0:T(8,128)(2,1)} %copy-done.32), channel_id=1, source_target_pairs={{0,24},{4,28},{8,16},{12,20},{16,8},{20,12},{24,0},{28,4},{1,25},{... | collective-permute-start | bytes 2359304 | tf_op jit(solution)/shard_map/ppermute | solution.py:547
  396.6 43.6 %collective-permute-start.26 = (bf16[1,128,3072]{2,1,0:T(8,128)(2,1)S(1)}, bf16[1,128,3072]{2,1,0:T(8,128)(2,1)}, u32[]{:S(2)}, u32[]{:S(2)}) collective-permute-start(bf16[1,128,3072]{2,1,0:T(8,128)(2,1)S(1)} %get-tuple-element.203), channel_id=1, source_target_pairs={{0,16},{4,20},{8,24},{12,28},{16,0},{20,4},{24,8},{28,12},{1,17},{... | collective-permute-start | bytes 2359304 | tf_op jit(solution)/shard_map/ppermute | solution.py:547
  397.1 43.0 %collective-permute-start.25 = (bf16[1,128,3072]{2,1,0:T(8,128)(2,1)S(1)}, bf16[1,128,3072]{2,1,0:T(8,128)(2,1)}, u32[]{:S(2)}, u32[]{:S(2)}) collective-permute-start(bf16[1,128,3072]{2,1,0:T(8,128)(2,1)S(1)} %get-tuple-element.202), channel_id=1, source_target_pairs={{0,8},{4,12},{8,0},{12,4},{16,24},{20,28},{24,16},{28,20},{1,9},{5... | collective-permute-start | bytes 2359304 | tf_op jit(solution)/shard_map/ppermute | solution.py:547
  398.8 39.4 %collective-permute-start.31 = (bf16[128,512]{1,0:T(8,128)(2,1)}, bf16[128,512]{1,0:T(8,128)(2,1)S(1)}, u32[]{:S(2)}, u32[]{:S(2)}) collective-permute-start(bf16[128,512]{1,0:T(8,128)(2,1)} %fusion.80), channel_id=1, source_target_pairs={{0,8},{4,12},{8,0},{12,4},{16,24},{20,28},{24,16},{28,20},{1,9},{5... | collective-permute-start | bytes 393224 | tf_op jit(solution)/shard_map/ppermute | solution.py:547
  413.4 69.4 %all-to-all-start.10 = ((bf16[4,144,1024]{2,1,0:T(8,128)(2,1)}), bf16[4,144,1024]{2,1,0:T(8,128)(2,1)}, u32[]{:S(2)}, u32[]{:S(2)}) async-start(bf16[4,144,1024]{2,1,0:T(8,128)(2,1)} %broadcast_in_dim.11), calls=%async_computation.11 | async-start | bytes 2359296 | tf_op jit(solution)/shard_map/all_to_all | solution.py:577
  453.3 27.2 %collective-permute-start.29 = (bf16[128,3,256]{2,0,1:T(8,128)(2,1)S(1)}, bf16[128,3,256]{2,0,1:T(8,128)(2,1)S(1)}, u32[]{:S(2)}, u32[]{:S(2)}) collective-permute-start(bf16[128,3,256]{2,0,1:T(8,128)(2,1)S(1)} %bitcast.253), channel_id=1, source_target_pairs={{0,2},{1,3},{2,0},{3,1},{4,6},{5,7},{6,4},{7,5},{8,10},{9,11},{10,... | collective-permute-start | bytes 589832 | tf_op jit(solution)/shard_map/ppermute | solution.py:533
  456.1 24.4 %collective-permute-start.28 = (bf16[128,3,256]{2,0,1:T(8,128)(2,1)S(1)}, bf16[128,3,256]{2,0,1:T(8,128)(2,1)S(1)}, u32[]{:S(2)}, u32[]{:S(2)}) collective-permute-start(bf16[128,3,256]{2,0,1:T(8,128)(2,1)S(1)} %bitcast.254), channel_id=1, source_target_pairs={{0,1},{1,0},{2,3},{3,2},{4,5},{5,4},{6,7},{7,6},{8,9},{9,8},{10,11... | collective-permute-start | bytes 589832 | tf_op jit(solution)/shard_map/ppermute | solution.py:533
  (88 other events, 734.5 us)
Sparse Core Ops, SparseCore 0:
  12.3 28.7 all-gather.4
  45.6 62.7 all-gather.6
  110.8 59.1 all-gather.8
  212.3 72.1 reduce-scatter.2
  286.4 56.4 all-gather.10
  345.2 96.9 reduce-scatter.4

commit v3 on v2

--- a/solution.py
+++ b/solution.py
@@ -10,6 +10,7 @@
 EPSILON = 1e-05
 HEAD = 64
 KEY_TILE = 512
+STAT_ROWS = 16
 ROW_TILE = 512
 COST_SHARE = 10
 VMEM_BYTES = 50 * 1024 * 1024
@@ -132,61 +133,83 @@
         lse_ref[0, :, i * block : (i + 1) * block] = top + jnp.log(total)
 
 
+def spread(values):
+    rows = []
+    for _ in range(3):
+        rows.append(values.astype(BF16))
+        values = values - rows[-1].astype(F32)
+    return rows
+
+
+def gathered(rows, at):
+    return sum(rows[at + i : at + i + 1].astype(F32) for i in range(3))
+
+
 def cross_forward_kernel(q_ref, *refs):
-    kv_refs, (o_ref, lse_ref) = refs[:-2], refs[-2:]
-    halves, blocks, _, part = q_ref.shape
-    query = with_zeros_below(gather_chunks(q_ref))
-    top = total = mixed = None
-    for kv_ref in kv_refs:
-        for start in range(0, kv_ref.shape[1], KEY_TILE):
-            pair = kv_ref[0, start : start + KEY_TILE]
-            scores = contract(pair, query, 1, 0)
-            tile_top = jnp.max(scores, 0, keepdims=True)
-            new_top = tile_top if top is None else jnp.maximum(top, tile_top)
-            weight = jnp.exp(scores - new_top)
-            tile_total = jnp.sum(weight, 0, keepdims=True)
-            tile_mixed = contract(pair, weight.astype(BF16), 0, 0)
-            if top is None:
-                total, mixed = tile_total, tile_mixed
-            else:
-                fade = jnp.exp(top - new_top)
-                total = total * fade + tile_total
-                mixed = mixed * fade + tile_mixed
-            top = new_top
-    out = (mixed[HEAD:] / total).astype(BF16)
+    kv_refs, o_ref = refs[:-1], refs[-1]
+    halves, blocks, features, part = q_ref.shape
+    queries = gather_chunks(q_ref)
+    heads = features // HEAD
+    outs, stats = [], []
+    for n in range(heads):
+        query = with_zeros_below(queries[n * HEAD : (n + 1) * HEAD])
+        lanes = slice(n * 2 * HEAD, (n + 1) * 2 * HEAD)
+        top = total = mixed = None
+        for kv_ref in kv_refs:
+            for start in range(0, kv_ref.shape[1], KEY_TILE):
+                pair = kv_ref[0, start : start + KEY_TILE, lanes]
+                scores = contract(pair, query, 1, 0)
+                tile_top = jnp.max(scores, 0, keepdims=True)
+                new_top = tile_top if top is None else jnp.maximum(top, tile_top)
+                weight = jnp.exp(scores - new_top)
+                tile_total = jnp.sum(weight, 0, keepdims=True)
+                tile_mixed = contract(pair, weight.astype(BF16), 0, 0)
+                if top is None:
+                    total, mixed = tile_total, tile_mixed
+                else:
+                    fade = jnp.exp(top - new_top)
+                    total = total * fade + tile_total
+                    mixed = mixed * fade + tile_mixed
+                top = new_top
+        outs.append((mixed[HEAD:] / total).astype(BF16))
+        stats += spread(top + jnp.log(total))
+    spare = jnp.zeros((STAT_ROWS - len(stats), stats[0].shape[1]), BF16)
+    out = jnp.concatenate([*outs, *stats, spare], 0)
     for h in range(halves):
         for b in range(blocks):
             at = (h * blocks + b) * part
             o_ref[h, b] = out[:, at : at + part]
-    lse_ref[0] = top + jnp.log(total)
-
-
-def cross_backward_kernel(q_ref, o_ref, do_ref, lse_ref, *refs):
+
+
+def cross_backward_kernel(q_ref, do_ref, *refs):
     count = (len(refs) - 1) // 2
     kv_refs, dkv_refs, dq_ref = refs[:count], refs[count:-1], refs[-1]
-    halves, blocks, _, part = q_ref.shape
+    halves, blocks, features, part = q_ref.shape
     width = halves * blocks * part
-    query = with_zeros_below(gather_chunks(q_ref))
-    grad = gather_chunks(do_ref)
-    inner = jnp.sum(
-        grad.astype(F32) * gather_chunks(o_ref).astype(F32), 0, keepdims=True
-    )
-    grad = with_zeros_above(grad)
-    both = jnp.concatenate([query, grad], 1)
-    lse = lse_ref[0]
-    query_grad = None
-    for kv_ref, dkv_ref in zip(kv_refs, dkv_refs):
-        for start in range(0, kv_ref.shape[1], KEY_TILE):
-            pair = kv_ref[0, start : start + KEY_TILE]
-            products = contract(pair, both, 1, 0)
-            weight = jnp.exp(products[:, :width] - lse)
-            slope = (weight * (products[:, width:] - inner)).astype(BF16)
-            dkv_ref[0, start : start + KEY_TILE] = (
-                contract(slope, query, 1, 1) + contract(weight.astype(BF16), grad, 1, 1)
-            ).astype(BF16)
-            part_grad = contract(pair, slope, 0, 0)
-            query_grad = part_grad if query_grad is None else query_grad + part_grad
-    out = (query_grad[:HEAD] * HEAD**-0.5).astype(BF16)
+    queries, grads = gather_chunks(q_ref), gather_chunks(do_ref)
+    heads = features // HEAD
+    outs = []
+    for n in range(heads):
+        query = with_zeros_below(queries[n * HEAD : (n + 1) * HEAD])
+        grad = with_zeros_above(grads[n * HEAD : (n + 1) * HEAD])
+        lse = gathered(grads, features + 6 * n)
+        inner = gathered(grads, features + 6 * n + 3)
+        lanes = slice(n * 2 * HEAD, (n + 1) * 2 * HEAD)
+        both = jnp.concatenate([query, grad], 1)
+        query_grad = None
+        for kv_ref, dkv_ref in zip(kv_refs, dkv_refs):
+            for start in range(0, kv_ref.shape[1], KEY_TILE):
+                pair = kv_ref[0, start : start + KEY_TILE, lanes]
+                products = contract(pair, both, 1, 0)
+                weight = jnp.exp(products[:, :width] - lse)
+                slope = (weight * (products[:, width:] - inner)).astype(BF16)
+                dkv_ref[0, start : start + KEY_TILE, lanes] = (
+                    contract(slope, query, 1, 1) + contract(weight.astype(BF16), grad, 1, 1)
+                ).astype(BF16)
+                part_grad = contract(pair, slope, 0, 0)
+                query_grad = part_grad if query_grad is None else query_grad + part_grad
+        outs.append((query_grad[:HEAD] * HEAD**-0.5).astype(BF16))
+    out = jnp.concatenate(outs, 0)
     for h in range(halves):
         for b in range(blocks):
             at = (h * blocks + b) * part
@@ -240,13 +263,13 @@
     out_refs, all_ref = refs[:-1], refs[-1]
     all_ref[...] = (contract(e_ref[...], w_ref[...], 1, 0) + b_ref[...]).astype(BF16)
     for k, out_ref in enumerate(out_refs):
-        out_ref[...] = all_ref[:, slot_at(at_ref[0], k, 2 * HEAD)]
+        out_ref[...] = all_ref[:, slot_at(at_ref[0], k, out_ref.shape[1])]
 
 
 def encoder_back_kernel(at_ref, e_ref, w_ref, *refs):
     grad_refs, (part_ref, sum_ref, dw_ref, total_ref, all_ref) = refs[:-5], refs[-5:]
     for k, grad_ref in enumerate(grad_refs):
-        all_ref[:, slot_at(at_ref[0], k, 2 * HEAD)] = grad_ref[...]
+        all_ref[:, slot_at(at_ref[0], k, grad_ref.shape[1])] = grad_ref[...]
     grads = all_ref[...]
     part_ref[...] = contract(grads, w_ref[...], 1, 1).astype(BF16)
 
@@ -295,6 +318,28 @@
         for j in range(size):
             total = keep_ref[i * size + j].astype(F32) + got_ref[i * size + j].astype(F32)
             out_ref[j] = total.astype(BF16)
+
+
+def rank_split_kernel(count, at_ref, *refs):
+    part_refs, own_ref, send_refs = refs[:count], refs[count], refs[count + 1 :]
+    kinds, _, columns = own_ref.shape
+    for i in range(kinds):
+        for k, out_ref in enumerate((own_ref, *send_refs)):
+            first = (i * (len(send_refs) + 1) + (at_ref[0] ^ k)) * columns
+            here = pl.ds(pl.multiple_of(first, columns), columns)
+            total = sum(part_ref[0, :, here].astype(F32) for part_ref in part_refs)
+            out_ref[i] = total.astype(out_ref.dtype)
+
+
+def input_grad_kernel(stacked_ref, proj_ref, first_ref, out_ref, all_ref):
+    @pl.when(pl.program_id(0) == 0)
+    def _():
+        heads = stacked_ref.shape[0]
+        for j in range(3):
+            rows = [stacked_ref[h, j * HEAD : (j + 1) * HEAD] for h in range(heads)]
+            all_ref[:, j * heads * HEAD : (j + 1) * heads * HEAD] = jnp.concatenate(rows, 0).T
+
+    out_ref[...] = (first_ref[...] + contract(all_ref[...], proj_ref[...], 1, 1)).astype(BF16)
 
 
 def by_first(shape, lead=1):
@@ -356,37 +401,36 @@
 
 def cross_forward(query, pairs):
     seqs = pairs[0].shape[0]
-    halves, blocks, _, part = query.shape
+    halves, blocks, features, part = query.shape
     halves //= seqs
     length = halves * blocks * part
     keys = sum(p.shape[1] for p in pairs)
-    lse = (seqs, 1, length)
+    out = (halves * seqs, blocks, features + STAT_ROWS, part)
     return call(
         cross_forward_kernel,
         seqs,
         [by_first(query.shape, halves)] + [by_first(p.shape) for p in pairs],
-        [by_first(query.shape, halves), by_first(lse)],
-        [shaped(query.shape, BF16), shaped(lse, F32)],
+        [by_first(out, halves)],
+        [shaped(out, BF16)],
         [query, *pairs],
-        (seqs * length * keys * 8 * HEAD, seqs * length * keys),
-    )
-
-
-def cross_backward(query, mixed, grad, lse, pairs):
+        (seqs * length * keys * 8 * features, seqs * length * keys * features // HEAD),
+    )[0]
+
+
+def cross_backward(query, grad, pairs):
     seqs = pairs[0].shape[0]
-    halves, blocks, _, part = query.shape
+    halves, blocks, features, part = query.shape
     halves //= seqs
     length = halves * blocks * part
     keys = sum(p.shape[1] for p in pairs)
-    chunk = by_first(query.shape, halves)
     return call(
         cross_backward_kernel,
         seqs,
-        [chunk, chunk, chunk, by_first(lse.shape)] + [by_first(p.shape) for p in pairs],
-        [by_first(p.shape) for p in pairs] + [chunk],
+        [by_first(query.shape, halves), by_first(grad.shape, halves)] + [by_first(p.shape) for p in pairs],
+        [by_first(p.shape) for p in pairs] + [by_first(query.shape, halves)],
         [shaped(p.shape, BF16) for p in pairs] + [shaped(query.shape, BF16)],
-        [query, mixed, grad, lse, *pairs],
-        (seqs * length * keys * 20 * HEAD, seqs * length * keys),
+        [query, grad, *pairs],
+        (seqs * length * keys * 20 * features, seqs * length * keys * features // HEAD),
     )
 
 
@@ -413,7 +457,7 @@
 def encoder_pairs(at, rows, weights, bias, count):
     length, width = rows.shape
     tile = min(ROW_TILE, length)
-    pair = (length, 2 * HEAD)
+    pair = (length, weights.shape[1] // count)
     return call(
         encoder_kernel,
         length // tile,
@@ -474,6 +518,36 @@
         [keep, got],
         (keep.size, 0),
     )
+
+
+def rank_split(at, parts, kinds, ranks):
+    _, rows, columns = parts[0].shape
+    out = (kinds, rows, columns // kinds // ranks)
+    return call(
+        functools.partial(rank_split_kernel, len(parts)),
+        1,
+        [IN_SMEM] + [whole(v.shape) for v in parts],
+        [whole(out)] * ranks,
+        [shaped(out, F32)] + [shaped(out, BF16)] * (ranks - 1),
+        [at, *parts],
+        (len(parts) * parts[0].size, 0),
+    )
+
+
+def input_grads(stacked, proj, first):
+    part, width = first.shape
+    tile = 256
+    strip = pl.BlockSpec((part, tile), lambda i: (0, i))
+    return call(
+        input_grad_kernel,
+        width // tile,
+        [whole(stacked.shape), by_first(proj.shape, tile), strip],
+        [strip],
+        [shaped(first.shape, BF16)],
+        [stacked, proj, first],
+        (2 * part * proj.size, 0),
+        [pltpu.VMEM((part, proj.shape[1]), BF16)],
+    )[0]
 
 
 def plane_grads(at, items, ready, shard):
@@ -541,6 +615,10 @@
     def in_swap_order(values, axis):
         return [lax.dynamic_index_in_dim(values, own_ctx ^ k, axis, keepdims=False) for k in slots]
 
+    cores = 2
+    pair_heads = heads_here // cores
+    pair_rows = pair_heads * HEAD
+    core_at = lax.rem(own_ctx, cores).reshape(1)
     ctx_at, plane_at = own_ctx.reshape(1), (lax.axis_index("dp") * blocks + own_ctx).reshape(1)
 
     def plane_swap(values, k):
@@ -592,12 +670,13 @@
         square_pack_kernel, (3, shard, local_width), self_out_proj, cross_q_proj, cross_out_proj
     )
     square = rank_parts(square)
+    square, first_proj, core_tokens, x_tokens = together(square, self_proj, core_tokens, x_tokens)
     vectors = jnp.concatenate([norm_gain, norm_bias, out_bias])
     small = jnp.concatenate([v.reshape(-1) for v in (self_qv_bias, cross_qv_bias, up_bias)])
     small = jnp.concatenate([vectors, small.reshape(-1, shard)])
     small = jnp.pad(small, ((0, 16 - small.shape[0]), (0, 0)))
     first = one_step(
-        first_pack_kernel, (plane, 3 * HEAD + small.shape[0], shard), self_proj, small, flops=1 << 38
+        first_pack_kernel, (plane, 3 * HEAD + small.shape[0], shard), first_proj, small
     )
     first = lax.all_to_all(first, PLANE, split_axis=0, concat_axis=0, tiled=True)
     kv_weights = cross_kv_proj.reshape(2, shard, heads_here, HEAD).transpose(1, 2, 0, 3)
@@ -605,8 +684,8 @@
         kv_weights.reshape(shard, heads_here * 2 * HEAD), PLANE, axis=0, tiled=True
     )
 
-    core_tokens, x_tokens, first, square, up_proj, down_proj = together(
-        core_tokens, x_tokens, first, square, up_proj, down_proj
+    core_tokens, x_tokens, first, up_proj, down_proj = together(
+        core_tokens, x_tokens, first, up_proj, down_proj
     )
 
     square = lax.all_gather(from_ranks(square), PLANE, axis=0, tiled=True)
@@ -629,12 +708,21 @@
     up_vector = up_vector.reshape((plane,) + up_bias.shape).swapaxes(0, 1).reshape(1, hidden)
     enc_rows = encoder_states.reshape(-1, width)
     value_bias = jnp.concatenate([jnp.zeros((heads_here, HEAD), F32), cross_bias[:, HEAD:]], 1)
-    pairs = encoder_pairs(ctx_at, enc_rows, kv_weights, value_bias.reshape(1, -1), blocks)
+    pairs = encoder_pairs(core_at, enc_rows, kv_weights, value_bias.reshape(1, -1), cores)
     x_slots, pairs = together(x_slots, pairs)
     pairs = [
-        (ctx_swap(pair, k) if k else pair).reshape(seqs, enc_len, 2 * HEAD)
+        (ctx_swap(pair, k) if k else pair).reshape(seqs, enc_len, 2 * pair_rows)
         for k, pair in enumerate(pairs)
     ]
+
+    def to_pairs(values):
+        values = values.reshape(ranks, 1, cores, -1, part)
+        values = jnp.broadcast_to(values, (ranks, blocks // cores) + values.shape[2:])
+        return exchange(values.reshape(all_heads, -1, part)).reshape(ranks, blocks, -1, part)
+
+    def from_pairs(values):
+        values = exchange(values.reshape(all_heads, -1, part))
+        return values.reshape(ranks, blocks // cores, cores, -1, part)
     head_row = lax.dynamic_index_in_dim(self_bias, own_ctx, 0, keepdims=False)
     query_column = head_row[:HEAD].reshape(HEAD, 1)
     pair_row = jnp.concatenate([jnp.zeros((HEAD,), F32), head_row[HEAD:]]).reshape(1, 2 * HEAD)
@@ -659,16 +747,23 @@
     first_out, first_normed, first_inv = norm_forward(tokens_f + attn_branch, gains[0], shifts[0])
     first_low = first_out.astype(BF16)
     cross_query = contract(cross_q_all, first_low, 0, 1).astype(BF16)
-    cross_query = exchange(cross_query.reshape(all_heads, HEAD, part)).reshape(chunk_shape)
-    cross_row = lax.dynamic_index_in_dim(cross_bias, own_ctx, 0, keepdims=False)[:HEAD]
+    cross_query = to_pairs(cross_query)
+    cross_rows = lax.dynamic_slice_in_dim(cross_bias[:, :HEAD], core_at[0] * pair_heads, pair_heads, 0)
     cross_query = (
-        (cross_query.astype(F32) + cross_row.reshape(HEAD, 1)).astype(BF16) * HEAD**-0.5
-    )
-
-    cross_mixed, cross_lse = cross_forward(cross_query, pairs)
+        (cross_query.astype(F32) + cross_rows.reshape(pair_rows, 1)).astype(BF16) * HEAD**-0.5
+    )
+    cross_mixed = cross_forward(cross_query, pairs)
     cross_mixed, rank_proj = together(cross_mixed, rank_proj)
-    proj = from_ranks(rank_proj)
-    cross_t = exchange(cross_mixed.reshape(all_heads, HEAD, part)).reshape(width, part)
+    proj = lax.all_gather(from_ranks(rank_proj), PLANE, axis=0, tiled=True)
+    halves = from_pairs(cross_mixed)
+    stats = halves[:, :, :, pair_rows : pair_rows + 3 * pair_heads].astype(F32)
+    stats = jnp.sum(stats.reshape(ranks, blocks // cores, cores, pair_heads, 3, part), 4, keepdims=True)
+    top = jnp.max(stats, 1, keepdims=True)
+    shares = jnp.exp(stats - top)
+    total = jnp.sum(shares, 1, keepdims=True)
+    halves = halves[:, :, :, :pair_rows].reshape(ranks, blocks // cores, cores, pair_heads, HEAD, part)
+    cross_t = jnp.sum(halves.astype(F32) * (shares / total), 1).astype(BF16).reshape(width, part)
+    cross_lse = (top + jnp.log(total)).reshape(all_heads, part)
     cross_branch = contract(cross_t, cross_out_all, 0, 1) + branch_bias[1]
     second_out, second_normed, second_inv = norm_forward(
         first_low.astype(F32) + cross_branch, gains[1], shifts[1]
@@ -697,7 +792,6 @@
     pre_low = jax.vjp(exact_gelu, pre_act)[1](active_grad)[0].astype(BF16)
     mlp_grad = mlp_grads(two, pre_low, mlp_low, active)
     back_part = contract(pre_low, up_all, 1, 1)
-    back_part, mlp_grad = together(back_part, mlp_grad)
     mlp_grad = lax.psum_scatter(mlp_grad, PLANE, scatter_dimension=0, tiled=True)
     back = back_part[:part] + tp_swap(back_part[part:].astype(BF16), 1).astype(F32)
     up_bias_grad = jnp.sum(pre_low.astype(F32), 0).reshape(2, hidden)
@@ -707,19 +801,38 @@
     cross_bias_sum = jnp.sum(second_grad, 0)
     second_grad_low = second_grad.astype(BF16)
     mix_grad = contract(cross_out_all, second_grad_low, 0, 1).astype(BF16)
-    mix_grad = exchange(mix_grad.reshape(all_heads, HEAD, part)).reshape(chunk_shape)
-    mix_grad, hidden_out = together(mix_grad, hidden_out)
+    inner = jnp.sum(
+        mix_grad.reshape(all_heads, HEAD, part).astype(F32)
+        * cross_t.reshape(all_heads, HEAD, part).astype(F32),
+        1,
+    )
+    def spread_rows(values):
+        rows = []
+        for _ in range(3):
+            rows.append(lax.reduce_precision(values, 8, 7))
+            values = values - rows[-1]
+        return [row.astype(BF16) for row in rows]
+
+    stats = jnp.stack([*spread_rows(cross_lse), *spread_rows(inner)], 1).reshape(ranks * cores, -1, part)
+    stats = jnp.pad(stats, ((0, 0), (0, STAT_ROWS - stats.shape[1]), (0, 0)))
+    mix_grad = to_pairs(jnp.concatenate([mix_grad.reshape(ranks * cores, pair_rows, part), stats], 1))
+    mix_grad, hidden_out, proj = together(mix_grad, hidden_out, proj)
     hidden_out = whole_on_ranks(hidden_out)
-    *pair_grads, query_grad = cross_backward(cross_query, cross_mixed, mix_grad, cross_lse, pairs)
+    *pair_grads, query_grad = cross_backward(cross_query, mix_grad, pairs)
     query_grad, hidden_out = together(query_grad, hidden_out)
-    query_grad = exchange(query_grad.reshape(all_heads, HEAD, part)).reshape(width, part)
     pair_grads = [
-        (ctx_swap(g, k) if k else g).reshape(-1, 2 * HEAD) for k, g in enumerate(pair_grads)
+        (ctx_swap(g, k) if k else g).reshape(-1, 2 * pair_rows) for k, g in enumerate(pair_grads)
     ]
-    query_grad, proj = together(query_grad, proj)
-    proj = lax.all_gather(proj, PLANE, axis=0, tiled=True)
-    mlp_grad = mlp_grad.reshape(shard, 2, 2, hidden)
-    mlp_grad = [mlp_grad[:, :, 0], tp_swap(mlp_grad[:, :, 1], 2)]
+    enc_part, value_sum, kv_grad = encoder_back(core_at, enc_rows, kv_weights, pair_grads)
+    query_grad = from_pairs(query_grad)
+    query_grad, enc_part, value_sum, kv_grad, mlp_grad = together(
+        query_grad, enc_part, value_sum, kv_grad, mlp_grad
+    )
+    encoder_grad = lax.psum_scatter(
+        enc_part.reshape(seqs, enc_len, width), "tp", scatter_dimension=2, tiled=True
+    )
+    value_sum = value_sum.reshape(heads_here, 2 * HEAD)[:, HEAD:]
+    query_grad = jnp.sum(query_grad.astype(F32), 1).astype(BF16).reshape(width, part)
     query_sum = jnp.sum(query_grad.astype(F32), 1)
 
     first_grad, gain_zero, shift_zero = norm_backward(
@@ -732,47 +845,31 @@
 
     self_mix_grad = contract(self_out_all, first_grad_low, 0, 1).astype(BF16)
     self_mix_grad = exchange(self_mix_grad.reshape(all_heads, HEAD, part)).reshape(chunk_shape)
-    self_mix_grad, pair_grads = together(self_mix_grad, pair_grads)
-    enc_part, value_sum, kv_grad = encoder_back(ctx_at, enc_rows, kv_weights, pair_grads)
-    value_sum = value_sum.reshape(heads_here, 2 * HEAD)[:, HEAD:]
-    self_mix_grad, enc_part, mlp_grad, kv_grad = together(self_mix_grad, enc_part, mlp_grad, kv_grad)
-    mlp_grad = mlp_grad[0].astype(F32) + mlp_grad[1].astype(F32)
-    up_out, down_out = mlp_grad[:, 0], mlp_grad[:, 1].T
-    encoder_grad = lax.psum_scatter(
-        enc_part.reshape(seqs, enc_len, width), "tp", scatter_dimension=2, tiled=True
-    )
     kv_grad = sum_begin((), [kv_grad])
+    square_grad, kv_grad = sum_near(square_grad, 4), sum_near(kv_grad, 2)
+    self_mix_grad, square_grad, kv_grad = together(self_mix_grad, square_grad, kv_grad)
+    square_grad, kv_grad = sum_far(square_grad), sum_dp(kv_grad)
     stacked, head_grad, head_sum = self_backward(
         ctx_at, x_slots, self_query, self_pair, self_mixed, self_mix_grad, self_lse
     )
-    stacked, head_grad, square_grad, kv_grad = together(stacked, head_grad, square_grad, kv_grad)
-    kv_grad = sum_dp(sum_near(kv_grad, 2))
-    square_grad = sum_near(square_grad, 4)
-    stacked = exchange(stacked.reshape(all_heads, 3 * HEAD, part)).reshape(all_heads, 3, HEAD, part)
-    stacked, head_grad, square_grad, kv_grad = together(stacked, head_grad, square_grad, kv_grad)
-    square_grad, kv_grad = sum_far(square_grad), sum_x(kv_grad)
-    square_grad = sum_end(square_grad)
-    square_grad = square_grad.reshape(shard, 3, ranks, width // ranks)
-
-    stacked = stacked.swapaxes(0, 1).reshape(3, width, part)
-    input_grad = first_grad + (
-        contract(stacked[0], proj[:, :width], 0, 1)
-        + contract(stacked[1], proj[:, width : 2 * width], 0, 1)
-        + contract(stacked[2], proj[:, 2 * width :], 0, 1)
-    )
-    input_grad = input_grad.astype(BF16)
-
-    def for_rank(k):
-        return lax.dynamic_index_in_dim(square_grad, own_tp ^ k, 2, False)
-
-    square_grad = for_rank(0) + sum(
-        tp_swap(for_rank(k).astype(BF16), k).astype(F32) for k in range(1, ranks)
-    )
-    self_out_out, cross_q_out, cross_out_out = (
-        square_grad[:, 0].T,
-        square_grad[:, 1],
-        square_grad[:, 2].T,
-    )
+    stacked, head_grad, square_grad, kv_grad, mlp_grad = together(
+        stacked, head_grad, square_grad, kv_grad, mlp_grad
+    )
+    mlp_grad = mlp_grad.reshape(shard, 2, 2, hidden)
+    mlp_grad = [mlp_grad[:, :, 0], mlp_grad[:, :, 1]]
+    kv_grad = sum_x(kv_grad)
+    stacked = exchange(stacked.reshape(all_heads, 3 * HEAD, part))
+    stacked, head_grad, square_grad, kv_grad, mlp_grad, encoder_grad = together(
+        stacked, head_grad, square_grad, kv_grad, mlp_grad, encoder_grad
+    )
+    mlp_grad = [mlp_grad[0], tp_swap(mlp_grad[1], 2)]
+    if plane != 8:
+        square_grad = [sum_end(square_grad).astype(BF16)[None]]
+    square_grad = rank_split(rank_at, square_grad, 3, ranks)
+    square_grad = [tp_swap(v, k) if k else v for k, v in enumerate(square_grad)]
+    input_grad = input_grads(stacked, proj, first_grad)
+    input_grad = lax.all_gather(input_grad, "tp", axis=0, tiled=True)
+
     head_grad = head_grad.reshape(3 * HEAD, plane, shard).swapaxes(0, 1)
     head_sum = head_sum.reshape(3, HEAD)
     head_sum = jnp.concatenate([head_sum[0], head_sum[2]]).reshape(plane, bias_part, 1)
@@ -807,12 +904,16 @@
     ends = [0, norm_out.size]
     for size in (up_bias.size, up_bias.size, ranks * count, count, rms.size):
         ends.append(ends[-1] + size)
-    sums = jnp.pad(sums, (0, 16 * width - sums.size)).reshape(16, width).astype(BF16)
-
-    last = whole_on_ranks(jnp.concatenate([input_grad, sums]))
-    last, encoder_grad = together(last, encoder_grad)
-    input_grad, encoder_grad = last[:, :part].astype(F32), encoder_grad.astype(F32)
-    sums = last[:, part:].astype(F32).reshape(ranks, -1)
+    sums = jnp.pad(sums, (0, 16 * 256 - sums.size)).reshape(16, 256).astype(BF16)
+
+    sums, square_grad = together(sums, square_grad)
+    mlp_grad = mlp_grad[0].astype(F32) + mlp_grad[1].astype(F32)
+    up_out, down_out = mlp_grad[:, 0], mlp_grad[:, 1].T
+    square_grad = sum(v.astype(F32) for v in square_grad)
+    self_out_out, cross_q_out, cross_out_out = square_grad[0].T, square_grad[1], square_grad[2].T
+    sums, input_grad = together(whole_on_ranks(sums), input_grad)
+    input_grad, encoder_grad = input_grad.astype(F32), encoder_grad.astype(F32)
+    sums = sums.astype(F32).reshape(ranks, -1)
     norm_out, up_own, up_other, query_sums, value_sums, rms = (
         sums[:, i:j] for i, j in zip(ends, ends[1:])
     )

time: 509 us -> 492 us (0.967)
  local copies, waits for them, and re-layouts: 62.3 us -> 48.6 us
  matrix products: 40.6 us -> 31.6 us
  Pallas kernels: 84.2 us -> 92.7 us
  waiting for transfers between devices: 152 us -> 144 us
  blocking collectives: 27.2 us -> 34.6 us
    ppermute x7, waiting for transfers between devices: 13.1 us -> 29.9 us  [plane_swap(): return lax.ppermute(values, PLANE, [(i, i ^ k) for i in range(plane)])]
    all_to_all x0 -> x1, blocking collectives: none -> 12.6 us  [body(): lax.all_to_all(first, PLANE, split_axis=0, concat_axis=0, tiled=True)]
    all_to_all x2, starting transfers between devices: 16.1 us -> 28.2 us  [whole_on_ranks(): return lax.all_to_all(values, 'tp', split_axis=0, concat_axis=0, tiled=True)]
    all_gather x1, waiting for transfers between devices: 10.1 us -> 0.32 us  [body(): square = lax.all_gather(from_ranks(square), PLANE, axis=0, tiled=True)]
    ppermute x16, starting transfers between devices: 32.6 us -> 22.9 us  [tp_swap(): return lax.ppermute(values, 'tp', [(i, i ^ k) for i in range(ranks)])]
    dot_general x13 -> x10, matrix products: 40.6 us -> 31.6 us  [contract(): lax.dot_general(left, right, (((left_dim,), (right_dim,)), ((), ())), pre...]
    pallas_call x16 -> x18, Pallas kernels: 84.2 us -> 92.7 us  [call(): pl.pallas_call(kernel, grid=(seqs,), in_specs=in_specs, out_specs=out_spe...]
    all_to_all x5 -> x6, waiting for transfers between devices: 54 us -> 47.3 us  [exchange(): lax.all_to_all(values, HEADS, split_axis=0, concat_axis=0, tiled=True)]
  transfers between devices with their start and end apart: 47 -> 44, of which waited for: 19 -> 21; matrix products, arithmetic and copies ran while one was open for 15% -> 15% of each run, Pallas kernels for 16% -> 19%
where the time goes in v3:
time: 492 us; the launch traced here: 484 us
  waiting for transfers between devices  144 us (29%)
  starting transfers between devices  94.6 us (19%)
  Pallas kernels  92.7 us (19%)
  local copies, waits for them, and re-layouts  48.6 us (10%)
  blocking collectives  34.6 us (7%)
  matrix products  31.6 us (6%)
  other arithmetic  22.5 us (5%)
  between operations  15.6 us (3%)
    pallas_call x18, Pallas kernels, call(): pl.pallas_call(kernel, grid=(seqs,), in_specs=in_specs, out_specs=out_spe...  92.7 us
    ppermute x16, waiting for transfers between devices, tp_swap(): return lax.ppermute(values, 'tp', [(i, i ^ k) for i in range(ranks)])  57.5 us
    all_to_all x6, waiting for transfers between devices, exchange(): lax.all_to_all(values, HEADS, split_axis=0, concat_axis=0, tiled=True)  47.3 us
    dot_general x10, matrix products, contract(): lax.dot_general(left, right, (((left_dim,), (right_dim,)), ((), ())), pre...  31.6 us
    ppermute x7, waiting for transfers between devices, plane_swap(): return lax.ppermute(values, PLANE, [(i, i ^ k) for i in range(plane)])  29.9 us
    unnamed x157, local copies, waits for them, and re-layouts  29.4 us
    all_to_all x2, starting transfers between devices, whole_on_ranks(): return lax.all_to_all(values, 'tp', split_axis=0, concat_axis=0, tiled=True)  28.2 us
    all_to_all x6, starting transfers between devices, exchange(): lax.all_to_all(values, HEADS, split_axis=0, concat_axis=0, tiled=True)  27.2 us
  transfers between devices with their start and end apart: 44, of which 21 were waited for; matrix products, arithmetic and copies ran while one was open for 15% of the time, Pallas kernels for 19%

profile of v3, /device:TPU:0, one launch (start us, length us, event | category | flops | bytes accessed | tf_op | source)
XLA Modules:
  0.0 484.1 jit_solution(12976072862535171072)
XLA Ops:
  19.4 6.2 %collective-permute-done.refs_1_ = bf16[3,128,256]{2,1,0:T(8,128)(2,1)S(1)} collective-permute-done((bf16[3,128,256]{2,1,0:T(8,128)(2,1)S(1)}, bf16[3,128,256]{2,1,0:T(8,128)(2,1)S(1)}, u32[]{:S(2)}, u32[]{:S(2)}) %collective-permute-start) | collective-permute-done | bytes 196640 | tf_op jit(solution)/shard_map/ppermute | solution.py:607
  25.6 8.1 %collective-permute-done.1.refs_2_ = bf16[3,128,256]{2,1,0:T(8,128)(2,1)S(1)} collective-permute-done((bf16[3,128,256]{2,1,0:T(8,128)(2,1)S(1)}, bf16[3,128,256]{2,1,0:T(8,128)(2,1)S(1)}, u32[]{:S(2)}, u32[]{:S(2)}) %collective-permute-start.1) | collective-permute-done | bytes 196640 | tf_op jit(solution)/shard_map/ppermute | solution.py:607
  33.7 6.9 %collective-permute-done.4.refs_2_ = bf16[2,256,1024]{2,1,0:T(8,128)(2,1)} collective-permute-done((bf16[2,256,1024]{2,1,0:T(8,128)(2,1)}, bf16[2,256,1024]{2,1,0:T(8,128)(2,1)}, u32[]{:S(2)}, u32[]{:S(2)}) %collective-permute-start.4) | collective-permute-done | bytes 1048608 | tf_op jit(solution)/shard_map/ppermute | solution.py:604
  42.3 12.6 %all_to_all.55 = bf16[8,208,128]{2,1,0:T(8,128)(2,1)S(1)} all-to-all(bf16[8,208,128]{2,1,0:T(8,128)(2,1)S(1)} %shard_map.288), channel_id=1, replica_groups=mesh['dp'=2,'ctx'=4,'tp'=4] {'dp','ctx'}, dimensions={0} | all-to-all | bytes 851968 | tf_op jit(solution)/shard_map/all_to_all | solution.py:681
  60.1 5.7 %shard_map.289 = (bf16[2048,256]{1,0:T(8,128)(2,1)S(1)}, bf16[2048,256]{1,0:T(8,128)(2,1)}) custom-call(s32[1]{0:T(128)} %bitcast.2.at_ref, bf16[2048,1024]{1,0:T(8,128)(2,1)} %bitcast.229, bf16[1024,512]{1,0:T(8,128)(2,1)S(1)} %copy-done.2, f32[1,512]{1,0:T(1,128)S(1)} %bitcast.228), custom_call_target="tpu_custom_call" | custom-call | flops 214748368 | bytes 734208 | tf_op jit(solution)/shard_map/pallas_call | solution.py:361
  67.3 8.3 %shard_map.290 = (bf16[2,64,1024]{2,1,0:T(8,128)(2,1)S(1)}, bf16[2,1024,128]{2,1,0:T(8,128)(2,1)S(1)}, bf16[4,4,64,128]{3,2,1,0:T(8,128)(2,1)}, f32[2,1,1024]{2,1,0:T(1,128)S(1)}) custom-call(s32[1]{0:T(128)} %bitcast.at_ref, bf16[2,256,1024]{2,1,0:T(8,128)(2,1)S(1)} %copy-done, bf16[2,256,1024]{2,1,0:T(8,128)(2,1)S(1)} %collective-permute-done.3.refs_1_, ...), custom_call_target="tpu_custom_call" | custom-call | flops 187904816 | bytes 564506 | tf_op jit(solution)/shard_map/pallas_call | solution.py:361
  82.6 8.0 %all-to-all-done.1 = bf16[16,64,128]{2,1,0:T(8,128)(2,1)S(1)} async-done(((bf16[16,64,128]{2,1,0:T(8,128)(2,1)}), bf16[16,64,128]{2,1,0:T(8,128)(2,1)S(1)}, u32[]{:S(2)}, u32[]{:S(2)}) %all-to-all-start.1) | async-done | bytes 262176 | tf_op jit(solution)/shard_map/all_to_all | solution.py:610
  100.8 5.3 %all-to-all-start.2 = ((bf16[16,128,128]{2,1,0:T(8,128)(2,1)}), bf16[16,128,128]{2,1,0:T(8,128)(2,1)S(1)}, u32[]{:S(2)}, u32[]{:S(2)}) async-start(bf16[16,128,128]{2,1,0:T(8,128)(2,1)} %bitcast.27), calls=%async_computation.2 | async-start | bytes 1048576 | tf_op jit(solution)/shard_map/all_to_all | solution.py:610
  111.1 9.8 %all-to-all-done.2 = bf16[16,128,128]{2,1,0:T(8,128)(2,1)S(1)} async-done(((bf16[16,128,128]{2,1,0:T(8,128)(2,1)}), bf16[16,128,128]{2,1,0:T(8,128)(2,1)S(1)}, u32[]{:S(2)}, u32[]{:S(2)}) %all-to-all-start.2) | async-done | bytes 524320 | tf_op jit(solution)/shard_map/all_to_all | solution.py:610
  122.4 14.0 %shard_map.293 = bf16[4,4,144,128]{3,2,1,0:T(8,128)(2,1)S(1)} custom-call(bf16[4,4,128,128]{3,2,1,0:T(8,128)(2,1)S(1)} %fusion.58.q_ref, bf16[2,1024,256]{2,1,0:T(8,128)(2,1)S(1)} %bitcast.217, bf16[2,1024,256]{2,1,0:T(8,128)(2,1)} %bitcast.18.refs_1_), custom_call_target="tpu_custom_call" | custom-call | flops 429496736 | bytes 321126 | tf_op jit(solution)/shard_map/pallas_call | solution.py:361
  137.4 21.9 %all_to_all.56 = bf16[16,144,128]{2,1,0:T(8,128)(2,1)S(1)} all-to-all(bf16[16,144,128]{2,1,0:T(8,128)(2,1)S(1)} %bitcast.215), channel_id=1, replica_groups=mesh['dp'=2,'ctx'=4,'tp'=4] {'tp','ctx'}, dimensions={0} | all-to-all | bytes 1179648 | tf_op jit(solution)/shard_map/all_to_all | solution.py:610
  167.1 4.4 collective-permute-done.12
  174.0 7.6 %multiply_convert_fusion = (bf16[256,2048]{1,0:T(8,128)(2,1)S(1)}, f32[256,2048]{1,0:T(8,128)S(1)}, f32[256,2048]{1,0:T(8,128)S(1)}) fusion(f32[2048]{0:T(1024)S(1)} %maximum_convert_fusion, bf16[1024,4096]{1,0:T(8,128)(2,1)} %all-gather.10.cloned.1.call-done, bf16[128,1024]{1,0:T(8,128)(2,1)} %copy-done.48, bf16[128,1024]{1,0:T(8,128)(2,1)} %copy-done.44), kind=kOutput, calls=%fused_computation.13 | convolution fusion | flops 1109393408 | bytes 9969664 | tf_op jit(solution)/shard_map/dot_general | solution.py:25
  183.7 7.0 %collective-permute-done.13 = bf16[128,1024]{1,0:T(8,128)(2,1)S(1)} collective-permute-done((bf16[128,1024]{1,0:T(8,128)(2,1)S(1)}, bf16[128,1024]{1,0:T(8,128)(2,1)S(1)}, u32[]{:S(2)}, u32[]{:S(2)}) %collective-permute-start.13) | collective-permute-done | bytes 262176 | tf_op jit(solution)/shard_map/ppermute | solution.py:607
  194.7 6.3 %collective-permute-done.14 = bf16[128,1024]{1,0:T(8,128)(2,1)S(1)} collective-permute-done((bf16[128,1024]{1,0:T(8,128)(2,1)S(1)}, bf16[128,1024]{1,0:T(8,128)(2,1)S(1)}, u32[]{:S(2)}, u32[]{:S(2)}) %collective-permute-start.14) | collective-permute-done | bytes 262176 | tf_op jit(solution)/shard_map/ppermute | solution.py:607
  202.9 5.1 %shard_map.297 = bf16[1024,4096]{1,0:T(8,128)(2,1)} custom-call(bf16[256,1024]{1,0:T(8,128)(2,1)S(1)} %pad_maximum_fusion.1.two_ref, bf16[256,2048]{1,0:T(8,128)(2,1)S(1)} %get-tuple-element.396.pre_ref, bf16[256,1024]{1,0:T(8,128)(2,1)S(1)} %pad_maximum_fusion.2.low_ref, bf16[256,2048]{1,0:T(8,128)(2,1)S(1)} %get-tuple-element.349.active_ref), custom_call_target="tpu_custom_call" | custom-call | flops 214748368 | bytes 1153433 | tf_op jit(solution)/shard_map/pallas_call | solution.py:361
  214.1 6.1 %collective-permute-done.15 = bf16[128,1024]{1,0:T(8,128)(2,1)S(1)} collective-permute-done((bf16[128,1024]{1,0:T(8,128)(2,1)S(1)}, bf16[128,1024]{1,0:T(8,128)(2,1)S(1)}, u32[]{:S(2)}, u32[]{:S(2)}) %collective-permute-start.15) | collective-permute-done | bytes 262176 | tf_op jit(solution)/shard_map/ppermute | solution.py:607
  229.2 15.5 %all-to-all-done.4 = bf16[16,144,128]{2,1,0:T(8,128)(2,1)S(1)} async-done(((bf16[16,144,128]{2,1,0:T(8,128)(2,1)}), bf16[16,144,128]{2,1,0:T(8,128)(2,1)S(1)}, u32[]{:S(2)}, u32[]{:S(2)}) %all-to-all-start.4) | async-done | bytes 589856 | tf_op jit(solution)/shard_map/all_to_all | solution.py:610
  251.2 22.3 %shard_map.295 = (bf16[2,1024,256]{2,1,0:T(8,128)(2,1)S(1)}, bf16[2,1024,256]{2,1,0:T(8,128)(2,1)}, bf16[4,4,128,128]{3,2,1,0:T(8,128)(2,1)}) custom-call(bf16[4,4,128,128]{3,2,1,0:T(8,128)(2,1)S(1)} %fusion.58.q_ref, bf16[4,4,144,128]{3,2,1,0:T(8,128)(2,1)S(1)} %bitcast.227, bf16[2,1024,256]{2,1,0:T(8,128)(2,1)} %bitcast.216, ...), custom_call_target="tpu_custom_call" | custom-call | flops 1073741824 | bytes 583270 | tf_op jit(solution)/shard_map/pallas_call | solution.py:361
  276.3 4.3 all-to-all-start.6
  283.2 8.8 %shard_map.296 = (bf16[2048,1024]{1,0:T(8,128)(2,1)}, f32[1,512]{1,0:T(1,128)S(1)}, bf16[1024,512]{1,0:T(8,128)(2,1)S(1)}) custom-call(s32[1]{0:T(128)} %bitcast.2.at_ref, bf16[2048,1024]{1,0:T(8,128)(2,1)} %bitcast.230, bf16[1024,512]{1,0:T(8,128)(2,1)S(1)} %copy-done.3, bf16[2048,256]{1,0:T(8,128)(2,1)S(1)} %bitcast.226, bf16[2048,256]{1,0:T(8,128)(2,1)} %bitcast.242), custom_call_target="tpu_custom_call" | custom-call | flops 429496736 | bytes 1258496 | tf_op jit(solution)/shard_map/pallas_call | solution.py:361
  309.7 4.3 all-to-all-start.7
  317.6 5.9 %shard_map.299 = (bf16[1,128,3072]{2,1,0:T(8,128)(2,1)S(1)}, bf16[1,128,3072]{2,1,0:T(8,128)(2,1)}, bf16[1,128,3072]{2,1,0:T(8,128)(2,1)}, bf16[1,128,3072]{2,1,0:T(8,128)(2,1)}) custom-call(bf16[4,128,3072]{2,1,0:T(8,128)(2,1)} %get-tuple-element.166.keep_ref, bf16[4,128,3072]{2,1,0:T(8,128)(2,1)} %collective-permute-done.17.got_ref), custom_call_target="tpu_custom_call" | custom-call | flops 157286 | bytes 943718 | tf_op jit(solution)/shard_map/pallas_call | solution.py:361
  323.6 5.1 %all-to-all-done.7 = bf16[16,64,128]{2,1,0:T(8,128)(2,1)S(1)} async-done(((bf16[16,64,128]{2,1,0:T(8,128)(2,1)}), bf16[16,64,128]{2,1,0:T(8,128)(2,1)S(1)}, u32[]{:S(2)}, u32[]{:S(2)}) %all-to-all-start.7) | async-done | bytes 262176 | tf_op jit(solution)/shard_map/all_to_all | solution.py:610
  335.7 7.8 %shard_map.302 = (bf16[4,4,192,128]{3,2,1,0:T(8,128)(2,1)}, f32[192,1024]{1,0:T(8,128)S(1)}, f32[192,1]{1,0:T(8,128)S(1)}) custom-call(s32[1]{0:T(128)} %bitcast.at_ref, bf16[2,256,1024]{2,1,0:T(8,128)(2,1)S(1)} %copy-done, bf16[2,256,1024]{2,1,0:T(8,128)(2,1)} %copy-done.1, bf16[2,256,1024]{2,1,0:T(8,128)(2,1)} %collective-permute-done.4.refs_2_, ...), custom_call_target="tpu_custom_call" | custom-call | flops 348966080 | bytes 708685 | tf_op jit(solution)/shard_map/pallas_call | solution.py:361
  343.5 28.4 %collective-permute-done.22 = bf16[2,128,512]{2,1,0:T(8,128)(2,1)} collective-permute-done((bf16[2,128,512]{2,1,0:T(8,128)(2,1)}, bf16[2,128,512]{2,1,0:T(8,128)(2,1)}, u32[]{:S(2)}, u32[]{:S(2)}) %collective-permute-start.22) | collective-permute-done | bytes 262176 | tf_op jit(solution)/shard_map/ppermute | solution.py:625
  372.0 6.0 %all-to-all-start.8 = ((bf16[16,192,128]{2,1,0:T(8,128)(2,1)}), bf16[16,192,128]{2,1,0:T(8,128)(2,1)S(1)}, u32[]{:S(2)}, u32[]{:S(2)}) async-start(bf16[16,192,128]{2,1,0:T(8,128)(2,1)} %bitcast.59), calls=%async_computation.9 | async-start | bytes 1572864 | tf_op jit(solution)/shard_map/all_to_all | solution.py:610
  390.9 5.8 %all-to-all-done.8.stacked_ref = bf16[16,192,128]{2,1,0:T(8,128)(2,1)S(1)} async-done(((bf16[16,192,128]{2,1,0:T(8,128)(2,1)}), bf16[16,192,128]{2,1,0:T(8,128)(2,1)S(1)}, u32[]{:S(2)}, u32[]{:S(2)}) %all-to-all-start.8) | async-done | bytes 786464 | tf_op jit(solution)/shard_map/all_to_all | solution.py:610
  409.3 5.8 %shard_map.304 = bf16[128,1024]{1,0:T(8,128)(2,1)} custom-call(bf16[16,192,128]{2,1,0:T(8,128)(2,1)S(1)} %all-to-all-done.8.stacked_ref, bf16[1024,3072]{1,0:T(8,128)(2,1)} %all-gather.12.cloned.1.call-done.proj_ref, f32[128,1024]{1,0:T(8,128)S(1)} %get-tuple-element.341.first_ref), custom_call_target="tpu_custom_call" | custom-call | flops 80530640 | bytes 786432 | tf_op jit(solution)/shard_map/pallas_call | solution.py:361
  421.1 11.4 %collective-permute-done.25 = bf16[3,128,256]{2,1,0:T(8,128)(2,1)} collective-permute-done((bf16[3,128,256]{2,1,0:T(8,128)(2,1)S(1)}, bf16[3,128,256]{2,1,0:T(8,128)(2,1)}, u32[]{:S(2)}, u32[]{:S(2)}) %collective-permute-start.25) | collective-permute-done | bytes 196640 | tf_op jit(solution)/shard_map/ppermute | solution.py:607
  433.1 24.0 %all-to-all-start.10 = ((bf16[4,16,256]{2,1,0:T(8,128)(2,1)}), bf16[4,16,256]{2,1,0:T(8,128)(2,1)S(1)}, u32[]{:S(2)}, u32[]{:S(2)}) async-start(bf16[4,16,256]{2,1,0:T(8,128)(2,1)} %broadcast_in_dim.23), calls=%async_computation.12 | async-start | bytes 65536 | tf_op jit(solution)/shard_map/all_to_all | solution.py:655
  462.1 4.9 %collective-permute-done.27 = bf16[128,2,1024]{2,0,1:T(8,128)(2,1)S(1)} collective-permute-done((bf16[128,2,1024]{2,0,1:T(8,128)(2,1)}, bf16[128,2,1024]{2,0,1:T(8,128)(2,1)S(1)}, u32[]{:S(2)}, u32[]{:S(2)}) %collective-permute-start.27) | collective-permute-done | bytes 524320 | tf_op jit(solution)/shard_map/ppermute | solution.py:607
  (407 shorter events, 164.9 us)
Async XLA Ops:
  7.3 51.6 %all-gather.6.cloned.1.call-start = ((), (), s32[]{:S(2)}) async-start(), calls=%async_computation.13 | async-start | bytes 1179648 | tf_op jit(solution)/shard_map/all_gather | solution.py:683
  9.2 81.8 %all-gather.8.cloned.1.call-start = ((), (), s32[]{:S(2)}) async-start(), calls=%async_computation.14 | async-start | bytes 7077888 | tf_op jit(solution)/shard_map/all_gather | solution.py:691
  9.2 24.5 %collective-permute-start.3 = (bf16[2,256,1024]{2,1,0:T(8,128)(2,1)}, bf16[2,256,1024]{2,1,0:T(8,128)(2,1)S(1)}, u32[]{:S(2)}, u32[]{:S(2)}) collective-permute-start(bf16[2,256,1024]{2,1,0:T(8,128)(2,1)} %refs_0_.2), channel_id=1, source_target_pairs={{0,4},{4,0},{8,12},{12,8},{1,5},{5,1},{9,13},{13,9},{2,6},{6,2},{1... | collective-permute-start | bytes 3145736 | tf_op jit(solution)/shard_map/ppermute | solution.py:604
  9.8 30.8 %collective-permute-start.4 = (bf16[2,256,1024]{2,1,0:T(8,128)(2,1)}, bf16[2,256,1024]{2,1,0:T(8,128)(2,1)}, u32[]{:S(2)}, u32[]{:S(2)}) collective-permute-start(bf16[2,256,1024]{2,1,0:T(8,128)(2,1)} %refs_0_.2), channel_id=1, source_target_pairs={{0,8},{4,12},{8,0},{12,4},{1,9},{5,13},{9,1},{13,5},{2,10},{6,14},... | collective-permute-start | bytes 3145736 | tf_op jit(solution)/shard_map/ppermute | solution.py:604
  16.6 17.1 %collective-permute-start.1 = (bf16[3,128,256]{2,1,0:T(8,128)(2,1)S(1)}, bf16[3,128,256]{2,1,0:T(8,128)(2,1)S(1)}, u32[]{:S(2)}, u32[]{:S(2)}) collective-permute-start(bf16[3,128,256]{2,1,0:T(8,128)(2,1)S(1)} %shard_map.287.refs_0_), channel_id=1, source_target_pairs={{0,2},{1,3},{2,0},{3,1},{4,6},{5,7},{6,4},{7,5},{8,10},{9,11},{10,... | collective-permute-start | bytes 589832 | tf_op jit(solution)/shard_map/ppermute | solution.py:607
  19.2 14.5 %collective-permute-start.2 = (bf16[3,128,256]{2,1,0:T(8,128)(2,1)S(1)}, bf16[3,128,256]{2,1,0:T(8,128)(2,1)S(1)}, u32[]{:S(2)}, u32[]{:S(2)}) collective-permute-start(bf16[3,128,256]{2,1,0:T(8,128)(2,1)S(1)} %shard_map.287.refs_0_), channel_id=1, source_target_pairs={{0,3},{1,2},{2,1},{3,0},{4,7},{5,6},{6,5},{7,4},{8,11},{9,10},{10,... | collective-permute-start | bytes 589832 | tf_op jit(solution)/shard_map/ppermute | solution.py:607
  55.5 27.1 %collective-permute-start.6 = (bf16[128,2048]{1,0:T(8,128)(2,1)S(1)}, bf16[128,2048]{1,0:T(8,128)(2,1)}, u32[]{:S(2)}, u32[]{:S(2)}) collective-permute-start(bf16[128,2048]{1,0:T(8,128)(2,1)S(1)} %shard_map.292), channel_id=1, source_target_pairs={{0,2},{1,3},{2,0},{3,1},{4,6},{5,7},{6,4},{7,5},{8,10},{9,11},{10,... | collective-permute-start | bytes 1572872 | tf_op jit(solution)/shard_map/ppermute | solution.py:607
  66.8 23.9 %collective-permute-start.7 = (bf16[2048,256]{1,0:T(8,128)(2,1)}, bf16[2048,256]{1,0:T(8,128)(2,1)}, u32[]{:S(2)}, u32[]{:S(2)}) collective-permute-start(bf16[2048,256]{1,0:T(8,128)(2,1)} %get-tuple-element.140), channel_id=1, source_target_pairs={{0,4},{4,0},{8,12},{12,8},{1,5},{5,1},{9,13},{13,9},{2,6},{6,2},{1... | collective-permute-start | bytes 3145736 | tf_op jit(solution)/shard_map/ppermute | solution.py:604
  80.7 93.4 %all-gather.10.cloned.1.call-start = ((), (), s32[]{:S(2)}) async-start(), calls=%async_computation.15 | async-start | bytes 9437184 | tf_op jit(solution)/shard_map/all_gather | solution.py:743
  100.8 20.1 %all-to-all-start.2 = ((bf16[16,128,128]{2,1,0:T(8,128)(2,1)}), bf16[16,128,128]{2,1,0:T(8,128)(2,1)S(1)}, u32[]{:S(2)}, u32[]{:S(2)}) async-start(bf16[16,128,128]{2,1,0:T(8,128)(2,1)} %bitcast.27), calls=%async_computation.2 | async-start | bytes 1048576 | tf_op jit(solution)/shard_map/all_to_all | solution.py:610
  106.0 123.1 %all-gather.12.cloned.1.call-start = ((), (), s32[]{:S(2)}) async-start(), calls=%async_computation.16 | async-start | bytes 7077888 | tf_op jit(solution)/shard_map/all_gather | solution.py:757
  106.7 29.6 %collective-permute-start.8 = (bf16[3,128,256]{2,1,0:T(8,128)(2,1)S(1)}, bf16[3,128,256]{2,1,0:T(8,128)(2,1)S(1)}, u32[]{:S(2)}, u32[]{:S(2)}) collective-permute-start(bf16[3,128,256]{2,1,0:T(8,128)(2,1)S(1)} %copy-done.17), channel_id=1, source_target_pairs={{0,1},{1,0},{2,3},{3,2},{4,5},{5,4},{6,7},{7,6},{8,9},{9,8},{10,11... | collective-permute-start | bytes 589832 | tf_op jit(solution)/shard_map/ppermute | solution.py:607
  108.6 27.7 %collective-permute-start.9 = (bf16[3,128,256]{2,1,0:T(8,128)(2,1)S(1)}, bf16[3,128,256]{2,1,0:T(8,128)(2,1)S(1)}, u32[]{:S(2)}, u32[]{:S(2)}) collective-permute-start(bf16[3,128,256]{2,1,0:T(8,128)(2,1)S(1)} %copy-done.17), channel_id=1, source_target_pairs={{0,2},{1,3},{2,0},{3,1},{4,6},{5,7},{6,4},{7,5},{8,10},{9,11},{10,... | collective-permute-start | bytes 589832 | tf_op jit(solution)/shard_map/ppermute | solution.py:607
  111.0 25.3 %collective-permute-start.10 = (bf16[3,128,256]{2,1,0:T(8,128)(2,1)S(1)}, bf16[3,128,256]{2,1,0:T(8,128)(2,1)S(1)}, u32[]{:S(2)}, u32[]{:S(2)}) collective-permute-start(bf16[3,128,256]{2,1,0:T(8,128)(2,1)S(1)} %copy-done.17), channel_id=1, source_target_pairs={{0,3},{1,2},{2,1},{3,0},{4,7},{5,6},{6,5},{7,4},{8,11},{9,10},{10,... | collective-permute-start | bytes 589832 | tf_op jit(solution)/shard_map/ppermute | solution.py:607
  137.4 157.7 %reduce-scatter.3.cloned.1.call-start = ((), (), s32[]{:S(2)}) async-start(), calls=%async_computation.17 | async-start | bytes 9437184 | tf_op jit(solution)/shard_map/reduce_scatter | solution.py:795
  225.3 19.3 %all-to-all-start.4 = ((bf16[16,144,128]{2,1,0:T(8,128)(2,1)}), bf16[16,144,128]{2,1,0:T(8,128)(2,1)S(1)}, u32[]{:S(2)}, u32[]{:S(2)}) async-start(bf16[16,144,128]{2,1,0:T(8,128)(2,1)} %bitcast.232), calls=%async_computation.4 | async-start | bytes 1179648 | tf_op jit(solution)/shard_map/all_to_all | solution.py:610
  245.9 30.5 %all-to-all-start.5 = ((bf16[4,128,1024]{2,1,0:T(8,128)(2,1)}), bf16[4,128,1024]{2,1,0:T(8,128)(2,1)}, u32[]{:S(2)}, u32[]{:S(2)}) async-start(bf16[4,128,1024]{2,1,0:T(8,128)(2,1)} %broadcast_in_dim.20), calls=%async_computation.5 | async-start | bytes 2097152 | tf_op jit(solution)/shard_map/all_to_all | solution.py:655
  276.3 18.7 %all-to-all-start.6 = ((bf16[16,128,128]{2,1,0:T(8,128)(2,1)}), bf16[16,128,128]{2,1,0:T(8,128)(2,1)}, u32[]{:S(2)}, u32[]{:S(2)}) async-start(bf16[16,128,128]{2,1,0:T(8,128)(2,1)} %bitcast.51), calls=%async_computation.6 | async-start | bytes 1048576 | tf_op jit(solution)/shard_map/all_to_all | solution.py:610
  280.6 116.2 %reduce-scatter.5.cloned.1.call-start = ((), (), s32[]{:S(2)}) async-start(), calls=%async_computation.18 | async-start | bytes 5242880 | tf_op jit(solution)/shard_map/reduce_scatter | solution.py:831
  309.7 18.9 %all-to-all-start.7 = ((bf16[16,64,128]{2,1,0:T(8,128)(2,1)}), bf16[16,64,128]{2,1,0:T(8,128)(2,1)S(1)}, u32[]{:S(2)}, u32[]{:S(2)}) async-start(bf16[16,64,128]{2,1,0:T(8,128)(2,1)} %bitcast.56), calls=%async_computation.8 | async-start | bytes 524288 | tf_op jit(solution)/shard_map/all_to_all | solution.py:610
  328.6 43.3 %collective-permute-start.19 = (bf16[1,128,3072]{2,1,0:T(8,128)(2,1)}, bf16[1,128,3072]{2,1,0:T(8,128)(2,1)}, u32[]{:S(2)}, u32[]{:S(2)}) collective-permute-start(bf16[1,128,3072]{2,1,0:T(8,128)(2,1)} %get-tuple-element.182), channel_id=1, source_target_pairs={{0,8},{4,12},{8,0},{12,4},{16,24},{20,28},{24,16},{28,20},{1,9},{5... | collective-permute-start | bytes 2359304 | tf_op jit(solution)/shard_map/ppermute | solution.py:625
  329.1 42.8 %collective-permute-start.20 = (bf16[1,128,3072]{2,1,0:T(8,128)(2,1)}, bf16[1,128,3072]{2,1,0:T(8,128)(2,1)}, u32[]{:S(2)}, u32[]{:S(2)}) collective-permute-start(bf16[1,128,3072]{2,1,0:T(8,128)(2,1)} %get-tuple-element.183), channel_id=1, source_target_pairs={{0,16},{4,20},{8,24},{12,28},{16,0},{20,4},{24,8},{28,12},{1,17},{... | collective-permute-start | bytes 2359304 | tf_op jit(solution)/shard_map/ppermute | solution.py:625
  330.6 41.4 %collective-permute-start.21 = (bf16[1,128,3072]{2,1,0:T(8,128)(2,1)}, bf16[1,128,3072]{2,1,0:T(8,128)(2,1)}, u32[]{:S(2)}, u32[]{:S(2)}) collective-permute-start(bf16[1,128,3072]{2,1,0:T(8,128)(2,1)} %get-tuple-element.184), channel_id=1, source_target_pairs={{0,24},{4,28},{8,16},{12,20},{16,8},{20,12},{24,0},{28,4},{1,25},{... | collective-permute-start | bytes 2359304 | tf_op jit(solution)/shard_map/ppermute | solution.py:625
  332.2 39.8 %collective-permute-start.22 = (bf16[2,128,512]{2,1,0:T(8,128)(2,1)}, bf16[2,128,512]{2,1,0:T(8,128)(2,1)}, u32[]{:S(2)}, u32[]{:S(2)}) collective-permute-start(bf16[2,128,512]{2,1,0:T(8,128)(2,1)} %get-tuple-element.186), channel_id=1, source_target_pairs={{0,16},{4,20},{8,24},{12,28},{16,0},{20,4},{24,8},{28,12},{1,17},{... | collective-permute-start | bytes 786440 | tf_op jit(solution)/shard_map/ppermute | solution.py:625
  372.0 24.8 %all-to-all-start.8 = ((bf16[16,192,128]{2,1,0:T(8,128)(2,1)}), bf16[16,192,128]{2,1,0:T(8,128)(2,1)S(1)}, u32[]{:S(2)}, u32[]{:S(2)}) async-start(bf16[16,192,128]{2,1,0:T(8,128)(2,1)} %bitcast.59), calls=%async_computation.9 | async-start | bytes 1572864 | tf_op jit(solution)/shard_map/all_to_all | solution.py:610
  397.7 22.0 %all-to-all-start.9 = ((bf16[8,224,128]{2,1,0:T(8,128)(2,1)}), bf16[8,224,128]{2,1,0:T(8,128)(2,1)}, u32[]{:S(2)}, u32[]{:S(2)}) async-start(bf16[8,224,128]{2,1,0:T(8,128)(2,1)} %pad_maximum_fusion.3), calls=%async_computation.11 | async-start | bytes 917504 | tf_op jit(solution)/shard_map/all_to_all | solution.py:893
  401.8 67.3 %all-gather.14.cloned.1.call-start = ((), (), s32[]{:S(2)}) async-start(), calls=%async_computation.19 | async-start | bytes 1310720 | tf_op jit(solution)/shard_map/all_gather | solution.py:871
  404.1 16.9 %collective-permute-start.24 = (bf16[3,128,256]{2,1,0:T(8,128)(2,1)S(1)}, bf16[3,128,256]{2,1,0:T(8,128)(2,1)}, u32[]{:S(2)}, u32[]{:S(2)}) collective-permute-start(bf16[3,128,256]{2,1,0:T(8,128)(2,1)S(1)} %get-tuple-element.206), channel_id=1, source_target_pairs={{0,1},{1,0},{2,3},{3,2},{4,5},{5,4},{6,7},{7,6},{8,9},{9,8},{10,11... | collective-permute-start | bytes 589832 | tf_op jit(solution)/shard_map/ppermute | solution.py:607
  406.3 26.1 %collective-permute-start.25 = (bf16[3,128,256]{2,1,0:T(8,128)(2,1)S(1)}, bf16[3,128,256]{2,1,0:T(8,128)(2,1)}, u32[]{:S(2)}, u32[]{:S(2)}) collective-permute-start(bf16[3,128,256]{2,1,0:T(8,128)(2,1)S(1)} %get-tuple-element.207), channel_id=1, source_target_pairs={{0,2},{1,3},{2,0},{3,1},{4,6},{5,7},{6,4},{7,5},{8,10},{9,11},{10,... | collective-permute-start | bytes 589832 | tf_op jit(solution)/shard_map/ppermute | solution.py:607
  407.9 24.5 %collective-permute-start.26 = (bf16[3,128,256]{2,1,0:T(8,128)(2,1)S(1)}, bf16[3,128,256]{2,1,0:T(8,128)(2,1)}, u32[]{:S(2)}, u32[]{:S(2)}) collective-permute-start(bf16[3,128,256]{2,1,0:T(8,128)(2,1)S(1)} %get-tuple-element.208), channel_id=1, source_target_pairs={{0,3},{1,2},{2,1},{3,0},{4,7},{5,6},{6,5},{7,4},{8,11},{9,10},{10,... | collective-permute-start | bytes 589832 | tf_op jit(solution)/shard_map/ppermute | solution.py:607
  417.7 49.3 %collective-permute-start.27 = (bf16[128,2,1024]{2,0,1:T(8,128)(2,1)}, bf16[128,2,1024]{2,0,1:T(8,128)(2,1)S(1)}, u32[]{:S(2)}, u32[]{:S(2)}) collective-permute-start(bf16[128,2,1024]{2,0,1:T(8,128)(2,1)} %bitcast.209), channel_id=1, source_target_pairs={{0,2},{1,3},{2,0},{3,1},{4,6},{5,7},{6,4},{7,5},{8,10},{9,11},{10,... | collective-permute-start | bytes 1572872 | tf_op jit(solution)/shard_map/ppermute | solution.py:607
  433.1 36.0 %all-to-all-start.10 = ((bf16[4,16,256]{2,1,0:T(8,128)(2,1)}), bf16[4,16,256]{2,1,0:T(8,128)(2,1)S(1)}, u32[]{:S(2)}, u32[]{:S(2)}) async-start(bf16[4,16,256]{2,1,0:T(8,128)(2,1)} %broadcast_in_dim.23), calls=%async_computation.12 | async-start | bytes 65536 | tf_op jit(solution)/shard_map/all_to_all | solution.py:655
  (79 other events, 824.3 us)
Sparse Core Ops, SparseCore 0:
  10.6 30.5 all-gather.5
  43.0 47.9 all-gather.7
  93.5 65.8 all-gather.9
  161.1 45.6 all-gather.11
  210.1 73.5 reduce-scatter.2
  295.2 80.2 reduce-scatter.4
  415.3 44.8 all-gather.13

commit v4 on v3

--- a/solution.py
+++ b/solution.py
@@ -136,13 +136,13 @@
 def spread(values):
     rows = []
     for _ in range(3):
-        rows.append(values.astype(BF16))
-        values = values - rows[-1].astype(F32)
+        rows.append(values.astype(BF16).astype(F32))
+        values = values - rows[-1]
     return rows
 
 
 def gathered(rows, at):
-    return sum(rows[at + i : at + i + 1].astype(F32) for i in range(3))
+    return sum(rows[at + i : at + i + 1] for i in range(3))
 
 
 def cross_forward_kernel(q_ref, *refs):
@@ -173,8 +173,8 @@
                 top = new_top
         outs.append((mixed[HEAD:] / total).astype(BF16))
         stats += spread(top + jnp.log(total))
-    spare = jnp.zeros((STAT_ROWS - len(stats), stats[0].shape[1]), BF16)
-    out = jnp.concatenate([*outs, *stats, spare], 0)
+    spare = jnp.zeros((STAT_ROWS - len(stats), stats[0].shape[1]), F32)
+    out = jnp.concatenate([*outs, jnp.concatenate([*stats, spare], 0).astype(BF16)], 0)
     for h in range(halves):
         for b in range(blocks):
             at = (h * blocks + b) * part
@@ -188,12 +188,13 @@
     width = halves * blocks * part
     queries, grads = gather_chunks(q_ref), gather_chunks(do_ref)
     heads = features // HEAD
+    stats = grads[features:].astype(F32)
     outs = []
     for n in range(heads):
         query = with_zeros_below(queries[n * HEAD : (n + 1) * HEAD])
         grad = with_zeros_above(grads[n * HEAD : (n + 1) * HEAD])
-        lse = gathered(grads, features + 6 * n)
-        inner = gathered(grads, features + 6 * n + 3)
+        lse = gathered(stats, 6 * n)
+        inner = gathered(stats, 6 * n + 3)
         lanes = slice(n * 2 * HEAD, (n + 1) * 2 * HEAD)
         both = jnp.concatenate([query, grad], 1)
         query_grad = None
@@ -848,21 +849,21 @@
     kv_grad = sum_begin((), [kv_grad])
     square_grad, kv_grad = sum_near(square_grad, 4), sum_near(kv_grad, 2)
     self_mix_grad, square_grad, kv_grad = together(self_mix_grad, square_grad, kv_grad)
-    square_grad, kv_grad = sum_far(square_grad), sum_dp(kv_grad)
+    kv_grad = sum_dp(kv_grad)
     stacked, head_grad, head_sum = self_backward(
         ctx_at, x_slots, self_query, self_pair, self_mixed, self_mix_grad, self_lse
     )
+    mlp_grad = mlp_grad.reshape(shard, 2, 2, hidden)
+    mlp_grad = [mlp_grad[:, :, 0], mlp_grad[:, :, 1]]
     stacked, head_grad, square_grad, kv_grad, mlp_grad = together(
         stacked, head_grad, square_grad, kv_grad, mlp_grad
     )
-    mlp_grad = mlp_grad.reshape(shard, 2, 2, hidden)
-    mlp_grad = [mlp_grad[:, :, 0], mlp_grad[:, :, 1]]
-    kv_grad = sum_x(kv_grad)
+    square_grad, kv_grad = sum_far(square_grad), sum_x(kv_grad)
     stacked = exchange(stacked.reshape(all_heads, 3 * HEAD, part))
+    mlp_grad = [mlp_grad[0], tp_swap(mlp_grad[1], 2)]
     stacked, head_grad, square_grad, kv_grad, mlp_grad, encoder_grad = together(
         stacked, head_grad, square_grad, kv_grad, mlp_grad, encoder_grad
     )
-    mlp_grad = [mlp_grad[0], tp_swap(mlp_grad[1], 2)]
     if plane != 8:
         square_grad = [sum_end(square_grad).astype(BF16)[None]]
     square_grad = rank_split(rank_at, square_grad, 3, ranks)

time: 492 us -> 485 us (0.986)
  starting transfers between devices: 94.6 us -> 76.3 us
  waiting for transfers between devices: 144 us -> 149 us
    all_to_all x2, starting transfers between devices: 28.2 us -> 10.4 us  [whole_on_ranks(): return lax.all_to_all(values, 'tp', split_axis=0, concat_axis=0, tiled=True)]
    all_to_all x6, waiting for transfers between devices: 47.3 us -> 36.4 us  [exchange(): lax.all_to_all(values, HEADS, split_axis=0, concat_axis=0, tiled=True)]
    all_gather x1, waiting for transfers between devices: 0.01 us -> 9.03 us  [body(): input_grad = lax.all_gather(input_grad, 'tp', axis=0, tiled=True)]
    ppermute x7, waiting for transfers between devices: 29.9 us -> 36.7 us  [plane_swap(): return lax.ppermute(values, PLANE, [(i, i ^ k) for i in range(plane)])]
    unnamed x157 -> x169, local copies, waits for them, and re-layouts: 29.4 us -> 34.9 us
  transfers between devices with their start and end apart: 44 -> 44, of which waited for: 21 -> 19; matrix products, arithmetic and copies ran while one was open for 15% -> 15% of each run, Pallas kernels for 19% -> 19%
where the time goes in v4:
time: 485 us; the launch traced here: 476 us
  waiting for transfers between devices  149 us (31%)
  Pallas kernels  92.1 us (19%)
  starting transfers between devices  76.3 us (16%)
  local copies, waits for them, and re-layouts  53 us (11%)
  blocking collectives  34.6 us (7%)
  matrix products  31.7 us (7%)
  other arithmetic  24 us (5%)
  between operations  15.7 us (3%)
    pallas_call x18, Pallas kernels, call(): pl.pallas_call(kernel, grid=(seqs,), in_specs=in_specs, out_specs=out_spe...  92.1 us
    ppermute x16, waiting for transfers between devices, tp_swap(): return lax.ppermute(values, 'tp', [(i, i ^ k) for i in range(ranks)])  57 us
    ppermute x7, waiting for transfers between devices, plane_swap(): return lax.ppermute(values, PLANE, [(i, i ^ k) for i in range(plane)])  36.7 us
    all_to_all x6, waiting for transfers between devices, exchange(): lax.all_to_all(values, HEADS, split_axis=0, concat_axis=0, tiled=True)  36.4 us
    unnamed x169, local copies, waits for them, and re-layouts  34.9 us
    dot_general x10, matrix products, contract(): lax.dot_general(left, right, (((left_dim,), (right_dim,)), ((), ())), pre...  31.7 us
    all_to_all x6, starting transfers between devices, exchange(): lax.all_to_all(values, HEADS, split_axis=0, concat_axis=0, tiled=True)  27.2 us
    ppermute x16, starting transfers between devices, tp_swap(): return lax.ppermute(values, 'tp', [(i, i ^ k) for i in range(ranks)])  23 us
  transfers between devices with their start and end apart: 44, of which 19 were waited for; matrix products, arithmetic and copies ran while one was open for 15% of the time, Pallas kernels for 19%

profile of v4, /device:TPU:0, one launch (start us, length us, event | category | flops | bytes accessed | tf_op | source)
XLA Modules:
  0.0 476.3 jit_solution(18000023816915109224)
XLA Ops:
  19.4 6.2 %collective-permute-done.refs_1_ = bf16[3,128,256]{2,1,0:T(8,128)(2,1)S(1)} collective-permute-done((bf16[3,128,256]{2,1,0:T(8,128)(2,1)S(1)}, bf16[3,128,256]{2,1,0:T(8,128)(2,1)S(1)}, u32[]{:S(2)}, u32[]{:S(2)}) %collective-permute-start) | collective-permute-done | bytes 196640 | tf_op jit(solution)/shard_map/ppermute | solution.py:608
  25.6 8.1 %collective-permute-done.1.refs_2_ = bf16[3,128,256]{2,1,0:T(8,128)(2,1)S(1)} collective-permute-done((bf16[3,128,256]{2,1,0:T(8,128)(2,1)S(1)}, bf16[3,128,256]{2,1,0:T(8,128)(2,1)S(1)}, u32[]{:S(2)}, u32[]{:S(2)}) %collective-permute-start.1) | collective-permute-done | bytes 196640 | tf_op jit(solution)/shard_map/ppermute | solution.py:608
  33.7 6.9 %collective-permute-done.4.refs_2_ = bf16[2,256,1024]{2,1,0:T(8,128)(2,1)} collective-permute-done((bf16[2,256,1024]{2,1,0:T(8,128)(2,1)}, bf16[2,256,1024]{2,1,0:T(8,128)(2,1)}, u32[]{:S(2)}, u32[]{:S(2)}) %collective-permute-start.4) | collective-permute-done | bytes 1048608 | tf_op jit(solution)/shard_map/ppermute | solution.py:605
  42.3 12.6 %all_to_all.55 = bf16[8,208,128]{2,1,0:T(8,128)(2,1)S(1)} all-to-all(bf16[8,208,128]{2,1,0:T(8,128)(2,1)S(1)} %shard_map.288), channel_id=1, replica_groups=mesh['dp'=2,'ctx'=4,'tp'=4] {'dp','ctx'}, dimensions={0} | all-to-all | bytes 851968 | tf_op jit(solution)/shard_map/all_to_all | solution.py:682
  60.1 5.7 %shard_map.289 = (bf16[2048,256]{1,0:T(8,128)(2,1)S(1)}, bf16[2048,256]{1,0:T(8,128)(2,1)}) custom-call(s32[1]{0:T(128)} %bitcast.2.at_ref, bf16[2048,1024]{1,0:T(8,128)(2,1)} %bitcast.229, bf16[1024,512]{1,0:T(8,128)(2,1)S(1)} %copy-done.2, f32[1,512]{1,0:T(1,128)S(1)} %bitcast.228), custom_call_target="tpu_custom_call" | custom-call | flops 214748368 | bytes 734208 | tf_op jit(solution)/shard_map/pallas_call | solution.py:362
  67.3 8.3 %shard_map.290 = (bf16[2,64,1024]{2,1,0:T(8,128)(2,1)S(1)}, bf16[2,1024,128]{2,1,0:T(8,128)(2,1)S(1)}, bf16[4,4,64,128]{3,2,1,0:T(8,128)(2,1)}, f32[2,1,1024]{2,1,0:T(1,128)S(1)}) custom-call(s32[1]{0:T(128)} %bitcast.at_ref, bf16[2,256,1024]{2,1,0:T(8,128)(2,1)S(1)} %copy-done, bf16[2,256,1024]{2,1,0:T(8,128)(2,1)S(1)} %collective-permute-done.3.refs_1_, ...), custom_call_target="tpu_custom_call" | custom-call | flops 187904816 | bytes 564506 | tf_op jit(solution)/shard_map/pallas_call | solution.py:362
  82.6 8.0 %all-to-all-done.1 = bf16[16,64,128]{2,1,0:T(8,128)(2,1)S(1)} async-done(((bf16[16,64,128]{2,1,0:T(8,128)(2,1)}), bf16[16,64,128]{2,1,0:T(8,128)(2,1)S(1)}, u32[]{:S(2)}, u32[]{:S(2)}) %all-to-all-start.1) | async-done | bytes 262176 | tf_op jit(solution)/shard_map/all_to_all | solution.py:611
  100.8 5.3 %all-to-all-start.2 = ((bf16[16,128,128]{2,1,0:T(8,128)(2,1)}), bf16[16,128,128]{2,1,0:T(8,128)(2,1)S(1)}, u32[]{:S(2)}, u32[]{:S(2)}) async-start(bf16[16,128,128]{2,1,0:T(8,128)(2,1)} %bitcast.27), calls=%async_computation.2 | async-start | bytes 1048576 | tf_op jit(solution)/shard_map/all_to_all | solution.py:611
  111.1 9.8 %all-to-all-done.2 = bf16[16,128,128]{2,1,0:T(8,128)(2,1)S(1)} async-done(((bf16[16,128,128]{2,1,0:T(8,128)(2,1)}), bf16[16,128,128]{2,1,0:T(8,128)(2,1)S(1)}, u32[]{:S(2)}, u32[]{:S(2)}) %all-to-all-start.2) | async-done | bytes 524320 | tf_op jit(solution)/shard_map/all_to_all | solution.py:611
  122.4 13.9 %shard_map.293 = bf16[4,4,144,128]{3,2,1,0:T(8,128)(2,1)S(1)} custom-call(bf16[4,4,128,128]{3,2,1,0:T(8,128)(2,1)S(1)} %fusion.58.q_ref, bf16[2,1024,256]{2,1,0:T(8,128)(2,1)S(1)} %bitcast.217, bf16[2,1024,256]{2,1,0:T(8,128)(2,1)} %bitcast.18.refs_1_), custom_call_target="tpu_custom_call" | custom-call | flops 429496736 | bytes 321126 | tf_op jit(solution)/shard_map/pallas_call | solution.py:362
  137.4 22.0 %all_to_all.56 = bf16[16,144,128]{2,1,0:T(8,128)(2,1)S(1)} all-to-all(bf16[16,144,128]{2,1,0:T(8,128)(2,1)S(1)} %bitcast.215), channel_id=1, replica_groups=mesh['dp'=2,'ctx'=4,'tp'=4] {'tp','ctx'}, dimensions={0} | all-to-all | bytes 1179648 | tf_op jit(solution)/shard_map/all_to_all | solution.py:611
  167.1 4.4 collective-permute-done.12
  174.0 7.6 %multiply_convert_fusion = (bf16[256,2048]{1,0:T(8,128)(2,1)S(1)}, f32[256,2048]{1,0:T(8,128)S(1)}, f32[256,2048]{1,0:T(8,128)S(1)}) fusion(f32[2048]{0:T(1024)S(1)} %maximum_convert_fusion, bf16[1024,4096]{1,0:T(8,128)(2,1)} %all-gather.10.cloned.1.call-done, bf16[128,1024]{1,0:T(8,128)(2,1)} %copy-done.54, bf16[128,1024]{1,0:T(8,128)(2,1)} %copy-done.50), kind=kOutput, calls=%fused_computation.13 | convolution fusion | flops 1109393408 | bytes 9969664 | tf_op jit(solution)/shard_map/dot_general | solution.py:25
  183.7 7.0 %collective-permute-done.13 = bf16[128,1024]{1,0:T(8,128)(2,1)S(1)} collective-permute-done((bf16[128,1024]{1,0:T(8,128)(2,1)S(1)}, bf16[128,1024]{1,0:T(8,128)(2,1)S(1)}, u32[]{:S(2)}, u32[]{:S(2)}) %collective-permute-start.13) | collective-permute-done | bytes 262176 | tf_op jit(solution)/shard_map/ppermute | solution.py:608
  193.7 6.3 %collective-permute-done.14 = bf16[128,1024]{1,0:T(8,128)(2,1)S(1)} collective-permute-done((bf16[128,1024]{1,0:T(8,128)(2,1)S(1)}, bf16[128,1024]{1,0:T(8,128)(2,1)S(1)}, u32[]{:S(2)}, u32[]{:S(2)}) %collective-permute-start.14) | collective-permute-done | bytes 262176 | tf_op jit(solution)/shard_map/ppermute | solution.py:608
  201.9 5.1 %shard_map.297 = bf16[1024,4096]{1,0:T(8,128)(2,1)} custom-call(bf16[256,1024]{1,0:T(8,128)(2,1)S(1)} %pad_maximum_fusion.1.two_ref, bf16[256,2048]{1,0:T(8,128)(2,1)S(1)} %get-tuple-element.398.pre_ref, bf16[256,1024]{1,0:T(8,128)(2,1)S(1)} %pad_maximum_fusion.2.low_ref, bf16[256,2048]{1,0:T(8,128)(2,1)S(1)} %get-tuple-element.351.active_ref), custom_call_target="tpu_custom_call" | custom-call | flops 214748368 | bytes 1153433 | tf_op jit(solution)/shard_map/pallas_call | solution.py:362
  213.1 6.1 %collective-permute-done.15 = bf16[128,1024]{1,0:T(8,128)(2,1)S(1)} collective-permute-done((bf16[128,1024]{1,0:T(8,128)(2,1)S(1)}, bf16[128,1024]{1,0:T(8,128)(2,1)S(1)}, u32[]{:S(2)}, u32[]{:S(2)}) %collective-permute-start.15) | collective-permute-done | bytes 262176 | tf_op jit(solution)/shard_map/ppermute | solution.py:608
  228.2 15.5 %all-to-all-done.4 = bf16[16,144,128]{2,1,0:T(8,128)(2,1)S(1)} async-done(((bf16[16,144,128]{2,1,0:T(8,128)(2,1)}), bf16[16,144,128]{2,1,0:T(8,128)(2,1)S(1)}, u32[]{:S(2)}, u32[]{:S(2)}) %all-to-all-start.4) | async-done | bytes 589856 | tf_op jit(solution)/shard_map/all_to_all | solution.py:611
  244.9 4.3 all-to-all-start.5
  250.3 22.3 %shard_map.295 = (bf16[2,1024,256]{2,1,0:T(8,128)(2,1)S(1)}, bf16[2,1024,256]{2,1,0:T(8,128)(2,1)}, bf16[4,4,128,128]{3,2,1,0:T(8,128)(2,1)}) custom-call(bf16[4,4,128,128]{3,2,1,0:T(8,128)(2,1)S(1)} %fusion.58.q_ref, bf16[4,4,144,128]{3,2,1,0:T(8,128)(2,1)S(1)} %bitcast.227, bf16[2,1024,256]{2,1,0:T(8,128)(2,1)} %bitcast.216, ...), custom_call_target="tpu_custom_call" | custom-call | flops 1073741824 | bytes 583270 | tf_op jit(solution)/shard_map/pallas_call | solution.py:362
  275.3 4.3 all-to-all-start.6
  282.3 8.8 %shard_map.296 = (bf16[2048,1024]{1,0:T(8,128)(2,1)}, f32[1,512]{1,0:T(1,128)S(1)}, bf16[1024,512]{1,0:T(8,128)(2,1)S(1)}) custom-call(s32[1]{0:T(128)} %bitcast.2.at_ref, bf16[2048,1024]{1,0:T(8,128)(2,1)} %bitcast.230, bf16[1024,512]{1,0:T(8,128)(2,1)S(1)} %copy-done.3, bf16[2048,256]{1,0:T(8,128)(2,1)S(1)} %bitcast.226, bf16[2048,256]{1,0:T(8,128)(2,1)} %bitcast.242), custom_call_target="tpu_custom_call" | custom-call | flops 429496736 | bytes 1258496 | tf_op jit(solution)/shard_map/pallas_call | solution.py:362
  308.9 4.3 all-to-all-start.7
  321.7 4.7 shard_map.299
  337.1 7.8 %shard_map.302 = (bf16[4,4,192,128]{3,2,1,0:T(8,128)(2,1)}, f32[192,1024]{1,0:T(8,128)S(1)}, f32[192,1]{1,0:T(8,128)S(1)}) custom-call(s32[1]{0:T(128)} %bitcast.at_ref, bf16[2,256,1024]{2,1,0:T(8,128)(2,1)S(1)} %copy-done, bf16[2,256,1024]{2,1,0:T(8,128)(2,1)} %copy-done.1, bf16[2,256,1024]{2,1,0:T(8,128)(2,1)} %collective-permute-done.4.refs_2_, ...), custom_call_target="tpu_custom_call" | custom-call | flops 348966080 | bytes 708685 | tf_op jit(solution)/shard_map/pallas_call | solution.py:362
  344.9 6.1 %all-to-all-start.8 = ((bf16[16,192,128]{2,1,0:T(8,128)(2,1)}), bf16[16,192,128]{2,1,0:T(8,128)(2,1)S(1)}, u32[]{:S(2)}, u32[]{:S(2)}) async-start(bf16[16,192,128]{2,1,0:T(8,128)(2,1)} %bitcast.61), calls=%async_computation.9 | async-start | bytes 1572864 | tf_op jit(solution)/shard_map/all_to_all | solution.py:611
  362.4 36.7 %collective-permute-done.23 = bf16[128,512]{1,0:T(8,128)(2,1)S(1)} collective-permute-done((bf16[128,512]{1,0:T(8,128)(2,1)S(1)}, bf16[128,512]{1,0:T(8,128)(2,1)S(1)}, u32[]{:S(2)}, u32[]{:S(2)}) %collective-permute-start.23) | collective-permute-done | bytes 131104 | tf_op jit(solution)/shard_map/ppermute | solution.py:626
  399.1 15.9 %collective-permute-done.24 = bf16[128,2,1024]{2,0,1:T(8,128)(2,1)} collective-permute-done((bf16[128,2,1024]{2,0,1:T(8,128)(2,1)}, bf16[128,2,1024]{2,0,1:T(8,128)(2,1)}, u32[]{:S(2)}, u32[]{:S(2)}) %collective-permute-start.24) | collective-permute-done | bytes 524320 | tf_op jit(solution)/shard_map/ppermute | solution.py:608
  415.9 4.1 all-to-all-start.9
  426.8 5.8 %shard_map.304 = bf16[128,1024]{1,0:T(8,128)(2,1)} custom-call(bf16[16,192,128]{2,1,0:T(8,128)(2,1)S(1)} %all-to-all-done.8.stacked_ref, bf16[1024,3072]{1,0:T(8,128)(2,1)} %all-gather.12.cloned.1.call-done.proj_ref, f32[128,1024]{1,0:T(8,128)S(1)} %get-tuple-element.343.first_ref), custom_call_target="tpu_custom_call" | custom-call | flops 80530640 | bytes 786432 | tf_op jit(solution)/shard_map/pallas_call | solution.py:362
  440.3 6.1 %all-to-all-start.10 = ((bf16[4,16,256]{2,1,0:T(8,128)(2,1)}), bf16[4,16,256]{2,1,0:T(8,128)(2,1)S(1)}, u32[]{:S(2)}, u32[]{:S(2)}) async-start(bf16[4,16,256]{2,1,0:T(8,128)(2,1)} %broadcast_in_dim.23), calls=%async_computation.12 | async-start | bytes 65536 | tf_op jit(solution)/shard_map/all_to_all | solution.py:656
  452.2 9.0 %all-gather.14.cloned.1.call-done = bf16[512,1024]{1,0:T(8,128)(2,1)} async-done(((bf16[128,1024]{1,0:T(8,128)(2,1)}), bf16[512,1024]{1,0:T(8,128)(2,1)}) %all-gather.14.cloned.1.call-update) | async-done | bytes 1048592 | tf_op jit(solution)/shard_map/all_gather | solution.py:872
  (419 shorter events, 161.7 us)
Async XLA Ops:
  7.3 51.6 %all-gather.6.cloned.1.call-start = ((), (), s32[]{:S(2)}) async-start(), calls=%async_computation.13 | async-start | bytes 1179648 | tf_op jit(solution)/shard_map/all_gather | solution.py:684
  9.2 81.8 %all-gather.8.cloned.1.call-start = ((), (), s32[]{:S(2)}) async-start(), calls=%async_computation.14 | async-start | bytes 7077888 | tf_op jit(solution)/shard_map/all_gather | solution.py:692
  9.2 24.5 %collective-permute-start.3 = (bf16[2,256,1024]{2,1,0:T(8,128)(2,1)}, bf16[2,256,1024]{2,1,0:T(8,128)(2,1)S(1)}, u32[]{:S(2)}, u32[]{:S(2)}) collective-permute-start(bf16[2,256,1024]{2,1,0:T(8,128)(2,1)} %refs_0_.2), channel_id=1, source_target_pairs={{0,4},{4,0},{8,12},{12,8},{1,5},{5,1},{9,13},{13,9},{2,6},{6,2},{1... | collective-permute-start | bytes 3145736 | tf_op jit(solution)/shard_map/ppermute | solution.py:605
  9.8 30.8 %collective-permute-start.4 = (bf16[2,256,1024]{2,1,0:T(8,128)(2,1)}, bf16[2,256,1024]{2,1,0:T(8,128)(2,1)}, u32[]{:S(2)}, u32[]{:S(2)}) collective-permute-start(bf16[2,256,1024]{2,1,0:T(8,128)(2,1)} %refs_0_.2), channel_id=1, source_target_pairs={{0,8},{4,12},{8,0},{12,4},{1,9},{5,13},{9,1},{13,5},{2,10},{6,14},... | collective-permute-start | bytes 3145736 | tf_op jit(solution)/shard_map/ppermute | solution.py:605
  16.6 17.1 %collective-permute-start.1 = (bf16[3,128,256]{2,1,0:T(8,128)(2,1)S(1)}, bf16[3,128,256]{2,1,0:T(8,128)(2,1)S(1)}, u32[]{:S(2)}, u32[]{:S(2)}) collective-permute-start(bf16[3,128,256]{2,1,0:T(8,128)(2,1)S(1)} %shard_map.287.refs_0_), channel_id=1, source_target_pairs={{0,2},{1,3},{2,0},{3,1},{4,6},{5,7},{6,4},{7,5},{8,10},{9,11},{10,... | collective-permute-start | bytes 589832 | tf_op jit(solution)/shard_map/ppermute | solution.py:608
  55.5 27.1 %collective-permute-start.6 = (bf16[128,2048]{1,0:T(8,128)(2,1)S(1)}, bf16[128,2048]{1,0:T(8,128)(2,1)}, u32[]{:S(2)}, u32[]{:S(2)}) collective-permute-start(bf16[128,2048]{1,0:T(8,128)(2,1)S(1)} %shard_map.292), channel_id=1, source_target_pairs={{0,2},{1,3},{2,0},{3,1},{4,6},{5,7},{6,4},{7,5},{8,10},{9,11},{10,... | collective-permute-start | bytes 1572872 | tf_op jit(solution)/shard_map/ppermute | solution.py:608
  66.8 23.9 %collective-permute-start.7 = (bf16[2048,256]{1,0:T(8,128)(2,1)}, bf16[2048,256]{1,0:T(8,128)(2,1)}, u32[]{:S(2)}, u32[]{:S(2)}) collective-permute-start(bf16[2048,256]{1,0:T(8,128)(2,1)} %get-tuple-element.141), channel_id=1, source_target_pairs={{0,4},{4,0},{8,12},{12,8},{1,5},{5,1},{9,13},{13,9},{2,6},{6,2},{1... | collective-permute-start | bytes 3145736 | tf_op jit(solution)/shard_map/ppermute | solution.py:605
  80.7 93.4 %all-gather.10.cloned.1.call-start = ((), (), s32[]{:S(2)}) async-start(), calls=%async_computation.15 | async-start | bytes 9437184 | tf_op jit(solution)/shard_map/all_gather | solution.py:744
  100.8 20.1 %all-to-all-start.2 = ((bf16[16,128,128]{2,1,0:T(8,128)(2,1)}), bf16[16,128,128]{2,1,0:T(8,128)(2,1)S(1)}, u32[]{:S(2)}, u32[]{:S(2)}) async-start(bf16[16,128,128]{2,1,0:T(8,128)(2,1)} %bitcast.27), calls=%async_computation.2 | async-start | bytes 1048576 | tf_op jit(solution)/shard_map/all_to_all | solution.py:611
  106.1 122.1 %all-gather.12.cloned.1.call-start = ((), (), s32[]{:S(2)}) async-start(), calls=%async_computation.16 | async-start | bytes 7077888 | tf_op jit(solution)/shard_map/all_gather | solution.py:758
  106.7 29.6 %collective-permute-start.8 = (bf16[3,128,256]{2,1,0:T(8,128)(2,1)S(1)}, bf16[3,128,256]{2,1,0:T(8,128)(2,1)S(1)}, u32[]{:S(2)}, u32[]{:S(2)}) collective-permute-start(bf16[3,128,256]{2,1,0:T(8,128)(2,1)S(1)} %copy-done.17), channel_id=1, source_target_pairs={{0,1},{1,0},{2,3},{3,2},{4,5},{5,4},{6,7},{7,6},{8,9},{9,8},{10,11... | collective-permute-start | bytes 589832 | tf_op jit(solution)/shard_map/ppermute | solution.py:608
  108.7 27.7 %collective-permute-start.9 = (bf16[3,128,256]{2,1,0:T(8,128)(2,1)S(1)}, bf16[3,128,256]{2,1,0:T(8,128)(2,1)S(1)}, u32[]{:S(2)}, u32[]{:S(2)}) collective-permute-start(bf16[3,128,256]{2,1,0:T(8,128)(2,1)S(1)} %copy-done.17), channel_id=1, source_target_pairs={{0,2},{1,3},{2,0},{3,1},{4,6},{5,7},{6,4},{7,5},{8,10},{9,11},{10,... | collective-permute-start | bytes 589832 | tf_op jit(solution)/shard_map/ppermute | solution.py:608
  111.0 25.3 %collective-permute-start.10 = (bf16[3,128,256]{2,1,0:T(8,128)(2,1)S(1)}, bf16[3,128,256]{2,1,0:T(8,128)(2,1)S(1)}, u32[]{:S(2)}, u32[]{:S(2)}) collective-permute-start(bf16[3,128,256]{2,1,0:T(8,128)(2,1)S(1)} %copy-done.17), channel_id=1, source_target_pairs={{0,3},{1,2},{2,1},{3,0},{4,7},{5,6},{6,5},{7,4},{8,11},{9,10},{10,... | collective-permute-start | bytes 589832 | tf_op jit(solution)/shard_map/ppermute | solution.py:608
  137.4 156.7 %reduce-scatter.3.cloned.1.call-start = ((), (), s32[]{:S(2)}) async-start(), calls=%async_computation.17 | async-start | bytes 9437184 | tf_op jit(solution)/shard_map/reduce_scatter | solution.py:796
  224.4 19.3 %all-to-all-start.4 = ((bf16[16,144,128]{2,1,0:T(8,128)(2,1)}), bf16[16,144,128]{2,1,0:T(8,128)(2,1)S(1)}, u32[]{:S(2)}, u32[]{:S(2)}) async-start(bf16[16,144,128]{2,1,0:T(8,128)(2,1)} %bitcast.232), calls=%async_computation.4 | async-start | bytes 1179648 | tf_op jit(solution)/shard_map/all_to_all | solution.py:611
  244.9 30.5 %all-to-all-start.5 = ((bf16[4,128,1024]{2,1,0:T(8,128)(2,1)}), bf16[4,128,1024]{2,1,0:T(8,128)(2,1)}, u32[]{:S(2)}, u32[]{:S(2)}) async-start(bf16[4,128,1024]{2,1,0:T(8,128)(2,1)} %broadcast_in_dim.20), calls=%async_computation.5 | async-start | bytes 2097152 | tf_op jit(solution)/shard_map/all_to_all | solution.py:656
  275.3 18.7 %all-to-all-start.6 = ((bf16[16,128,128]{2,1,0:T(8,128)(2,1)}), bf16[16,128,128]{2,1,0:T(8,128)(2,1)}, u32[]{:S(2)}, u32[]{:S(2)}) async-start(bf16[16,128,128]{2,1,0:T(8,128)(2,1)} %bitcast.51), calls=%async_computation.6 | async-start | bytes 1048576 | tf_op jit(solution)/shard_map/all_to_all | solution.py:611
  279.6 135.4 %reduce-scatter.5.cloned.1.call-start = ((), (), s32[]{:S(2)}) async-start(), calls=%async_computation.18 | async-start | bytes 5242880 | tf_op jit(solution)/shard_map/reduce_scatter | solution.py:832
  302.4 18.6 %collective-permute-start.17 = (bf16[4,128,3072]{2,1,0:T(8,128)(2,1)}, bf16[4,128,3072]{2,1,0:T(8,128)(2,1)}, u32[]{:S(2)}, u32[]{:S(2)}) collective-permute-start(bf16[4,128,3072]{2,1,0:T(8,128)(2,1)} %get-tuple-element.168), channel_id=1, source_target_pairs={{0,4},{4,0},{8,12},{12,8},{16,20},{20,16},{24,28},{28,24},{1,5},{5... | collective-permute-start | bytes 9437192 | tf_op jit(solution)/shard_map/ppermute | solution.py:626
  308.9 19.4 %all-to-all-start.7 = ((bf16[16,64,128]{2,1,0:T(8,128)(2,1)}), bf16[16,64,128]{2,1,0:T(8,128)(2,1)S(1)}, u32[]{:S(2)}, u32[]{:S(2)}) async-start(bf16[16,64,128]{2,1,0:T(8,128)(2,1)} %bitcast.56), calls=%async_computation.8 | async-start | bytes 524288 | tf_op jit(solution)/shard_map/all_to_all | solution.py:611
  328.3 16.7 %collective-permute-start.19 = (bf16[2,128,512]{2,1,0:T(8,128)(2,1)}, bf16[2,128,512]{2,1,0:T(8,128)(2,1)}, u32[]{:S(2)}, u32[]{:S(2)}) collective-permute-start(bf16[2,128,512]{2,1,0:T(8,128)(2,1)} %copy-done.35), channel_id=1, source_target_pairs={{0,16},{4,20},{8,24},{12,28},{16,0},{20,4},{24,8},{28,12},{1,17},{... | collective-permute-start | bytes 786440 | tf_op jit(solution)/shard_map/ppermute | solution.py:626
  344.9 70.0 %all-to-all-start.8 = ((bf16[16,192,128]{2,1,0:T(8,128)(2,1)}), bf16[16,192,128]{2,1,0:T(8,128)(2,1)S(1)}, u32[]{:S(2)}, u32[]{:S(2)}) async-start(bf16[16,192,128]{2,1,0:T(8,128)(2,1)} %bitcast.61), calls=%async_computation.9 | async-start | bytes 1572864 | tf_op jit(solution)/shard_map/all_to_all | solution.py:611
  351.7 63.2 %collective-permute-start.20 = (bf16[1,128,3072]{2,1,0:T(8,128)(2,1)}, bf16[1,128,3072]{2,1,0:T(8,128)(2,1)}, u32[]{:S(2)}, u32[]{:S(2)}) collective-permute-start(bf16[1,128,3072]{2,1,0:T(8,128)(2,1)} %copy-done.34), channel_id=1, source_target_pairs={{0,8},{4,12},{8,0},{12,4},{16,24},{20,28},{24,16},{28,20},{1,9},{5... | collective-permute-start | bytes 2359304 | tf_op jit(solution)/shard_map/ppermute | solution.py:626
  353.6 61.3 %collective-permute-start.21 = (bf16[1,128,3072]{2,1,0:T(8,128)(2,1)}, bf16[1,128,3072]{2,1,0:T(8,128)(2,1)}, u32[]{:S(2)}, u32[]{:S(2)}) collective-permute-start(bf16[1,128,3072]{2,1,0:T(8,128)(2,1)} %copy-done.33), channel_id=1, source_target_pairs={{0,16},{4,20},{8,24},{12,28},{16,0},{20,4},{24,8},{28,12},{1,17},{... | collective-permute-start | bytes 2359304 | tf_op jit(solution)/shard_map/ppermute | solution.py:626
  353.9 61.0 %collective-permute-start.22 = (bf16[1,128,3072]{2,1,0:T(8,128)(2,1)}, bf16[1,128,3072]{2,1,0:T(8,128)(2,1)}, u32[]{:S(2)}, u32[]{:S(2)}) collective-permute-start(bf16[1,128,3072]{2,1,0:T(8,128)(2,1)} %copy-done.32), channel_id=1, source_target_pairs={{0,24},{4,28},{8,16},{12,20},{16,8},{20,12},{24,0},{28,4},{1,25},{... | collective-permute-start | bytes 2359304 | tf_op jit(solution)/shard_map/ppermute | solution.py:626
  355.2 59.7 %collective-permute-start.24 = (bf16[128,2,1024]{2,0,1:T(8,128)(2,1)}, bf16[128,2,1024]{2,0,1:T(8,128)(2,1)}, u32[]{:S(2)}, u32[]{:S(2)}) collective-permute-start(bf16[128,2,1024]{2,0,1:T(8,128)(2,1)} %bitcast.246), channel_id=1, source_target_pairs={{0,2},{1,3},{2,0},{3,1},{4,6},{5,7},{6,4},{7,5},{8,10},{9,11},{10,... | collective-permute-start | bytes 1572872 | tf_op jit(solution)/shard_map/ppermute | solution.py:608
  360.6 38.5 %collective-permute-start.23 = (bf16[128,512]{1,0:T(8,128)(2,1)S(1)}, bf16[128,512]{1,0:T(8,128)(2,1)S(1)}, u32[]{:S(2)}, u32[]{:S(2)}) collective-permute-start(bf16[128,512]{1,0:T(8,128)(2,1)S(1)} %get-tuple-element.365), channel_id=1, source_target_pairs={{0,8},{4,12},{8,0},{12,4},{16,24},{20,28},{24,16},{28,20},{1,9},{5... | collective-permute-start | bytes 393224 | tf_op jit(solution)/shard_map/ppermute | solution.py:626
  415.9 22.5 %all-to-all-start.9 = ((bf16[8,224,128]{2,1,0:T(8,128)(2,1)}), bf16[8,224,128]{2,1,0:T(8,128)(2,1)}, u32[]{:S(2)}, u32[]{:S(2)}) async-start(bf16[8,224,128]{2,1,0:T(8,128)(2,1)} %pad_maximum_fusion.3), calls=%async_computation.11 | async-start | bytes 917504 | tf_op jit(solution)/shard_map/all_to_all | solution.py:894
  420.1 41.2 %all-gather.14.cloned.1.call-start = ((), (), s32[]{:S(2)}) async-start(), calls=%async_computation.19 | async-start | bytes 1310720 | tf_op jit(solution)/shard_map/all_gather | solution.py:872
  422.3 17.3 %collective-permute-start.25 = (bf16[3,128,256]{2,1,0:T(8,128)(2,1)S(1)}, bf16[3,128,256]{2,1,0:T(8,128)(2,1)S(1)}, u32[]{:S(2)}, u32[]{:S(2)}) collective-permute-start(bf16[3,128,256]{2,1,0:T(8,128)(2,1)S(1)} %get-tuple-element.208), channel_id=1, source_target_pairs={{0,1},{1,0},{2,3},{3,2},{4,5},{5,4},{6,7},{7,6},{8,9},{9,8},{10,11... | collective-permute-start | bytes 589832 | tf_op jit(solution)/shard_map/ppermute | solution.py:608
  422.4 17.3 %collective-permute-start.26 = (bf16[3,128,256]{2,1,0:T(8,128)(2,1)S(1)}, bf16[3,128,256]{2,1,0:T(8,128)(2,1)}, u32[]{:S(2)}, u32[]{:S(2)}) collective-permute-start(bf16[3,128,256]{2,1,0:T(8,128)(2,1)S(1)} %get-tuple-element.209), channel_id=1, source_target_pairs={{0,2},{1,3},{2,0},{3,1},{4,6},{5,7},{6,4},{7,5},{8,10},{9,11},{10,... | collective-permute-start | bytes 589832 | tf_op jit(solution)/shard_map/ppermute | solution.py:608
  424.4 15.3 %collective-permute-start.27 = (bf16[3,128,256]{2,1,0:T(8,128)(2,1)S(1)}, bf16[3,128,256]{2,1,0:T(8,128)(2,1)}, u32[]{:S(2)}, u32[]{:S(2)}) collective-permute-start(bf16[3,128,256]{2,1,0:T(8,128)(2,1)S(1)} %get-tuple-element.210), channel_id=1, source_target_pairs={{0,3},{1,2},{2,1},{3,0},{4,7},{5,6},{6,5},{7,4},{8,11},{9,10},{10,... | collective-permute-start | bytes 589832 | tf_op jit(solution)/shard_map/ppermute | solution.py:608
  (85 other events, 794.4 us)
Sparse Core Ops, SparseCore 0:
  10.6 30.5 all-gather.5
  43.0 47.9 all-gather.7
  93.5 65.8 all-gather.9
  161.1 45.6 all-gather.11
  210.1 73.1 reduce-scatter.2
  294.2 97.6 reduce-scatter.4
  432.7 28.4 all-gather.13

commit v5 on v4

--- a/solution.py
+++ b/solution.py
@@ -9,9 +9,9 @@
 
 EPSILON = 1e-05
 HEAD = 64
-KEY_TILE = 512
+KEY_TILE = 1024
 STAT_ROWS = 16
-ROW_TILE = 512
+ROW_TILE = 1024
 COST_SHARE = 10
 VMEM_BYTES = 50 * 1024 * 1024
 PLANE = ("dp", "ctx")
@@ -70,6 +70,18 @@
 def gather_chunks(ref):
     halves, blocks = ref.shape[:2]
     return jnp.concatenate([ref[h, b] for h in range(halves) for b in range(blocks)], 1)
+
+
+def copy_kernel(in_ref, out_ref):
+    out_ref[...] = in_ref[...]
+
+
+def mlp_split_kernel(in_ref, *out_refs):
+    width = out_refs[0].shape[2]
+    for i, out_ref in enumerate(out_refs):
+        for kind in range(2):
+            at = (2 * kind + i) * width
+            out_ref[kind] = in_ref[:, at : at + width]
 
 
 def slot_at(own, k, size):
@@ -378,8 +390,11 @@
 
 
 def one_step(kernel, out, *operands, flops=0):
+    outs = out if isinstance(out, list) else [out]
     specs = [IN_SMEM if v.dtype == jnp.int32 else whole(v.shape) for v in operands]
-    return call(kernel, 1, specs, [whole(out)], [shaped(out, BF16)], operands, (flops, 0))[0]
+    shapes = [shaped(v, BF16) for v in outs]
+    results = call(kernel, 1, specs, [whole(v) for v in outs], shapes, operands, (flops, 0))
+    return results if isinstance(out, list) else results[0]
 
 
 def self_forward(at, slots, weights, query_bias, pair_bias, chunk_shape):
@@ -853,16 +868,16 @@
     stacked, head_grad, head_sum = self_backward(
         ctx_at, x_slots, self_query, self_pair, self_mixed, self_mix_grad, self_lse
     )
-    mlp_grad = mlp_grad.reshape(shard, 2, 2, hidden)
-    mlp_grad = [mlp_grad[:, :, 0], mlp_grad[:, :, 1]]
-    stacked, head_grad, square_grad, kv_grad, mlp_grad = together(
-        stacked, head_grad, square_grad, kv_grad, mlp_grad
-    )
+    mlp_grad = one_step(mlp_split_kernel, [(2, shard, hidden)] * 2, mlp_grad)
+    stacked, head_grad, square_grad, kv_grad, mlp_grad, hidden_out = together(
+        stacked, head_grad, square_grad, kv_grad, mlp_grad, hidden_out
+    )
+    hidden_out = one_step(copy_kernel, (rows, width), hidden_out.reshape(rows, width))
     square_grad, kv_grad = sum_far(square_grad), sum_x(kv_grad)
     stacked = exchange(stacked.reshape(all_heads, 3 * HEAD, part))
     mlp_grad = [mlp_grad[0], tp_swap(mlp_grad[1], 2)]
-    stacked, head_grad, square_grad, kv_grad, mlp_grad, encoder_grad = together(
-        stacked, head_grad, square_grad, kv_grad, mlp_grad, encoder_grad
+    head_grad, square_grad, kv_grad, mlp_grad, encoder_grad, hidden_out = together(
+        head_grad, square_grad, kv_grad, mlp_grad, encoder_grad, hidden_out
     )
     if plane != 8:
         square_grad = [sum_end(square_grad).astype(BF16)[None]]
@@ -907,12 +922,11 @@
         ends.append(ends[-1] + size)
     sums = jnp.pad(sums, (0, 16 * 256 - sums.size)).reshape(16, 256).astype(BF16)
 
-    sums, square_grad = together(sums, square_grad)
     mlp_grad = mlp_grad[0].astype(F32) + mlp_grad[1].astype(F32)
-    up_out, down_out = mlp_grad[:, 0], mlp_grad[:, 1].T
+    up_out, down_out = mlp_grad[0], mlp_grad[1].T
+    sums, input_grad, square_grad = together(whole_on_ranks(sums), input_grad, square_grad)
     square_grad = sum(v.astype(F32) for v in square_grad)
     self_out_out, cross_q_out, cross_out_out = square_grad[0].T, square_grad[1], square_grad[2].T
-    sums, input_grad = together(whole_on_ranks(sums), input_grad)
     input_grad, encoder_grad = input_grad.astype(F32), encoder_grad.astype(F32)
     sums = sums.astype(F32).reshape(ranks, -1)
     norm_out, up_own, up_other, query_sums, value_sums, rms = (

time: 485 us -> 474 us (0.977)
  local copies, waits for them, and re-layouts: 53 us -> 48 us
    ppermute x7, waiting for transfers between devices: 36.7 us -> 12.1 us  [plane_swap(): return lax.ppermute(values, PLANE, [(i, i ^ k) for i in range(plane)])]
    all_to_all x6, waiting for transfers between devices: 36.4 us -> 55.3 us  [exchange(): lax.all_to_all(values, HEADS, split_axis=0, concat_axis=0, tiled=True)]
    pallas_call x18 -> x20, Pallas kernels: 92.1 us -> 90.2 us  [call(): pl.pallas_call(kernel, grid=(seqs,), in_specs=in_specs, out_specs=out_spe...]
    unnamed x169 -> x164, local copies, waits for them, and re-layouts: 34.9 us -> 34.3 us
  transfers between devices with their start and end apart: 44 -> 44, of which waited for: 19 -> 22; matrix products, arithmetic and copies ran while one was open for 15% -> 14% of each run, Pallas kernels for 19% -> 19%
where the time goes in v5:
time: 474 us; the launch traced here: 466 us
  waiting for transfers between devices  149 us (31%)
  Pallas kernels  90.2 us (19%)
  starting transfers between devices  72.8 us (15%)
  local copies, waits for them, and re-layouts  48 us (10%)
  blocking collectives  35.4 us (7%)
  matrix products  31.6 us (7%)
  other arithmetic  23.9 us (5%)
  between operations  15.6 us (3%)
    pallas_call x20, Pallas kernels, call(): pl.pallas_call(kernel, grid=(seqs,), in_specs=in_specs, out_specs=out_spe...  90.2 us
    ppermute x16, waiting for transfers between devices, tp_swap(): return lax.ppermute(values, 'tp', [(i, i ^ k) for i in range(ranks)])  57 us
    all_to_all x6, waiting for transfers between devices, exchange(): lax.all_to_all(values, HEADS, split_axis=0, concat_axis=0, tiled=True)  55.3 us
    unnamed x164, local copies, waits for them, and re-layouts  34.3 us
    dot_general x10, matrix products, contract(): lax.dot_general(left, right, (((left_dim,), (right_dim,)), ((), ())), pre...  31.6 us
    all_to_all x6, starting transfers between devices, exchange(): lax.all_to_all(values, HEADS, split_axis=0, concat_axis=0, tiled=True)  25.8 us
    ppermute x16, starting transfers between devices, tp_swap(): return lax.ppermute(values, 'tp', [(i, i ^ k) for i in range(ranks)])  24.1 us
    all_to_all x1, blocking collectives, exchange(): lax.all_to_all(values, HEADS, split_axis=0, concat_axis=0, tiled=True)  22.8 us
  transfers between devices with their start and end apart: 44, of which 22 were waited for; matrix products, arithmetic and copies ran while one was open for 14% of the time, Pallas kernels for 19%

profile of v5, /device:TPU:0, one launch (start us, length us, event | category | flops | bytes accessed | tf_op | source)
XLA Modules:
  0.0 466.1 jit_solution(7369707458798667595)
XLA Ops:
  19.4 6.2 %collective-permute-done.refs_1_ = bf16[3,128,256]{2,1,0:T(8,128)(2,1)S(1)} collective-permute-done((bf16[3,128,256]{2,1,0:T(8,128)(2,1)S(1)}, bf16[3,128,256]{2,1,0:T(8,128)(2,1)S(1)}, u32[]{:S(2)}, u32[]{:S(2)}) %collective-permute-start) | collective-permute-done | bytes 196640 | tf_op jit(solution)/shard_map/ppermute | solution.py:623
  25.6 8.1 %collective-permute-done.1.refs_2_ = bf16[3,128,256]{2,1,0:T(8,128)(2,1)S(1)} collective-permute-done((bf16[3,128,256]{2,1,0:T(8,128)(2,1)S(1)}, bf16[3,128,256]{2,1,0:T(8,128)(2,1)S(1)}, u32[]{:S(2)}, u32[]{:S(2)}) %collective-permute-start.1) | collective-permute-done | bytes 196640 | tf_op jit(solution)/shard_map/ppermute | solution.py:623
  33.7 6.9 %collective-permute-done.4.refs_2_ = bf16[2,256,1024]{2,1,0:T(8,128)(2,1)} collective-permute-done((bf16[2,256,1024]{2,1,0:T(8,128)(2,1)}, bf16[2,256,1024]{2,1,0:T(8,128)(2,1)}, u32[]{:S(2)}, u32[]{:S(2)}) %collective-permute-start.4) | collective-permute-done | bytes 1048608 | tf_op jit(solution)/shard_map/ppermute | solution.py:620
  42.3 12.6 %all_to_all.55 = bf16[8,208,128]{2,1,0:T(8,128)(2,1)S(1)} all-to-all(bf16[8,208,128]{2,1,0:T(8,128)(2,1)S(1)} %shard_map.288), channel_id=1, replica_groups=mesh['dp'=2,'ctx'=4,'tp'=4] {'dp','ctx'}, dimensions={0} | all-to-all | bytes 851968 | tf_op jit(solution)/shard_map/all_to_all | solution.py:697
  60.5 5.1 %shard_map.289 = (bf16[2048,256]{1,0:T(8,128)(2,1)S(1)}, bf16[2048,256]{1,0:T(8,128)(2,1)}) custom-call(s32[1]{0:T(128)} %bitcast.2.at_ref, bf16[2048,1024]{1,0:T(8,128)(2,1)} %bitcast.227, bf16[1024,512]{1,0:T(8,128)(2,1)S(1)} %copy-done.2, f32[1,512]{1,0:T(1,128)S(1)} %bitcast.226), custom_call_target="tpu_custom_call" | custom-call | flops 214748368 | bytes 734208 | tf_op jit(solution)/shard_map/pallas_call | solution.py:374
  66.9 8.0 %shard_map.290 = (bf16[2,64,1024]{2,1,0:T(8,128)(2,1)S(1)}, bf16[2,1024,128]{2,1,0:T(8,128)(2,1)S(1)}, bf16[4,4,64,128]{3,2,1,0:T(8,128)(2,1)}, f32[2,1,1024]{2,1,0:T(1,128)S(1)}) custom-call(s32[1]{0:T(128)} %bitcast.at_ref, bf16[2,256,1024]{2,1,0:T(8,128)(2,1)S(1)} %copy-done, bf16[2,256,1024]{2,1,0:T(8,128)(2,1)S(1)} %collective-permute-done.3.refs_1_, ...), custom_call_target="tpu_custom_call" | custom-call | flops 187904816 | bytes 564506 | tf_op jit(solution)/shard_map/pallas_call | solution.py:374
  82.6 7.3 %all-to-all-done.1 = bf16[16,64,128]{2,1,0:T(8,128)(2,1)S(1)} async-done(((bf16[16,64,128]{2,1,0:T(8,128)(2,1)}), bf16[16,64,128]{2,1,0:T(8,128)(2,1)S(1)}, u32[]{:S(2)}, u32[]{:S(2)}) %all-to-all-start.1) | async-done | bytes 262176 | tf_op jit(solution)/shard_map/all_to_all | solution.py:626
  101.1 4.9 %all-to-all-start.2 = ((bf16[16,128,128]{2,1,0:T(8,128)(2,1)}), bf16[16,128,128]{2,1,0:T(8,128)(2,1)S(1)}, u32[]{:S(2)}, u32[]{:S(2)}) async-start(bf16[16,128,128]{2,1,0:T(8,128)(2,1)} %bitcast.27), calls=%async_computation.2 | async-start | bytes 1048576 | tf_op jit(solution)/shard_map/all_to_all | solution.py:626
  111.1 9.8 %all-to-all-done.2 = bf16[16,128,128]{2,1,0:T(8,128)(2,1)S(1)} async-done(((bf16[16,128,128]{2,1,0:T(8,128)(2,1)}), bf16[16,128,128]{2,1,0:T(8,128)(2,1)S(1)}, u32[]{:S(2)}, u32[]{:S(2)}) %all-to-all-start.2) | async-done | bytes 524320 | tf_op jit(solution)/shard_map/all_to_all | solution.py:626
  122.3 13.2 %shard_map.293 = bf16[4,4,144,128]{3,2,1,0:T(8,128)(2,1)S(1)} custom-call(bf16[4,4,128,128]{3,2,1,0:T(8,128)(2,1)S(1)} %fusion.58.q_ref, bf16[2,1024,256]{2,1,0:T(8,128)(2,1)S(1)} %bitcast.213, bf16[2,1024,256]{2,1,0:T(8,128)(2,1)} %bitcast.18.refs_1_), custom_call_target="tpu_custom_call" | custom-call | flops 429496736 | bytes 321126 | tf_op jit(solution)/shard_map/pallas_call | solution.py:374
  136.6 22.8 %all_to_all.56 = bf16[16,144,128]{2,1,0:T(8,128)(2,1)S(1)} all-to-all(bf16[16,144,128]{2,1,0:T(8,128)(2,1)S(1)} %bitcast.211), channel_id=1, replica_groups=mesh['dp'=2,'ctx'=4,'tp'=4] {'tp','ctx'}, dimensions={0} | all-to-all | bytes 1179648 | tf_op jit(solution)/shard_map/all_to_all | solution.py:626
  165.3 4.4 collective-permute-done.12
  171.6 7.5 %multiply_convert_fusion = (bf16[256,2048]{1,0:T(8,128)(2,1)S(1)}, f32[256,2048]{1,0:T(8,128)S(1)}, f32[256,2048]{1,0:T(8,128)S(1)}) fusion(f32[2048]{0:T(1024)S(1)} %maximum_convert_fusion, bf16[1024,4096]{1,0:T(8,128)(2,1)} %all-gather.10.cloned.1.call-done, bf16[128,1024]{1,0:T(8,128)(2,1)S(1)} %collective-permute-done.11, ...), kind=kOutput, calls=%fused_computation.13 | convolution fusion | flops 1109393408 | bytes 9969664 | tf_op jit(solution)/shard_map/dot_general | solution.py:25
  181.1 6.9 %collective-permute-done.13 = bf16[128,1024]{1,0:T(8,128)(2,1)S(1)} collective-permute-done((bf16[128,1024]{1,0:T(8,128)(2,1)S(1)}, bf16[128,1024]{1,0:T(8,128)(2,1)S(1)}, u32[]{:S(2)}, u32[]{:S(2)}) %collective-permute-start.13) | collective-permute-done | bytes 262176 | tf_op jit(solution)/shard_map/ppermute | solution.py:623
  191.1 5.7 %collective-permute-done.14 = bf16[128,1024]{1,0:T(8,128)(2,1)S(1)} collective-permute-done((bf16[128,1024]{1,0:T(8,128)(2,1)S(1)}, bf16[128,1024]{1,0:T(8,128)(2,1)S(1)}, u32[]{:S(2)}, u32[]{:S(2)}) %collective-permute-start.14) | collective-permute-done | bytes 262176 | tf_op jit(solution)/shard_map/ppermute | solution.py:623
  198.7 5.1 %shard_map.297 = bf16[1024,4096]{1,0:T(8,128)(2,1)} custom-call(bf16[256,1024]{1,0:T(8,128)(2,1)S(1)} %pad_maximum_fusion.1.two_ref, bf16[256,2048]{1,0:T(8,128)(2,1)S(1)} %get-tuple-element.401.pre_ref, bf16[256,1024]{1,0:T(8,128)(2,1)S(1)} %pad_maximum_fusion.2.low_ref, bf16[256,2048]{1,0:T(8,128)(2,1)S(1)} %get-tuple-element.355.active_ref), custom_call_target="tpu_custom_call" | custom-call | flops 214748368 | bytes 1153433 | tf_op jit(solution)/shard_map/pallas_call | solution.py:374
  210.7 5.4 %collective-permute-done.15 = bf16[128,1024]{1,0:T(8,128)(2,1)S(1)} collective-permute-done((bf16[128,1024]{1,0:T(8,128)(2,1)S(1)}, bf16[128,1024]{1,0:T(8,128)(2,1)S(1)}, u32[]{:S(2)}, u32[]{:S(2)}) %collective-permute-start.15) | collective-permute-done | bytes 262176 | tf_op jit(solution)/shard_map/ppermute | solution.py:623
  225.1 15.5 %all-to-all-done.4 = bf16[16,144,128]{2,1,0:T(8,128)(2,1)S(1)} async-done(((bf16[16,144,128]{2,1,0:T(8,128)(2,1)}), bf16[16,144,128]{2,1,0:T(8,128)(2,1)S(1)}, u32[]{:S(2)}, u32[]{:S(2)}) %all-to-all-start.4) | async-done | bytes 589856 | tf_op jit(solution)/shard_map/all_to_all | solution.py:626
  241.7 3.9 all-to-all-start.5
  245.6 22.1 %shard_map.295 = (bf16[2,1024,256]{2,1,0:T(8,128)(2,1)S(1)}, bf16[2,1024,256]{2,1,0:T(8,128)(2,1)}, bf16[4,4,128,128]{3,2,1,0:T(8,128)(2,1)S(1)}) custom-call(bf16[4,4,128,128]{3,2,1,0:T(8,128)(2,1)S(1)} %fusion.58.q_ref, bf16[4,4,144,128]{3,2,1,0:T(8,128)(2,1)S(1)} %bitcast.224, bf16[2,1024,256]{2,1,0:T(8,128)(2,1)} %bitcast.212, ...), custom_call_target="tpu_custom_call" | custom-call | flops 1073741824 | bytes 583270 | tf_op jit(solution)/shard_map/pallas_call | solution.py:374
  271.4 3.9 all-to-all-start.6
  278.2 8.6 %shard_map.296 = (bf16[2048,1024]{1,0:T(8,128)(2,1)}, f32[1,512]{1,0:T(1,128)S(1)}, bf16[1024,512]{1,0:T(8,128)(2,1)S(1)}) custom-call(s32[1]{0:T(128)} %bitcast.2.at_ref, bf16[2048,1024]{1,0:T(8,128)(2,1)} %bitcast.228, bf16[1024,512]{1,0:T(8,128)(2,1)S(1)} %copy-done.3, bf16[2048,256]{1,0:T(8,128)(2,1)S(1)} %bitcast.222, bf16[2048,256]{1,0:T(8,128)(2,1)} %bitcast.53.refs_1_), custom_call_target="tpu_custom_call" | custom-call | flops 429496736 | bytes 1258496 | tf_op jit(solution)/shard_map/pallas_call | solution.py:374
  306.6 4.4 all-to-all-start.7
  315.9 4.6 shard_map.299
  332.6 7.5 %shard_map.302 = (bf16[4,4,192,128]{3,2,1,0:T(8,128)(2,1)S(1)}, f32[192,1024]{1,0:T(8,128)S(1)}, f32[192,1]{1,0:T(8,128)S(1)}) custom-call(s32[1]{0:T(128)} %bitcast.at_ref, bf16[2,256,1024]{2,1,0:T(8,128)(2,1)S(1)} %copy-done, bf16[2,256,1024]{2,1,0:T(8,128)(2,1)} %copy-done.1, bf16[2,256,1024]{2,1,0:T(8,128)(2,1)} %collective-permute-done.4.refs_2_, ...), custom_call_target="tpu_custom_call" | custom-call | flops 348966080 | bytes 708685 | tf_op jit(solution)/shard_map/pallas_call | solution.py:374
  341.8 5.3 %all-to-all-start.10 = ((bf16[16,192,128]{2,1,0:T(8,128)(2,1)}), bf16[16,192,128]{2,1,0:T(8,128)(2,1)S(1)}, u32[]{:S(2)}, u32[]{:S(2)}) async-start(bf16[16,192,128]{2,1,0:T(8,128)(2,1)} %bitcast.223), calls=%async_computation.12 | async-start | bytes 1572864 | tf_op jit(solution)/shard_map/all_to_all | solution.py:626
  359.6 19.2 %all-to-all-done.10.stacked_ref = bf16[16,192,128]{2,1,0:T(8,128)(2,1)S(1)} async-done(((bf16[16,192,128]{2,1,0:T(8,128)(2,1)}), bf16[16,192,128]{2,1,0:T(8,128)(2,1)S(1)}, u32[]{:S(2)}, u32[]{:S(2)}) %all-to-all-start.10) | async-done | bytes 786464 | tf_op jit(solution)/shard_map/all_to_all | solution.py:626
  378.8 5.9 %shard_map.305 = bf16[128,1024]{1,0:T(8,128)(2,1)} custom-call(bf16[16,192,128]{2,1,0:T(8,128)(2,1)S(1)} %all-to-all-done.10.stacked_ref, bf16[1024,3072]{1,0:T(8,128)(2,1)} %all-gather.12.cloned.1.call-done.proj_ref, f32[128,1024]{1,0:T(8,128)S(1)} %get-tuple-element.351.first_ref), custom_call_target="tpu_custom_call" | custom-call | flops 80530640 | bytes 786432 | tf_op jit(solution)/shard_map/pallas_call | solution.py:374
  384.7 10.5 %collective-permute-done.23 = bf16[128,512]{1,0:T(8,128)(2,1)S(1)} collective-permute-done((bf16[128,512]{1,0:T(8,128)(2,1)S(1)}, bf16[128,512]{1,0:T(8,128)(2,1)S(1)}, u32[]{:S(2)}, u32[]{:S(2)}) %collective-permute-start.23) | collective-permute-done | bytes 131104 | tf_op jit(solution)/shard_map/ppermute | solution.py:641
  395.2 16.5 %collective-permute-done.24 = bf16[2,128,1024]{2,1,0:T(8,128)(2,1)} collective-permute-done((bf16[2,128,1024]{2,1,0:T(8,128)(2,1)}, bf16[2,128,1024]{2,1,0:T(8,128)(2,1)}, u32[]{:S(2)}, u32[]{:S(2)}) %collective-permute-start.24) | collective-permute-done | bytes 524320 | tf_op jit(solution)/shard_map/ppermute | solution.py:623
  412.7 4.3 all-to-all-start.8
  436.0 11.0 %all-gather.14.cloned.1.call-done = bf16[512,1024]{1,0:T(8,128)(2,1)} async-done(((bf16[128,1024]{1,0:T(8,128)(2,1)}), bf16[512,1024]{1,0:T(8,128)(2,1)}) %all-gather.14.cloned.1.call-update) | async-done | bytes 1048592 | tf_op jit(solution)/shard_map/all_gather | solution.py:887
  (414 shorter events, 167.6 us)
Async XLA Ops:
  7.3 52.0 %all-gather.6.cloned.1.call-start = ((), (), s32[]{:S(2)}) async-start(), calls=%async_computation.13 | async-start | bytes 1179648 | tf_op jit(solution)/shard_map/all_gather | solution.py:699
  9.2 82.2 %all-gather.8.cloned.1.call-start = ((), (), s32[]{:S(2)}) async-start(), calls=%async_computation.14 | async-start | bytes 7077888 | tf_op jit(solution)/shard_map/all_gather | solution.py:707
  9.2 24.5 %collective-permute-start.3 = (bf16[2,256,1024]{2,1,0:T(8,128)(2,1)}, bf16[2,256,1024]{2,1,0:T(8,128)(2,1)S(1)}, u32[]{:S(2)}, u32[]{:S(2)}) collective-permute-start(bf16[2,256,1024]{2,1,0:T(8,128)(2,1)} %refs_0_.2), channel_id=1, source_target_pairs={{0,4},{4,0},{8,12},{12,8},{1,5},{5,1},{9,13},{13,9},{2,6},{6,2},{1... | collective-permute-start | bytes 3145736 | tf_op jit(solution)/shard_map/ppermute | solution.py:620
  9.8 30.8 %collective-permute-start.4 = (bf16[2,256,1024]{2,1,0:T(8,128)(2,1)}, bf16[2,256,1024]{2,1,0:T(8,128)(2,1)}, u32[]{:S(2)}, u32[]{:S(2)}) collective-permute-start(bf16[2,256,1024]{2,1,0:T(8,128)(2,1)} %refs_0_.2), channel_id=1, source_target_pairs={{0,8},{4,12},{8,0},{12,4},{1,9},{5,13},{9,1},{13,5},{2,10},{6,14},... | collective-permute-start | bytes 3145736 | tf_op jit(solution)/shard_map/ppermute | solution.py:620
  16.6 17.1 %collective-permute-start.1 = (bf16[3,128,256]{2,1,0:T(8,128)(2,1)S(1)}, bf16[3,128,256]{2,1,0:T(8,128)(2,1)S(1)}, u32[]{:S(2)}, u32[]{:S(2)}) collective-permute-start(bf16[3,128,256]{2,1,0:T(8,128)(2,1)S(1)} %shard_map.287.refs_0_), channel_id=1, source_target_pairs={{0,2},{1,3},{2,0},{3,1},{4,6},{5,7},{6,4},{7,5},{8,10},{9,11},{10,... | collective-permute-start | bytes 589832 | tf_op jit(solution)/shard_map/ppermute | solution.py:623
  55.9 26.7 %collective-permute-start.6 = (bf16[128,2048]{1,0:T(8,128)(2,1)S(1)}, bf16[128,2048]{1,0:T(8,128)(2,1)}, u32[]{:S(2)}, u32[]{:S(2)}) collective-permute-start(bf16[128,2048]{1,0:T(8,128)(2,1)S(1)} %shard_map.292), channel_id=1, source_target_pairs={{0,2},{1,3},{2,0},{3,1},{4,6},{5,7},{6,4},{7,5},{8,10},{9,11},{10,... | collective-permute-start | bytes 1572872 | tf_op jit(solution)/shard_map/ppermute | solution.py:623
  66.6 23.4 %collective-permute-start.7 = (bf16[2048,256]{1,0:T(8,128)(2,1)}, bf16[2048,256]{1,0:T(8,128)(2,1)}, u32[]{:S(2)}, u32[]{:S(2)}) collective-permute-start(bf16[2048,256]{1,0:T(8,128)(2,1)} %get-tuple-element.145), channel_id=1, source_target_pairs={{0,4},{4,0},{8,12},{12,8},{1,5},{5,1},{9,13},{13,9},{2,6},{6,2},{1... | collective-permute-start | bytes 3145736 | tf_op jit(solution)/shard_map/ppermute | solution.py:620
  79.9 91.6 %all-gather.10.cloned.1.call-start = ((), (), s32[]{:S(2)}) async-start(), calls=%async_computation.15 | async-start | bytes 9437184 | tf_op jit(solution)/shard_map/all_gather | solution.py:759
  101.1 19.7 %all-to-all-start.2 = ((bf16[16,128,128]{2,1,0:T(8,128)(2,1)}), bf16[16,128,128]{2,1,0:T(8,128)(2,1)S(1)}, u32[]{:S(2)}, u32[]{:S(2)}) async-start(bf16[16,128,128]{2,1,0:T(8,128)(2,1)} %bitcast.27), calls=%async_computation.2 | async-start | bytes 1048576 | tf_op jit(solution)/shard_map/all_to_all | solution.py:626
  106.0 119.1 %all-gather.12.cloned.1.call-start = ((), (), s32[]{:S(2)}) async-start(), calls=%async_computation.16 | async-start | bytes 7077888 | tf_op jit(solution)/shard_map/all_gather | solution.py:773
  106.7 28.8 %collective-permute-start.8 = (bf16[3,128,256]{2,1,0:T(8,128)(2,1)S(1)}, bf16[3,128,256]{2,1,0:T(8,128)(2,1)S(1)}, u32[]{:S(2)}, u32[]{:S(2)}) collective-permute-start(bf16[3,128,256]{2,1,0:T(8,128)(2,1)S(1)} %copy-done.22), channel_id=1, source_target_pairs={{0,1},{1,0},{2,3},{3,2},{4,5},{5,4},{6,7},{7,6},{8,9},{9,8},{10,11... | collective-permute-start | bytes 589832 | tf_op jit(solution)/shard_map/ppermute | solution.py:623
  108.6 26.9 %collective-permute-start.9 = (bf16[3,128,256]{2,1,0:T(8,128)(2,1)S(1)}, bf16[3,128,256]{2,1,0:T(8,128)(2,1)S(1)}, u32[]{:S(2)}, u32[]{:S(2)}) collective-permute-start(bf16[3,128,256]{2,1,0:T(8,128)(2,1)S(1)} %copy-done.22), channel_id=1, source_target_pairs={{0,2},{1,3},{2,0},{3,1},{4,6},{5,7},{6,4},{7,5},{8,10},{9,11},{10,... | collective-permute-start | bytes 589832 | tf_op jit(solution)/shard_map/ppermute | solution.py:623
  111.0 24.5 %collective-permute-start.10 = (bf16[3,128,256]{2,1,0:T(8,128)(2,1)S(1)}, bf16[3,128,256]{2,1,0:T(8,128)(2,1)S(1)}, u32[]{:S(2)}, u32[]{:S(2)}) collective-permute-start(bf16[3,128,256]{2,1,0:T(8,128)(2,1)S(1)} %copy-done.22), channel_id=1, source_target_pairs={{0,3},{1,2},{2,1},{3,0},{4,7},{5,6},{6,5},{7,4},{8,11},{9,10},{10,... | collective-permute-start | bytes 589832 | tf_op jit(solution)/shard_map/ppermute | solution.py:623
  136.5 153.2 %reduce-scatter.3.cloned.1.call-start = ((), (), s32[]{:S(2)}) async-start(), calls=%async_computation.17 | async-start | bytes 9437184 | tf_op jit(solution)/shard_map/reduce_scatter | solution.py:811
  221.3 19.4 %all-to-all-start.4 = ((bf16[16,144,128]{2,1,0:T(8,128)(2,1)}), bf16[16,144,128]{2,1,0:T(8,128)(2,1)S(1)}, u32[]{:S(2)}, u32[]{:S(2)}) async-start(bf16[16,144,128]{2,1,0:T(8,128)(2,1)} %bitcast.47), calls=%async_computation.4 | async-start | bytes 1179648 | tf_op jit(solution)/shard_map/all_to_all | solution.py:626
  241.7 29.6 %all-to-all-start.5 = ((bf16[4,128,1024]{2,1,0:T(8,128)(2,1)}), bf16[4,128,1024]{2,1,0:T(8,128)(2,1)S(1)}, u32[]{:S(2)}, u32[]{:S(2)}) async-start(bf16[4,128,1024]{2,1,0:T(8,128)(2,1)} %broadcast_in_dim.20), calls=%async_computation.5 | async-start | bytes 2097152 | tf_op jit(solution)/shard_map/all_to_all | solution.py:671
  271.4 18.4 %all-to-all-start.6 = ((bf16[16,128,128]{2,1,0:T(8,128)(2,1)}), bf16[16,128,128]{2,1,0:T(8,128)(2,1)S(1)}, u32[]{:S(2)}, u32[]{:S(2)}) async-start(bf16[16,128,128]{2,1,0:T(8,128)(2,1)} %bitcast.225), calls=%async_computation.6 | async-start | bytes 1048576 | tf_op jit(solution)/shard_map/all_to_all | solution.py:626
  275.3 136.4 %reduce-scatter.5.cloned.1.call-start = ((), (), s32[]{:S(2)}) async-start(), calls=%async_computation.18 | async-start | bytes 5242880 | tf_op jit(solution)/shard_map/reduce_scatter | solution.py:847
  306.6 19.0 %all-to-all-start.7 = ((bf16[16,64,128]{2,1,0:T(8,128)(2,1)}), bf16[16,64,128]{2,1,0:T(8,128)(2,1)S(1)}, u32[]{:S(2)}, u32[]{:S(2)}) async-start(bf16[16,64,128]{2,1,0:T(8,128)(2,1)} %bitcast.55), calls=%async_computation.8 | async-start | bytes 524288 | tf_op jit(solution)/shard_map/all_to_all | solution.py:626
  325.6 16.2 %collective-permute-start.19 = (bf16[2,128,512]{2,1,0:T(8,128)(2,1)}, bf16[2,128,512]{2,1,0:T(8,128)(2,1)}, u32[]{:S(2)}, u32[]{:S(2)}) collective-permute-start(bf16[2,128,512]{2,1,0:T(8,128)(2,1)} %get-tuple-element.188), channel_id=1, source_target_pairs={{0,16},{4,20},{8,24},{12,28},{16,0},{20,4},{24,8},{28,12},{1,17},{... | collective-permute-start | bytes 786440 | tf_op jit(solution)/shard_map/ppermute | solution.py:641
  341.8 37.0 %all-to-all-start.10 = ((bf16[16,192,128]{2,1,0:T(8,128)(2,1)}), bf16[16,192,128]{2,1,0:T(8,128)(2,1)S(1)}, u32[]{:S(2)}, u32[]{:S(2)}) async-start(bf16[16,192,128]{2,1,0:T(8,128)(2,1)} %bitcast.223), calls=%async_computation.12 | async-start | bytes 1572864 | tf_op jit(solution)/shard_map/all_to_all | solution.py:626
  347.1 99.9 %all-gather.14.cloned.1.call-start = ((), (), s32[]{:S(2)}) async-start(), calls=%async_computation.19 | async-start | bytes 1310720 | tf_op jit(solution)/shard_map/all_gather | solution.py:887
  347.9 63.8 %collective-permute-start.20 = (bf16[1,128,3072]{2,1,0:T(8,128)(2,1)}, bf16[1,128,3072]{2,1,0:T(8,128)(2,1)}, u32[]{:S(2)}, u32[]{:S(2)}) collective-permute-start(bf16[1,128,3072]{2,1,0:T(8,128)(2,1)} %copy-done.38), channel_id=1, source_target_pairs={{0,8},{4,12},{8,0},{12,4},{16,24},{20,28},{24,16},{28,20},{1,9},{5... | collective-permute-start | bytes 2359304 | tf_op jit(solution)/shard_map/ppermute | solution.py:641
  349.9 61.8 %collective-permute-start.21 = (bf16[1,128,3072]{2,1,0:T(8,128)(2,1)}, bf16[1,128,3072]{2,1,0:T(8,128)(2,1)}, u32[]{:S(2)}, u32[]{:S(2)}) collective-permute-start(bf16[1,128,3072]{2,1,0:T(8,128)(2,1)} %copy-done.37), channel_id=1, source_target_pairs={{0,16},{4,20},{8,24},{12,28},{16,0},{20,4},{24,8},{28,12},{1,17},{... | collective-permute-start | bytes 2359304 | tf_op jit(solution)/shard_map/ppermute | solution.py:641
  350.2 61.5 %collective-permute-start.22 = (bf16[1,128,3072]{2,1,0:T(8,128)(2,1)}, bf16[1,128,3072]{2,1,0:T(8,128)(2,1)}, u32[]{:S(2)}, u32[]{:S(2)}) collective-permute-start(bf16[1,128,3072]{2,1,0:T(8,128)(2,1)} %copy-done.36), channel_id=1, source_target_pairs={{0,24},{4,28},{8,16},{12,20},{16,8},{20,12},{24,0},{28,4},{1,25},{... | collective-permute-start | bytes 2359304 | tf_op jit(solution)/shard_map/ppermute | solution.py:641
  351.4 60.2 %collective-permute-start.24 = (bf16[2,128,1024]{2,1,0:T(8,128)(2,1)}, bf16[2,128,1024]{2,1,0:T(8,128)(2,1)}, u32[]{:S(2)}, u32[]{:S(2)}) collective-permute-start(bf16[2,128,1024]{2,1,0:T(8,128)(2,1)} %copy-done.39), channel_id=1, source_target_pairs={{0,2},{1,3},{2,0},{3,1},{4,6},{5,7},{6,4},{7,5},{8,10},{9,11},{10,... | collective-permute-start | bytes 1572872 | tf_op jit(solution)/shard_map/ppermute | solution.py:623
  356.8 38.4 %collective-permute-start.23 = (bf16[128,512]{1,0:T(8,128)(2,1)S(1)}, bf16[128,512]{1,0:T(8,128)(2,1)S(1)}, u32[]{:S(2)}, u32[]{:S(2)}) collective-permute-start(bf16[128,512]{1,0:T(8,128)(2,1)S(1)} %get-tuple-element.367), channel_id=1, source_target_pairs={{0,8},{4,12},{8,0},{12,4},{16,24},{20,28},{24,16},{28,20},{1,9},{5... | collective-permute-start | bytes 393224 | tf_op jit(solution)/shard_map/ppermute | solution.py:641
  412.7 16.5 %all-to-all-start.8 = ((bf16[8,224,128]{2,1,0:T(8,128)(2,1)}), bf16[8,224,128]{2,1,0:T(8,128)(2,1)}, u32[]{:S(2)}, u32[]{:S(2)}) async-start(bf16[8,224,128]{2,1,0:T(8,128)(2,1)} %pad_maximum_fusion.3), calls=%async_computation.10 | async-start | bytes 917504 | tf_op jit(solution)/shard_map/all_to_all | solution.py:909
  419.1 27.9 %collective-permute-start.25 = (bf16[3,128,256]{2,1,0:T(8,128)(2,1)S(1)}, bf16[3,128,256]{2,1,0:T(8,128)(2,1)S(1)}, u32[]{:S(2)}, u32[]{:S(2)}) collective-permute-start(bf16[3,128,256]{2,1,0:T(8,128)(2,1)S(1)} %get-tuple-element.215), channel_id=1, source_target_pairs={{0,1},{1,0},{2,3},{3,2},{4,5},{5,4},{6,7},{7,6},{8,9},{9,8},{10,11... | collective-permute-start | bytes 589832 | tf_op jit(solution)/shard_map/ppermute | solution.py:623
  419.2 27.8 %collective-permute-start.26 = (bf16[3,128,256]{2,1,0:T(8,128)(2,1)S(1)}, bf16[3,128,256]{2,1,0:T(8,128)(2,1)}, u32[]{:S(2)}, u32[]{:S(2)}) collective-permute-start(bf16[3,128,256]{2,1,0:T(8,128)(2,1)S(1)} %get-tuple-element.216), channel_id=1, source_target_pairs={{0,2},{1,3},{2,0},{3,1},{4,6},{5,7},{6,4},{7,5},{8,10},{9,11},{10,... | collective-permute-start | bytes 589832 | tf_op jit(solution)/shard_map/ppermute | solution.py:623
  421.2 25.9 %collective-permute-start.27 = (bf16[3,128,256]{2,1,0:T(8,128)(2,1)S(1)}, bf16[3,128,256]{2,1,0:T(8,128)(2,1)}, u32[]{:S(2)}, u32[]{:S(2)}) collective-permute-start(bf16[3,128,256]{2,1,0:T(8,128)(2,1)S(1)} %get-tuple-element.217), channel_id=1, source_target_pairs={{0,3},{1,2},{2,1},{3,0},{4,7},{5,6},{6,5},{7,4},{8,11},{9,10},{10,... | collective-permute-start | bytes 589832 | tf_op jit(solution)/shard_map/ppermute | solution.py:623
  431.1 19.0 %all-to-all-start.9 = ((bf16[4,16,256]{2,1,0:T(8,128)(2,1)}), bf16[4,16,256]{2,1,0:T(8,128)(2,1)S(1)}, u32[]{:S(2)}, u32[]{:S(2)}) async-start(bf16[4,16,256]{2,1,0:T(8,128)(2,1)} %broadcast_in_dim.23), calls=%async_computation.11 | async-start | bytes 65536 | tf_op jit(solution)/shard_map/all_to_all | solution.py:671
  (84 other events, 1000.2 us)
Sparse Core Ops, SparseCore 0:
  10.6 30.5 all-gather.5
  43.0 48.2 all-gather.7
  93.8 65.5 all-gather.9
  161.1 45.6 all-gather.11
  210.2 76.3 reduce-scatter.2
  290.7 98.4 reduce-scatter.4
  390.8 56.1 all-gather.13

commit v6 on v5

--- a/solution.py
+++ b/solution.py
@@ -856,14 +856,14 @@
     )
     attn_bias_sum = jnp.sum(first_grad, 0)
     first_grad_low = first_grad.astype(BF16)
+    self_mix_grad = contract(self_out_all, first_grad_low, 0, 1).astype(BF16)
+    self_mix_grad, first_grad_low = together(self_mix_grad, first_grad_low)
     squares = [(first_grad_low, mixed_t, 1), (first_low, query_grad, 1), (second_grad_low, cross_t, 1)]
     square_grad = sum_begin(squares)
 
-    self_mix_grad = contract(self_out_all, first_grad_low, 0, 1).astype(BF16)
     self_mix_grad = exchange(self_mix_grad.reshape(all_heads, HEAD, part)).reshape(chunk_shape)
     kv_grad = sum_begin((), [kv_grad])
     square_grad, kv_grad = sum_near(square_grad, 4), sum_near(kv_grad, 2)
-    self_mix_grad, square_grad, kv_grad = together(self_mix_grad, square_grad, kv_grad)
     kv_grad = sum_dp(kv_grad)
     stacked, head_grad, head_sum = self_backward(
         ctx_at, x_slots, self_query, self_pair, self_mixed, self_mix_grad, self_lse

time: 474 us -> 475 us (level)
  waiting for transfers between devices: 149 us -> 155 us
    all_to_all x6, waiting for transfers between devices: 55.3 us -> 61.3 us  [exchange(): lax.all_to_all(values, HEADS, split_axis=0, concat_axis=0, tiled=True)]
    unnamed x164 -> x170, local copies, waits for them, and re-layouts: 34.3 us -> 29.6 us
  transfers between devices with their start and end apart: 44 -> 44, of which waited for: 22 -> 22; matrix products, arithmetic and copies ran while one was open for 14% -> 13% of each run, Pallas kernels for 19% -> 20%
where the time goes in v6:
time: 475 us; the launch traced here: 466 us
  waiting for transfers between devices  155 us (33%)
  Pallas kernels  91.2 us (19%)
  starting transfers between devices  72.2 us (15%)
  local copies, waits for them, and re-layouts  43.3 us (9%)
  blocking collectives  35.4 us (7%)
  matrix products  32.3 us (7%)
  other arithmetic  21 us (4%)
  between operations  15.7 us (3%)
    pallas_call x20, Pallas kernels, call(): pl.pallas_call(kernel, grid=(seqs,), in_specs=in_specs, out_specs=out_spe...  91.2 us
    all_to_all x6, waiting for transfers between devices, exchange(): lax.all_to_all(values, HEADS, split_axis=0, concat_axis=0, tiled=True)  61.3 us
    ppermute x16, waiting for transfers between devices, tp_swap(): return lax.ppermute(values, 'tp', [(i, i ^ k) for i in range(ranks)])  58.9 us
    dot_general x10, matrix products, contract(): lax.dot_general(left, right, (((left_dim,), (right_dim,)), ((), ())), pre...  32.3 us
    unnamed x170, local copies, waits for them, and re-layouts  29.6 us
    all_to_all x6, starting transfers between devices, exchange(): lax.all_to_all(values, HEADS, split_axis=0, concat_axis=0, tiled=True)  25.8 us
    ppermute x16, starting transfers between devices, tp_swap(): return lax.ppermute(values, 'tp', [(i, i ^ k) for i in range(ranks)])  23.2 us
    all_to_all x1, blocking collectives, exchange(): lax.all_to_all(values, HEADS, split_axis=0, concat_axis=0, tiled=True)  22.8 us
  transfers between devices with their start and end apart: 44, of which 22 were waited for; matrix products, arithmetic and copies ran while one was open for 13% of the time, Pallas kernels for 20%

profile of v6, /device:TPU:0, one launch (start us, length us, event | category | flops | bytes accessed | tf_op | source)
XLA Modules:
  0.0 466.4 jit_solution(6341667416282613168)
XLA Ops:
  19.4 6.2 %collective-permute-done.refs_1_ = bf16[3,128,256]{2,1,0:T(8,128)(2,1)S(1)} collective-permute-done((bf16[3,128,256]{2,1,0:T(8,128)(2,1)S(1)}, bf16[3,128,256]{2,1,0:T(8,128)(2,1)S(1)}, u32[]{:S(2)}, u32[]{:S(2)}) %collective-permute-start) | collective-permute-done | bytes 196640 | tf_op jit(solution)/shard_map/ppermute | solution.py:623
  25.6 8.1 %collective-permute-done.1.refs_2_ = bf16[3,128,256]{2,1,0:T(8,128)(2,1)S(1)} collective-permute-done((bf16[3,128,256]{2,1,0:T(8,128)(2,1)S(1)}, bf16[3,128,256]{2,1,0:T(8,128)(2,1)S(1)}, u32[]{:S(2)}, u32[]{:S(2)}) %collective-permute-start.1) | collective-permute-done | bytes 196640 | tf_op jit(solution)/shard_map/ppermute | solution.py:623
  33.7 6.9 %collective-permute-done.4.refs_2_ = bf16[2,256,1024]{2,1,0:T(8,128)(2,1)} collective-permute-done((bf16[2,256,1024]{2,1,0:T(8,128)(2,1)}, bf16[2,256,1024]{2,1,0:T(8,128)(2,1)}, u32[]{:S(2)}, u32[]{:S(2)}) %collective-permute-start.4) | collective-permute-done | bytes 1048608 | tf_op jit(solution)/shard_map/ppermute | solution.py:620
  42.3 12.6 %all_to_all.55 = bf16[8,208,128]{2,1,0:T(8,128)(2,1)S(1)} all-to-all(bf16[8,208,128]{2,1,0:T(8,128)(2,1)S(1)} %shard_map.288), channel_id=1, replica_groups=mesh['dp'=2,'ctx'=4,'tp'=4] {'dp','ctx'}, dimensions={0} | all-to-all | bytes 851968 | tf_op jit(solution)/shard_map/all_to_all | solution.py:697
  60.1 5.2 %shard_map.289 = (bf16[2048,256]{1,0:T(8,128)(2,1)S(1)}, bf16[2048,256]{1,0:T(8,128)(2,1)}) custom-call(s32[1]{0:T(128)} %bitcast.2.at_ref, bf16[2048,1024]{1,0:T(8,128)(2,1)} %bitcast.225, bf16[1024,512]{1,0:T(8,128)(2,1)S(1)} %copy-done.2, f32[1,512]{1,0:T(1,128)S(1)} %bitcast.224), custom_call_target="tpu_custom_call" | custom-call | flops 214748368 | bytes 734208 | tf_op jit(solution)/shard_map/pallas_call | solution.py:374
  66.8 8.0 %shard_map.290 = (bf16[2,64,1024]{2,1,0:T(8,128)(2,1)S(1)}, bf16[2,1024,128]{2,1,0:T(8,128)(2,1)S(1)}, bf16[4,4,64,128]{3,2,1,0:T(8,128)(2,1)}, f32[2,1,1024]{2,1,0:T(1,128)S(1)}) custom-call(s32[1]{0:T(128)} %bitcast.at_ref, bf16[2,256,1024]{2,1,0:T(8,128)(2,1)S(1)} %copy-done, bf16[2,256,1024]{2,1,0:T(8,128)(2,1)S(1)} %collective-permute-done.3.refs_1_, ...), custom_call_target="tpu_custom_call" | custom-call | flops 187904816 | bytes 564506 | tf_op jit(solution)/shard_map/pallas_call | solution.py:374
  82.7 7.2 %all-to-all-done.1 = bf16[16,64,128]{2,1,0:T(8,128)(2,1)S(1)} async-done(((bf16[16,64,128]{2,1,0:T(8,128)(2,1)}), bf16[16,64,128]{2,1,0:T(8,128)(2,1)S(1)}, u32[]{:S(2)}, u32[]{:S(2)}) %all-to-all-start.1) | async-done | bytes 262176 | tf_op jit(solution)/shard_map/all_to_all | solution.py:626
  101.3 4.8 %all-to-all-start.2 = ((bf16[16,128,128]{2,1,0:T(8,128)(2,1)}), bf16[16,128,128]{2,1,0:T(8,128)(2,1)S(1)}, u32[]{:S(2)}, u32[]{:S(2)}) async-start(bf16[16,128,128]{2,1,0:T(8,128)(2,1)} %bitcast.27), calls=%async_computation.2 | async-start | bytes 1048576 | tf_op jit(solution)/shard_map/all_to_all | solution.py:626
  111.2 9.8 %all-to-all-done.2 = bf16[16,128,128]{2,1,0:T(8,128)(2,1)S(1)} async-done(((bf16[16,128,128]{2,1,0:T(8,128)(2,1)}), bf16[16,128,128]{2,1,0:T(8,128)(2,1)S(1)}, u32[]{:S(2)}, u32[]{:S(2)}) %all-to-all-start.2) | async-done | bytes 524320 | tf_op jit(solution)/shard_map/all_to_all | solution.py:626
  122.4 13.2 %shard_map.293 = bf16[4,4,144,128]{3,2,1,0:T(8,128)(2,1)S(1)} custom-call(bf16[4,4,128,128]{3,2,1,0:T(8,128)(2,1)S(1)} %fusion.58.q_ref, bf16[2,1024,256]{2,1,0:T(8,128)(2,1)S(1)} %bitcast.213, bf16[2,1024,256]{2,1,0:T(8,128)(2,1)} %bitcast.18.refs_1_), custom_call_target="tpu_custom_call" | custom-call | flops 429496736 | bytes 321126 | tf_op jit(solution)/shard_map/pallas_call | solution.py:374
  136.7 22.8 %all_to_all.56 = bf16[16,144,128]{2,1,0:T(8,128)(2,1)S(1)} all-to-all(bf16[16,144,128]{2,1,0:T(8,128)(2,1)S(1)} %bitcast.211), channel_id=1, replica_groups=mesh['dp'=2,'ctx'=4,'tp'=4] {'tp','ctx'}, dimensions={0} | all-to-all | bytes 1179648 | tf_op jit(solution)/shard_map/all_to_all | solution.py:626
  165.5 4.4 collective-permute-done.12
  172.4 7.6 %multiply_convert_fusion = (bf16[256,2048]{1,0:T(8,128)(2,1)S(1)}, f32[256,2048]{1,0:T(8,128)S(1)}, f32[256,2048]{1,0:T(8,128)S(1)}) fusion(f32[2048]{0:T(1024)S(1)} %maximum_convert_fusion, bf16[1024,4096]{1,0:T(8,128)(2,1)} %all-gather.10.cloned.1.call-done, bf16[128,1024]{1,0:T(8,128)(2,1)} %copy-done.56, bf16[128,1024]{1,0:T(8,128)(2,1)} %copy-done.53), kind=kOutput, calls=%fused_computation.13 | convolution fusion | flops 1109393408 | bytes 9969664 | tf_op jit(solution)/shard_map/dot_general | solution.py:25
  182.0 6.9 %collective-permute-done.13 = bf16[128,1024]{1,0:T(8,128)(2,1)S(1)} collective-permute-done((bf16[128,1024]{1,0:T(8,128)(2,1)S(1)}, bf16[128,1024]{1,0:T(8,128)(2,1)S(1)}, u32[]{:S(2)}, u32[]{:S(2)}) %collective-permute-start.13) | collective-permute-done | bytes 262176 | tf_op jit(solution)/shard_map/ppermute | solution.py:623
  192.0 5.9 %collective-permute-done.14 = bf16[128,1024]{1,0:T(8,128)(2,1)S(1)} collective-permute-done((bf16[128,1024]{1,0:T(8,128)(2,1)S(1)}, bf16[128,1024]{1,0:T(8,128)(2,1)S(1)}, u32[]{:S(2)}, u32[]{:S(2)}) %collective-permute-start.14) | collective-permute-done | bytes 262176 | tf_op jit(solution)/shard_map/ppermute | solution.py:623
  199.9 5.1 %shard_map.297 = bf16[1024,4096]{1,0:T(8,128)(2,1)} custom-call(bf16[256,1024]{1,0:T(8,128)(2,1)S(1)} %pad_maximum_fusion.1.two_ref, bf16[256,2048]{1,0:T(8,128)(2,1)S(1)} %get-tuple-element.391.pre_ref, bf16[256,1024]{1,0:T(8,128)(2,1)S(1)} %pad_maximum_fusion.2.low_ref, bf16[256,2048]{1,0:T(8,128)(2,1)S(1)} %get-tuple-element.345.active_ref), custom_call_target="tpu_custom_call" | custom-call | flops 214748368 | bytes 1153433 | tf_op jit(solution)/shard_map/pallas_call | solution.py:374
  211.4 5.8 %collective-permute-done.15 = bf16[128,1024]{1,0:T(8,128)(2,1)S(1)} collective-permute-done((bf16[128,1024]{1,0:T(8,128)(2,1)S(1)}, bf16[128,1024]{1,0:T(8,128)(2,1)S(1)}, u32[]{:S(2)}, u32[]{:S(2)}) %collective-permute-start.15) | collective-permute-done | bytes 262176 | tf_op jit(solution)/shard_map/ppermute | solution.py:623
  226.3 15.5 %all-to-all-done.4 = bf16[16,144,128]{2,1,0:T(8,128)(2,1)S(1)} async-done(((bf16[16,144,128]{2,1,0:T(8,128)(2,1)}), bf16[16,144,128]{2,1,0:T(8,128)(2,1)S(1)}, u32[]{:S(2)}, u32[]{:S(2)}) %all-to-all-start.4) | async-done | bytes 589856 | tf_op jit(solution)/shard_map/all_to_all | solution.py:626
  243.0 3.9 all-to-all-start.5
  247.9 22.1 %shard_map.295 = (bf16[2,1024,256]{2,1,0:T(8,128)(2,1)S(1)}, bf16[2,1024,256]{2,1,0:T(8,128)(2,1)}, bf16[4,4,128,128]{3,2,1,0:T(8,128)(2,1)}) custom-call(bf16[4,4,128,128]{3,2,1,0:T(8,128)(2,1)S(1)} %fusion.58.q_ref, bf16[4,4,144,128]{3,2,1,0:T(8,128)(2,1)S(1)} %bitcast.223, bf16[2,1024,256]{2,1,0:T(8,128)(2,1)} %bitcast.212, ...), custom_call_target="tpu_custom_call" | custom-call | flops 1073741824 | bytes 583270 | tf_op jit(solution)/shard_map/pallas_call | solution.py:374
  272.6 4.1 all-to-all-start.6
  279.7 8.7 %shard_map.296 = (bf16[2048,1024]{1,0:T(8,128)(2,1)}, f32[1,512]{1,0:T(1,128)S(1)}, bf16[1024,512]{1,0:T(8,128)(2,1)S(1)}) custom-call(s32[1]{0:T(128)} %bitcast.2.at_ref, bf16[2048,1024]{1,0:T(8,128)(2,1)} %bitcast.226, bf16[1024,512]{1,0:T(8,128)(2,1)S(1)} %copy-done.3, bf16[2048,256]{1,0:T(8,128)(2,1)S(1)} %bitcast.222, bf16[2048,256]{1,0:T(8,128)(2,1)} %bitcast.53.refs_1_), custom_call_target="tpu_custom_call" | custom-call | flops 429496736 | bytes 1258496 | tf_op jit(solution)/shard_map/pallas_call | solution.py:374
  321.1 5.3 %all-to-all-done.7 = bf16[16,64,128]{2,1,0:T(8,128)(2,1)S(1)} async-done(((bf16[16,64,128]{2,1,0:T(8,128)(2,1)}), bf16[16,64,128]{2,1,0:T(8,128)(2,1)S(1)}, u32[]{:S(2)}, u32[]{:S(2)}) %all-to-all-start.7) | async-done | bytes 262176 | tf_op jit(solution)/shard_map/all_to_all | solution.py:626
  327.3 7.8 %shard_map.298 = (bf16[4,4,192,128]{3,2,1,0:T(8,128)(2,1)}, f32[192,1024]{1,0:T(8,128)S(1)}, f32[192,1]{1,0:T(8,128)S(1)}) custom-call(s32[1]{0:T(128)} %bitcast.at_ref, bf16[2,256,1024]{2,1,0:T(8,128)(2,1)S(1)} %copy-done, bf16[2,256,1024]{2,1,0:T(8,128)(2,1)} %copy-done.1, bf16[2,256,1024]{2,1,0:T(8,128)(2,1)} %collective-permute-done.4.refs_2_, ...), custom_call_target="tpu_custom_call" | custom-call | flops 348966080 | bytes 708685 | tf_op jit(solution)/shard_map/pallas_call | solution.py:374
  335.2 5.0 %shard_map.300 = (bf16[1,128,3072]{2,1,0:T(8,128)(2,1)S(1)}, bf16[1,128,3072]{2,1,0:T(8,128)(2,1)S(1)}, bf16[1,128,3072]{2,1,0:T(8,128)(2,1)S(1)}, bf16[1,128,3072]{2,1,0:T(8,128)(2,1)S(1)}) custom-call(bf16[4,128,3072]{2,1,0:T(8,128)(2,1)} %get-tuple-element.168.keep_ref, bf16[4,128,3072]{2,1,0:T(8,128)(2,1)} %collective-permute-done.17.got_ref), custom_call_target="tpu_custom_call" | custom-call | flops 157286 | bytes 943718 | tf_op jit(solution)/shard_map/pallas_call | solution.py:374
  341.6 5.7 %all-to-all-start.10 = ((bf16[16,192,128]{2,1,0:T(8,128)(2,1)}), bf16[16,192,128]{2,1,0:T(8,128)(2,1)S(1)}, u32[]{:S(2)}, u32[]{:S(2)}) async-start(bf16[16,192,128]{2,1,0:T(8,128)(2,1)} %bitcast.87), calls=%async_computation.12 | async-start | bytes 1572864 | tf_op jit(solution)/shard_map/all_to_all | solution.py:626
  358.4 21.7 %all-to-all-done.10.stacked_ref = bf16[16,192,128]{2,1,0:T(8,128)(2,1)S(1)} async-done(((bf16[16,192,128]{2,1,0:T(8,128)(2,1)}), bf16[16,192,128]{2,1,0:T(8,128)(2,1)S(1)}, u32[]{:S(2)}, u32[]{:S(2)}) %all-to-all-start.10) | async-done | bytes 786464 | tf_op jit(solution)/shard_map/all_to_all | solution.py:626
  380.1 5.8 %shard_map.305 = bf16[128,1024]{1,0:T(8,128)(2,1)} custom-call(bf16[16,192,128]{2,1,0:T(8,128)(2,1)S(1)} %all-to-all-done.10.stacked_ref, bf16[1024,3072]{1,0:T(8,128)(2,1)} %all-gather.12.cloned.1.call-done.proj_ref, f32[128,1024]{1,0:T(8,128)S(1)} %get-tuple-element.341.first_ref), custom_call_target="tpu_custom_call" | custom-call | flops 80530640 | bytes 786432 | tf_op jit(solution)/shard_map/pallas_call | solution.py:374
  385.9 9.4 %collective-permute-done.23 = bf16[128,512]{1,0:T(8,128)(2,1)S(1)} collective-permute-done((bf16[128,512]{1,0:T(8,128)(2,1)}, bf16[128,512]{1,0:T(8,128)(2,1)S(1)}, u32[]{:S(2)}, u32[]{:S(2)}) %collective-permute-start.23) | collective-permute-done | bytes 131104 | tf_op jit(solution)/shard_map/ppermute | solution.py:641
  395.4 17.5 %collective-permute-done.24 = bf16[2,128,1024]{2,1,0:T(8,128)(2,1)} collective-permute-done((bf16[2,128,1024]{2,1,0:T(8,128)(2,1)}, bf16[2,128,1024]{2,1,0:T(8,128)(2,1)}, u32[]{:S(2)}, u32[]{:S(2)}) %collective-permute-start.24) | collective-permute-done | bytes 524320 | tf_op jit(solution)/shard_map/ppermute | solution.py:623
  413.9 4.4 all-to-all-start.8
  437.5 10.8 %all-gather.14.cloned.1.call-done = bf16[512,1024]{1,0:T(8,128)(2,1)} async-done(((bf16[128,1024]{1,0:T(8,128)(2,1)}), bf16[512,1024]{1,0:T(8,128)(2,1)}) %all-gather.14.cloned.1.call-update) | async-done | bytes 1048592 | tf_op jit(solution)/shard_map/all_gather | solution.py:887
  (420 shorter events, 162.5 us)
Async XLA Ops:
  7.3 51.6 %all-gather.6.cloned.1.call-start = ((), (), s32[]{:S(2)}) async-start(), calls=%async_computation.13 | async-start | bytes 1179648 | tf_op jit(solution)/shard_map/all_gather | solution.py:699
  9.2 82.4 %all-gather.8.cloned.1.call-start = ((), (), s32[]{:S(2)}) async-start(), calls=%async_computation.14 | async-start | bytes 7077888 | tf_op jit(solution)/shard_map/all_gather | solution.py:707
  9.2 24.5 %collective-permute-start.3 = (bf16[2,256,1024]{2,1,0:T(8,128)(2,1)}, bf16[2,256,1024]{2,1,0:T(8,128)(2,1)S(1)}, u32[]{:S(2)}, u32[]{:S(2)}) collective-permute-start(bf16[2,256,1024]{2,1,0:T(8,128)(2,1)} %refs_0_.2), channel_id=1, source_target_pairs={{0,4},{4,0},{8,12},{12,8},{1,5},{5,1},{9,13},{13,9},{2,6},{6,2},{1... | collective-permute-start | bytes 3145736 | tf_op jit(solution)/shard_map/ppermute | solution.py:620
  9.8 30.8 %collective-permute-start.4 = (bf16[2,256,1024]{2,1,0:T(8,128)(2,1)}, bf16[2,256,1024]{2,1,0:T(8,128)(2,1)}, u32[]{:S(2)}, u32[]{:S(2)}) collective-permute-start(bf16[2,256,1024]{2,1,0:T(8,128)(2,1)} %refs_0_.2), channel_id=1, source_target_pairs={{0,8},{4,12},{8,0},{12,4},{1,9},{5,13},{9,1},{13,5},{2,10},{6,14},... | collective-permute-start | bytes 3145736 | tf_op jit(solution)/shard_map/ppermute | solution.py:620
  16.6 17.1 %collective-permute-start.1 = (bf16[3,128,256]{2,1,0:T(8,128)(2,1)S(1)}, bf16[3,128,256]{2,1,0:T(8,128)(2,1)S(1)}, u32[]{:S(2)}, u32[]{:S(2)}) collective-permute-start(bf16[3,128,256]{2,1,0:T(8,128)(2,1)S(1)} %shard_map.287.refs_0_), channel_id=1, source_target_pairs={{0,2},{1,3},{2,0},{3,1},{4,6},{5,7},{6,4},{7,5},{8,10},{9,11},{10,... | collective-permute-start | bytes 589832 | tf_op jit(solution)/shard_map/ppermute | solution.py:623
  55.5 27.1 %collective-permute-start.6 = (bf16[128,2048]{1,0:T(8,128)(2,1)S(1)}, bf16[128,2048]{1,0:T(8,128)(2,1)}, u32[]{:S(2)}, u32[]{:S(2)}) collective-permute-start(bf16[128,2048]{1,0:T(8,128)(2,1)S(1)} %shard_map.292), channel_id=1, source_target_pairs={{0,2},{1,3},{2,0},{3,1},{4,6},{5,7},{6,4},{7,5},{8,10},{9,11},{10,... | collective-permute-start | bytes 1572872 | tf_op jit(solution)/shard_map/ppermute | solution.py:623
  66.2 23.6 %collective-permute-start.7 = (bf16[2048,256]{1,0:T(8,128)(2,1)}, bf16[2048,256]{1,0:T(8,128)(2,1)}, u32[]{:S(2)}, u32[]{:S(2)}) collective-permute-start(bf16[2048,256]{1,0:T(8,128)(2,1)} %get-tuple-element.140), channel_id=1, source_target_pairs={{0,4},{4,0},{8,12},{12,8},{1,5},{5,1},{9,13},{13,9},{2,6},{6,2},{1... | collective-permute-start | bytes 3145736 | tf_op jit(solution)/shard_map/ppermute | solution.py:620
  79.8 92.6 %all-gather.10.cloned.1.call-start = ((), (), s32[]{:S(2)}) async-start(), calls=%async_computation.15 | async-start | bytes 9437184 | tf_op jit(solution)/shard_map/all_gather | solution.py:759
  101.3 19.6 %all-to-all-start.2 = ((bf16[16,128,128]{2,1,0:T(8,128)(2,1)}), bf16[16,128,128]{2,1,0:T(8,128)(2,1)S(1)}, u32[]{:S(2)}, u32[]{:S(2)}) async-start(bf16[16,128,128]{2,1,0:T(8,128)(2,1)} %bitcast.27), calls=%async_computation.2 | async-start | bytes 1048576 | tf_op jit(solution)/shard_map/all_to_all | solution.py:626
  106.1 120.2 %all-gather.12.cloned.1.call-start = ((), (), s32[]{:S(2)}) async-start(), calls=%async_computation.16 | async-start | bytes 7077888 | tf_op jit(solution)/shard_map/all_gather | solution.py:773
  106.8 28.8 %collective-permute-start.8 = (bf16[3,128,256]{2,1,0:T(8,128)(2,1)S(1)}, bf16[3,128,256]{2,1,0:T(8,128)(2,1)S(1)}, u32[]{:S(2)}, u32[]{:S(2)}) collective-permute-start(bf16[3,128,256]{2,1,0:T(8,128)(2,1)S(1)} %copy-done.21), channel_id=1, source_target_pairs={{0,1},{1,0},{2,3},{3,2},{4,5},{5,4},{6,7},{7,6},{8,9},{9,8},{10,11... | collective-permute-start | bytes 589832 | tf_op jit(solution)/shard_map/ppermute | solution.py:623
  108.7 26.9 %collective-permute-start.9 = (bf16[3,128,256]{2,1,0:T(8,128)(2,1)S(1)}, bf16[3,128,256]{2,1,0:T(8,128)(2,1)S(1)}, u32[]{:S(2)}, u32[]{:S(2)}) collective-permute-start(bf16[3,128,256]{2,1,0:T(8,128)(2,1)S(1)} %copy-done.21), channel_id=1, source_target_pairs={{0,2},{1,3},{2,0},{3,1},{4,6},{5,7},{6,4},{7,5},{8,10},{9,11},{10,... | collective-permute-start | bytes 589832 | tf_op jit(solution)/shard_map/ppermute | solution.py:623
  111.1 24.5 %collective-permute-start.10 = (bf16[3,128,256]{2,1,0:T(8,128)(2,1)S(1)}, bf16[3,128,256]{2,1,0:T(8,128)(2,1)S(1)}, u32[]{:S(2)}, u32[]{:S(2)}) collective-permute-start(bf16[3,128,256]{2,1,0:T(8,128)(2,1)S(1)} %copy-done.21), channel_id=1, source_target_pairs={{0,3},{1,2},{2,1},{3,0},{4,7},{5,6},{6,5},{7,4},{8,11},{9,10},{10,... | collective-permute-start | bytes 589832 | tf_op jit(solution)/shard_map/ppermute | solution.py:623
  136.6 154.6 %reduce-scatter.3.cloned.1.call-start = ((), (), s32[]{:S(2)}) async-start(), calls=%async_computation.17 | async-start | bytes 9437184 | tf_op jit(solution)/shard_map/reduce_scatter | solution.py:811
  222.4 19.4 %all-to-all-start.4 = ((bf16[16,144,128]{2,1,0:T(8,128)(2,1)}), bf16[16,144,128]{2,1,0:T(8,128)(2,1)S(1)}, u32[]{:S(2)}, u32[]{:S(2)}) async-start(bf16[16,144,128]{2,1,0:T(8,128)(2,1)} %bitcast.47), calls=%async_computation.4 | async-start | bytes 1179648 | tf_op jit(solution)/shard_map/all_to_all | solution.py:626
  243.0 29.6 %all-to-all-start.5 = ((bf16[4,128,1024]{2,1,0:T(8,128)(2,1)}), bf16[4,128,1024]{2,1,0:T(8,128)(2,1)S(1)}, u32[]{:S(2)}, u32[]{:S(2)}) async-start(bf16[4,128,1024]{2,1,0:T(8,128)(2,1)} %broadcast_in_dim.20), calls=%async_computation.5 | async-start | bytes 2097152 | tf_op jit(solution)/shard_map/all_to_all | solution.py:671
  272.6 18.6 %all-to-all-start.6 = ((bf16[16,128,128]{2,1,0:T(8,128)(2,1)}), bf16[16,128,128]{2,1,0:T(8,128)(2,1)S(1)}, u32[]{:S(2)}, u32[]{:S(2)}) async-start(bf16[16,128,128]{2,1,0:T(8,128)(2,1)} %bitcast.50), calls=%async_computation.6 | async-start | bytes 1048576 | tf_op jit(solution)/shard_map/all_to_all | solution.py:626
  276.7 136.2 %reduce-scatter.5.cloned.1.call-start = ((), (), s32[]{:S(2)}) async-start(), calls=%async_computation.18 | async-start | bytes 5242880 | tf_op jit(solution)/shard_map/reduce_scatter | solution.py:847
  304.0 31.1 %collective-permute-start.17 = (bf16[4,128,3072]{2,1,0:T(8,128)(2,1)}, bf16[4,128,3072]{2,1,0:T(8,128)(2,1)}, u32[]{:S(2)}, u32[]{:S(2)}) collective-permute-start(bf16[4,128,3072]{2,1,0:T(8,128)(2,1)} %get-tuple-element.169), channel_id=1, source_target_pairs={{0,4},{4,0},{8,12},{12,8},{16,20},{20,16},{24,28},{28,24},{1,5},{5... | collective-permute-start | bytes 9437192 | tf_op jit(solution)/shard_map/ppermute | solution.py:641
  307.9 18.5 %all-to-all-start.7 = ((bf16[16,64,128]{2,1,0:T(8,128)(2,1)}), bf16[16,64,128]{2,1,0:T(8,128)(2,1)S(1)}, u32[]{:S(2)}, u32[]{:S(2)}) async-start(bf16[16,64,128]{2,1,0:T(8,128)(2,1)} %bitcast.246), calls=%async_computation.8 | async-start | bytes 524288 | tf_op jit(solution)/shard_map/all_to_all | solution.py:626
  316.7 23.5 %collective-permute-start.19 = (bf16[2,128,512]{2,1,0:T(8,128)(2,1)}, bf16[2,128,512]{2,1,0:T(8,128)(2,1)}, u32[]{:S(2)}, u32[]{:S(2)}) collective-permute-start(bf16[2,128,512]{2,1,0:T(8,128)(2,1)} %get-tuple-element.178), channel_id=1, source_target_pairs={{0,16},{4,20},{8,24},{12,28},{16,0},{20,4},{24,8},{28,12},{1,17},{... | collective-permute-start | bytes 786440 | tf_op jit(solution)/shard_map/ppermute | solution.py:641
  341.6 38.5 %all-to-all-start.10 = ((bf16[16,192,128]{2,1,0:T(8,128)(2,1)}), bf16[16,192,128]{2,1,0:T(8,128)(2,1)S(1)}, u32[]{:S(2)}, u32[]{:S(2)}) async-start(bf16[16,192,128]{2,1,0:T(8,128)(2,1)} %bitcast.87), calls=%async_computation.12 | async-start | bytes 1572864 | tf_op jit(solution)/shard_map/all_to_all | solution.py:626
  347.3 100.9 %all-gather.14.cloned.1.call-start = ((), (), s32[]{:S(2)}) async-start(), calls=%async_computation.19 | async-start | bytes 1310720 | tf_op jit(solution)/shard_map/all_gather | solution.py:887
  347.4 65.5 %collective-permute-start.20 = (bf16[1,128,3072]{2,1,0:T(8,128)(2,1)}, bf16[1,128,3072]{2,1,0:T(8,128)(2,1)}, u32[]{:S(2)}, u32[]{:S(2)}) collective-permute-start(bf16[1,128,3072]{2,1,0:T(8,128)(2,1)} %copy-done.39), channel_id=1, source_target_pairs={{0,8},{4,12},{8,0},{12,4},{16,24},{20,28},{24,16},{28,20},{1,9},{5... | collective-permute-start | bytes 2359304 | tf_op jit(solution)/shard_map/ppermute | solution.py:641
  349.4 63.5 %collective-permute-start.21 = (bf16[1,128,3072]{2,1,0:T(8,128)(2,1)}, bf16[1,128,3072]{2,1,0:T(8,128)(2,1)}, u32[]{:S(2)}, u32[]{:S(2)}) collective-permute-start(bf16[1,128,3072]{2,1,0:T(8,128)(2,1)} %copy-done.38), channel_id=1, source_target_pairs={{0,16},{4,20},{8,24},{12,28},{16,0},{20,4},{24,8},{28,12},{1,17},{... | collective-permute-start | bytes 2359304 | tf_op jit(solution)/shard_map/ppermute | solution.py:641
  351.1 61.8 %collective-permute-start.22 = (bf16[1,128,3072]{2,1,0:T(8,128)(2,1)}, bf16[1,128,3072]{2,1,0:T(8,128)(2,1)}, u32[]{:S(2)}, u32[]{:S(2)}) collective-permute-start(bf16[1,128,3072]{2,1,0:T(8,128)(2,1)} %copy-done.37), channel_id=1, source_target_pairs={{0,24},{4,28},{8,16},{12,20},{16,8},{20,12},{24,0},{28,4},{1,25},{... | collective-permute-start | bytes 2359304 | tf_op jit(solution)/shard_map/ppermute | solution.py:641
  351.1 61.8 %collective-permute-start.24 = (bf16[2,128,1024]{2,1,0:T(8,128)(2,1)}, bf16[2,128,1024]{2,1,0:T(8,128)(2,1)}, u32[]{:S(2)}, u32[]{:S(2)}) collective-permute-start(bf16[2,128,1024]{2,1,0:T(8,128)(2,1)} %copy-done.40), channel_id=1, source_target_pairs={{0,2},{1,3},{2,0},{3,1},{4,6},{5,7},{6,4},{7,5},{8,10},{9,11},{10,... | collective-permute-start | bytes 1572872 | tf_op jit(solution)/shard_map/ppermute | solution.py:623
  355.6 39.8 %collective-permute-start.23 = (bf16[128,512]{1,0:T(8,128)(2,1)}, bf16[128,512]{1,0:T(8,128)(2,1)S(1)}, u32[]{:S(2)}, u32[]{:S(2)}) collective-permute-start(bf16[128,512]{1,0:T(8,128)(2,1)} %get-tuple-element.357), channel_id=1, source_target_pairs={{0,8},{4,12},{8,0},{12,4},{16,24},{20,28},{24,16},{28,20},{1,9},{5... | collective-permute-start | bytes 393224 | tf_op jit(solution)/shard_map/ppermute | solution.py:641
  420.5 27.7 %collective-permute-start.25 = (bf16[3,128,256]{2,1,0:T(8,128)(2,1)S(1)}, bf16[3,128,256]{2,1,0:T(8,128)(2,1)S(1)}, u32[]{:S(2)}, u32[]{:S(2)}) collective-permute-start(bf16[3,128,256]{2,1,0:T(8,128)(2,1)S(1)} %get-tuple-element.205), channel_id=1, source_target_pairs={{0,1},{1,0},{2,3},{3,2},{4,5},{5,4},{6,7},{7,6},{8,9},{9,8},{10,11... | collective-permute-start | bytes 589832 | tf_op jit(solution)/shard_map/ppermute | solution.py:623
  420.6 27.7 %collective-permute-start.26 = (bf16[3,128,256]{2,1,0:T(8,128)(2,1)S(1)}, bf16[3,128,256]{2,1,0:T(8,128)(2,1)S(1)}, u32[]{:S(2)}, u32[]{:S(2)}) collective-permute-start(bf16[3,128,256]{2,1,0:T(8,128)(2,1)S(1)} %get-tuple-element.206), channel_id=1, source_target_pairs={{0,2},{1,3},{2,0},{3,1},{4,6},{5,7},{6,4},{7,5},{8,10},{9,11},{10,... | collective-permute-start | bytes 589832 | tf_op jit(solution)/shard_map/ppermute | solution.py:623
  422.6 25.7 %collective-permute-start.27 = (bf16[3,128,256]{2,1,0:T(8,128)(2,1)S(1)}, bf16[3,128,256]{2,1,0:T(8,128)(2,1)S(1)}, u32[]{:S(2)}, u32[]{:S(2)}) collective-permute-start(bf16[3,128,256]{2,1,0:T(8,128)(2,1)S(1)} %get-tuple-element.207), channel_id=1, source_target_pairs={{0,3},{1,2},{2,1},{3,0},{4,7},{5,6},{6,5},{7,4},{8,11},{9,10},{10,... | collective-permute-start | bytes 589832 | tf_op jit(solution)/shard_map/ppermute | solution.py:623
  432.5 18.8 %all-to-all-start.9 = ((bf16[4,16,256]{2,1,0:T(8,128)(2,1)}), bf16[4,16,256]{2,1,0:T(8,128)(2,1)S(1)}, u32[]{:S(2)}, u32[]{:S(2)}) async-start(bf16[4,16,256]{2,1,0:T(8,128)(2,1)} %broadcast_in_dim.23), calls=%async_computation.11 | async-start | bytes 65536 | tf_op jit(solution)/shard_map/all_to_all | solution.py:671
  (87 other events, 883.2 us)
Sparse Core Ops, SparseCore 0:
  10.6 30.5 all-gather.5
  43.0 48.4 all-gather.7
  94.0 65.3 all-gather.9
  161.1 45.6 all-gather.11
  210.1 76.5 reduce-scatter.2
  292.1 99.3 reduce-scatter.4
  393.2 55.0 all-gather.13
